TPU v7x, 32 devices: a whole 2x2x4 slice. The times are simulated.
32 devices in a mesh: clip: 16 (over z, y, core), head: 2 (over x).
Axes of the slice: x: 2, y: 2, z: 4, core: 2. Of those that a mesh axis runs over, the one named last changes fastest.
Arguments:
- tokens: bfloat16 [3, 8192, 768], P(None, 'clip'), may hold values from -6 to 6
- cotangent: bfloat16 [3, 8192, 768], P(None, 'clip'), may hold values from -6 to 6
- clip_len: int32 [3, 8, 4], replicated, may hold values from 1 to 192, 256 in all within a row
- ln_params: float32 [16, 6, 768], P('clip'), as said below
- w_self: bfloat16 [16, 3, 768, 768], P('clip', None, None, 'head'), as said below
- w_self_out: bfloat16 [16, 768, 768], P('clip', 'head'), as said below
- w_offer: bfloat16 [16, 2, 768, 768], P('clip', None, None, 'head'), as said below
- w_query: bfloat16 [16, 768, 768], P('clip', None, 'head'), as said below
- w_cross_out: bfloat16 [16, 768, 768], P('clip', 'head'), as said below
- w_up: bfloat16 [16, 768, 3072], P('clip', None, 'head'), as said below
- w_down: bfloat16 [16, 3072, 768], P('clip', 'head'), as said below
Outputs:
- layer_out: bfloat16 [3, 8192, 768], P(None, 'clip')
- grad_tokens: float32 [3, 8192, 768], P(None, 'clip')
- grad_ln_params: float32 [16, 6, 768], P('clip')
- grad_w_self: float32 [16, 3, 768, 768], P('clip', None, None, 'head')
- grad_w_self_out: float32 [16, 768, 768], P('clip', 'head')
- grad_w_offer: float32 [16, 2, 768, 768], P('clip', None, None, 'head')
- grad_w_query: float32 [16, 768, 768], P('clip', None, 'head')
- grad_w_cross_out: float32 [16, 768, 768], P('clip', 'head')
- grad_w_up: float32 [16, 768, 3072], P('clip', None, 'head')
- grad_w_down: float32 [16, 3072, 768], P('clip', 'head')
Inputs may be any that keep to these rules, and one draw needn't show every extreme that they name: `clip_len`: each row (one clip set) sums to half of 512, and its largest entry is 192. `ln_params`: equal on all clip indices of one view range: 0 to 7, the next 4, the last 4. `w_self`: equal on all clip indices of one view range. `w_self_out`: equal on all clip indices of one view range. `w_offer`: equal on all clip indices of one view range. `w_query`: equal on all clip indices of one view range. `w_cross_out`: equal on all clip indices of one view range. `w_up`: equal on all clip indices of one view range. `w_down`: equal on all clip indices of one view range.
All inputs are finite; a program needn't handle non-finite values.
Results may differ from a plain program's by a relative error of at most 0.019.
Values may be sent and summed in bfloat16 or wider, within the bound.
No kernel may reach another device: no remote copies, remote signals or barrier semaphores. Data moves between devices by JAX's collectives and lax.ppermute only.
A program may use at most 256 MiB of HBM per device.

v0:
```python
from functools import partial

import jax
import jax.numpy as jnp
from jax import lax
from jax.sharding import PartitionSpec as P

HEAD_DIM = 64


EPSILON = 1e-06
SCORE_SCALE = 0.125
MASKED = -1e30


def shifted(block, axis, distance):
    devices = range(lax.axis_size(axis))
    route = [(i - distance, i) for i in devices if i - distance in devices]
    return lax.ppermute(block, axis, route)


def for_sending(value):
    return jax.tree.map(lambda a: a.astype(jnp.bfloat16) if a.dtype == jnp.float32 else a, value)


def swapped(value, axis, bit):
    mask = 2**bit
    pairs = [(source, source ^ mask) for source in range(lax.axis_size(axis))]
    return lax.ppermute(value, axis, pairs)


def normalize(inputs, norm_gain, norm_shift):
    row_mean = jnp.mean(inputs, axis=-1, keepdims=True)
    centered = inputs - row_mean
    variance = jnp.mean(centered * centered, axis=-1, keepdims=True)
    return centered * lax.rsqrt(variance + EPSILON) * norm_gain + norm_shift


def clip_ids(lengths, row_count):
    ends = jnp.cumsum(lengths)
    places = jnp.arange(row_count, dtype=jnp.int32)
    return jnp.sum((places[:, None] >= ends[None, :]).astype(jnp.int32), axis=1)


def product(left, right):
    return jnp.dot(left, right, preferred_element_type=jnp.float32)


def contract_rows(left, right):
    return lax.dot_general(
        left, right, (((0,), (0,)), ((), ())), preferred_element_type=jnp.float32
    )


def contract_cols(left, right):
    return lax.dot_general(
        left, right, (((1,), (1,)), ((), ())), preferred_element_type=jnp.float32
    )


def split_heads(matrix):
    return matrix.reshape(matrix.shape[0], -1, HEAD_DIM)


def head_total(partial_sum):
    return lax.psum(partial_sum, "head")


def masked_scores(query_heads, key_heads, query_ids, key_ids):
    scores = (
        jnp.einsum("qhd,khd->hqk", query_heads, key_heads, preferred_element_type=jnp.float32)
        * SCORE_SCALE
    )
    allowed = (query_ids[:, None] == key_ids[None, :])[None]
    return jnp.where(allowed, scores, MASKED)


def attend(query, key_rows, value_rows, query_ids, key_ids):
    value_heads = split_heads(value_rows)
    scores = masked_scores(split_heads(query), split_heads(key_rows), query_ids, key_ids)
    row_max = jnp.max(scores, axis=-1, keepdims=True)
    exponent = jnp.exp(scores - row_max)
    row_total = jnp.sum(exponent, axis=-1, keepdims=True)
    attn_probs = (exponent / row_total).astype(jnp.bfloat16)
    mixture = jnp.einsum(
        "hqk,khd->qhd", attn_probs, value_heads, preferred_element_type=jnp.float32
    )
    return (mixture.reshape(query.shape[0], -1), row_max + jnp.log(row_total))


def attend_back(query, key_rows, value_rows, query_ids, key_ids, log_total, grad_mix):
    query_heads = split_heads(query)
    key_heads = split_heads(key_rows)
    value_heads = split_heads(value_rows)
    grad_heads = split_heads(grad_mix)
    scores = masked_scores(query_heads, key_heads, query_ids, key_ids)
    attn_probs = jnp.exp(scores - log_total)
    grad_probs = jnp.einsum(
        "qhd,khd->hqk", grad_heads, value_heads, preferred_element_type=jnp.float32
    )
    row_delta = jnp.sum(attn_probs * grad_probs, axis=-1, keepdims=True)
    grad_scores = (attn_probs * (grad_probs - row_delta)).astype(jnp.bfloat16)
    grad_query = (
        jnp.einsum("hqk,khd->qhd", grad_scores, key_heads, preferred_element_type=jnp.float32)
        * SCORE_SCALE
    )
    grad_keys = (
        jnp.einsum("hqk,qhd->khd", grad_scores, query_heads, preferred_element_type=jnp.float32)
        * SCORE_SCALE
    )
    grad_values = jnp.einsum(
        "hqk,qhd->khd",
        attn_probs.astype(jnp.bfloat16),
        grad_heads,
        preferred_element_type=jnp.float32,
    )
    return (
        grad_query.reshape(query.shape[0], -1),
        grad_keys.reshape(key_rows.shape[0], -1),
        grad_values.reshape(value_rows.shape[0], -1),
    )


def local(
    tokens,
    cotangent,
    clip_len,
    ln_params,
    w_self,
    w_self_out,
    w_offer,
    w_query,
    w_cross_out,
    w_up,
    w_down,
):
    place_index = lax.axis_index("clip")
    quarter = lax.axis_size("clip") // 4
    view_id = jnp.where(place_index < 2 * quarter, 0, jnp.where(place_index < 3 * quarter, 1, 2))
    member = place_index % quarter
    first_quarter = place_index < quarter
    norm_table = ln_params[0]
    self_in = w_self[0]
    self_out = w_self_out[0]
    offer_in = w_offer[0]
    query_in = w_query[0]
    cross_out = w_cross_out[0]
    up_in = w_up[0]
    down_in = w_down[0]
    micro_count, row_count, model_width = tokens.shape
    local_width = query_in.shape[1]
    local_heads = local_width // HEAD_DIM
    clip_count = clip_len.shape[2]
    empty_clips = jnp.zeros((clip_count,), jnp.int32)
    unmatched = jnp.full((row_count,), -1, jnp.int32)
    grad_sums = tuple(
        (
            jnp.zeros(weight.shape, jnp.float32)
            for weight in (
                norm_table,
                self_in,
                self_out,
                offer_in,
                query_in,
                cross_out,
                up_in,
                down_in,
            )
        )
    )
    layer_rows = []
    grad_rows = []
    for micro in range(micro_count):
        lengths = clip_len[micro]
        own_set = lax.dynamic_index_in_dim(
            lengths, jnp.minimum(place_index, 2 * quarter - 1), 0, keepdims=False
        )
        first_set = lax.dynamic_index_in_dim(lengths, member, 0, keepdims=False)
        second_set = lax.dynamic_index_in_dim(lengths, member + quarter, 0, keepdims=False)
        small_ids = clip_ids(jnp.concatenate([first_set, second_set]), row_count)
        self_ids = jnp.where(
            view_id == 0,
            clip_ids(jnp.concatenate([2 * own_set, empty_clips]), row_count),
            small_ids,
        )
        first_ids = clip_ids(jnp.concatenate([2 * first_set, empty_clips]), row_count)
        second_ids = (
            clip_ids(jnp.concatenate([2 * second_set, empty_clips]), row_count) + clip_count
        )
        key_ids = jnp.where(
            view_id == 1,
            jnp.concatenate([second_ids, first_ids]),
            jnp.concatenate([small_ids, unmatched]),
        )
        inputs = tokens[micro].astype(jnp.float32)
        normed = normalize(inputs, norm_table[0], norm_table[1]).astype(jnp.bfloat16)
        self_qkv = jnp.einsum(
            "rd,cde->cre", normed, self_in, preferred_element_type=jnp.float32
        ).astype(jnp.bfloat16)
        self_mix, self_lse = attend(self_qkv[0], self_qkv[1], self_qkv[2], self_ids, self_ids)
        self_mix = self_mix.astype(jnp.bfloat16)
        hidden = inputs + head_total(product(self_mix, self_out))
        joined = normalize(hidden, norm_table[2], norm_table[3]).astype(jnp.bfloat16)

        def make_offer():
            offered_rows = jnp.einsum(
                "rd,cde->rce", joined, offer_in, preferred_element_type=jnp.float32
            )
            return offered_rows.reshape(row_count, 2 * local_width).astype(jnp.bfloat16)

        def skip_offer():
            return jnp.zeros((row_count, 2 * local_width), jnp.bfloat16)

        offered = lax.cond(view_id < 2, make_offer, skip_offer)
        parcel = offered
        arrived = []
        for turn in range(2):
            parcel = shifted(parcel, "clip", quarter)
            arrived.append(parcel)
        sources = jnp.concatenate(arrived, axis=0)

        def cross_forward():
            cross_query = product(joined, query_in).astype(jnp.bfloat16)
            cross_mix, cross_lse = attend(
                cross_query, sources[:, :local_width], sources[:, local_width:], small_ids, key_ids
            )
            cross_mix = cross_mix.astype(jnp.bfloat16)
            return (product(cross_mix, cross_out), cross_query, cross_mix, cross_lse)

        def skip_cross():
            return (
                jnp.zeros((row_count, model_width), jnp.float32),
                jnp.zeros((row_count, local_width), jnp.bfloat16),
                jnp.zeros((row_count, local_width), jnp.bfloat16),
                jnp.zeros((local_heads, row_count, 1), jnp.float32),
            )

        cross_part, cross_query, cross_mix, cross_lse = lax.cond(
            view_id > 0, cross_forward, skip_cross
        )
        second = hidden + head_total(cross_part)
        mlp_in = normalize(second, norm_table[4], norm_table[5]).astype(jnp.bfloat16)
        mlp_pre = product(mlp_in, up_in)
        activated = jax.nn.gelu(mlp_pre, approximate=False).astype(jnp.bfloat16)
        result = second + head_total(product(activated, down_in))
        layer_rows.append(result.astype(jnp.bfloat16))
        grad_out_b = cotangent[micro]
        grad_out = grad_out_b.astype(jnp.float32)
        grad_down = contract_rows(activated, grad_out_b)
        grad_act = contract_cols(grad_out_b, down_in)
        gelu_back = jax.vjp(partial(jax.nn.gelu, approximate=False), mlp_pre)[1]
        grad_up = gelu_back(grad_act)[0].astype(jnp.bfloat16)
        grad_upw = contract_rows(mlp_in, grad_up)
        grad_mlp_in = head_total(contract_cols(grad_up, up_in))
        third_back = jax.vjp(normalize, second, norm_table[4], norm_table[5])[1]
        back_third, gain_third, shift_third = third_back(grad_mlp_in)
        grad_second = grad_out + back_third
        grad_second_b = grad_second.astype(jnp.bfloat16)

        def cross_backward():
            grad_cross_out = contract_rows(cross_mix, grad_second_b)
            grad_cross_mix = contract_cols(grad_second_b, cross_out).astype(jnp.bfloat16)
            grad_query, grad_keys, grad_values = attend_back(
                cross_query,
                sources[:, :local_width],
                sources[:, local_width:],
                small_ids,
                key_ids,
                cross_lse,
                grad_cross_mix,
            )
            grad_query = grad_query.astype(jnp.bfloat16)
            grad_query_w = contract_rows(joined, grad_query)
            grad_joined_q = contract_cols(grad_query, query_in)
            grad_sources = jnp.concatenate([grad_keys, grad_values], axis=1).astype(jnp.bfloat16)
            return (grad_cross_out, grad_query_w, grad_joined_q, grad_sources)

        def skip_cross_back():
            return (
                jnp.zeros((local_width, model_width), jnp.float32),
                jnp.zeros((model_width, local_width), jnp.float32),
                jnp.zeros((row_count, model_width), jnp.float32),
                jnp.zeros((2 * row_count, 2 * local_width), jnp.bfloat16),
            )

        grad_cross_w, grad_query_w, grad_joined_q, grad_sources = lax.cond(
            view_id > 0, cross_backward, skip_cross_back
        )
        returned = grad_sources
        returns = []
        for turn in range(2):
            returned = shifted(returned, "clip", -quarter)
            returns.append(returned)
        grad_arrived = jnp.where(first_quarter, returns[1][row_count:], returns[0][:row_count])

        def offer_backward():
            grad_offer = grad_arrived.reshape(row_count, 2, local_width)
            return (
                jnp.einsum("rd,rce->cde", joined, grad_offer, preferred_element_type=jnp.float32),
                jnp.einsum("rce,cde->rd", grad_offer, offer_in, preferred_element_type=jnp.float32),
            )

        def skip_offer_back():
            return (
                jnp.zeros(offer_in.shape, jnp.float32),
                jnp.zeros((row_count, model_width), jnp.float32),
            )

        grad_offer_w, grad_joined_o = lax.cond(view_id < 2, offer_backward, skip_offer_back)
        grad_joined = head_total(grad_joined_q + grad_joined_o)
        middle_back = jax.vjp(normalize, hidden, norm_table[2], norm_table[3])[1]
        back_middle, gain_middle, shift_middle = middle_back(grad_joined)
        grad_hidden = grad_second + back_middle
        grad_hidden_b = grad_hidden.astype(jnp.bfloat16)
        grad_self_w = contract_rows(self_mix, grad_hidden_b)
        grad_self_mix = contract_cols(grad_hidden_b, self_out).astype(jnp.bfloat16)
        grad_q, grad_k, grad_v = attend_back(
            self_qkv[0], self_qkv[1], self_qkv[2], self_ids, self_ids, self_lse, grad_self_mix
        )
        grad_qkv = jnp.stack([grad_q, grad_k, grad_v]).astype(jnp.bfloat16)
        grad_in_w = jnp.einsum("rd,cre->cde", normed, grad_qkv, preferred_element_type=jnp.float32)
        grad_normed = head_total(
            jnp.einsum("cre,cde->rd", grad_qkv, self_in, preferred_element_type=jnp.float32)
        )
        first_back = jax.vjp(normalize, inputs, norm_table[0], norm_table[1])[1]
        back_first, gain_first, shift_first = first_back(grad_normed)
        grad_rows.append(grad_hidden + back_first)
        grad_norms = jnp.stack(
            [gain_first, shift_first, gain_middle, shift_middle, gain_third, shift_third]
        )
        grad_sums = tuple(
            (
                left + right
                for left, right in zip(
                    grad_sums,
                    (
                        grad_norms,
                        grad_in_w,
                        grad_self_w,
                        grad_offer_w,
                        grad_query_w,
                        grad_cross_w,
                        grad_upw,
                        grad_down,
                    ),
                )
            )
        )
    grad_sums = (grad_sums[0],) + grad_sums[1:]
    levels = (2 * quarter).bit_length() - 1
    top_level = levels - 1
    keep_pair = view_id == 0
    for level in range(levels):
        remote = jax.tree.map(
            lambda part, own: part.astype(own.dtype),
            swapped(for_sending(grad_sums), "clip", level),
            grad_sums,
        )
        if level == top_level:
            grad_sums = tuple(
                (
                    jnp.where(keep_pair, local_part + remote_part, local_part)
                    for local_part, remote_part in zip(grad_sums, remote)
                )
            )
        else:
            grad_sums = tuple(
                (local_part + remote_part for local_part, remote_part in zip(grad_sums, remote))
            )
    return (
        jnp.stack(layer_rows),
        jnp.stack(grad_rows),
        grad_sums[0][None],
        grad_sums[1][None],
        grad_sums[2][None],
        grad_sums[3][None],
        grad_sums[4][None],
        grad_sums[5][None],
        grad_sums[6][None],
        grad_sums[7][None],
    )


def solution(mesh):
    return jax.shard_map(
        local,
        mesh=mesh,
        in_specs=(
            P(None, "clip", None),
            P(None, "clip", None),
            P(),
            P("clip", None, None),
            P("clip", None, None, "head"),
            P("clip", "head", None),
            P("clip", None, None, "head"),
            P("clip", None, "head"),
            P("clip", "head", None),
            P("clip", None, "head"),
            P("clip", "head", None),
        ),
        out_specs=(
            P(None, "clip", None),
            P(None, "clip", None),
            P("clip", None, None),
            P("clip", None, None, "head"),
            P("clip", "head", None),
            P("clip", None, None, "head"),
            P("clip", None, "head"),
            P("clip", "head", None),
            P("clip", None, "head"),
            P("clip", "head", None),
        ),
        check_vma=False,
    )
```

profile of v0, /device:TPU:0, one launch (start us, length us, event | category | flops | bytes accessed | tf_op | source)
XLA Modules:
  0.0 1603.7 jit_solution(15633800864242299022)
XLA Ops:
  46.1 88.6 %all-reduce.47.cloned.1.call-done = (f32[512,768]{1,0:T(8,128)}, f32[512,768]{1,0:T(8,128)}) async-done(((f32[512,768]{1,0:T(8,128)}, f32[512,768]{1,0:T(8,128)}), (f32[512,768]{1,0:T(8,128)}, f32[512,768]{1,0:T(8,128)})) %all-reduce.47.cloned.1.call-update) | async-done | bytes 3145744 | tf_op jit(solution)/shard_map/psum | solution.py:66
  143.4 4.3 collective-permute-start.2
  154.9 10.1 collective-permute-done.2
  165.0 5.3 collective-permute-start.3
  170.4 11.4 collective-permute-done.4
  181.9 5.3 collective-permute-start.5
  192.6 6.1 collective-permute-done.3
  200.8 13.6 collective-permute-done.5
  221.0 115.2 %all-reduce.45.cloned.1.call-done = (f32[512,768]{1,0:T(8,128)}, f32[512,768]{1,0:T(8,128)}) async-done(((f32[512,768]{1,0:T(8,128)}, f32[512,768]{1,0:T(8,128)}), (f32[512,768]{1,0:T(8,128)}, f32[512,768]{1,0:T(8,128)})) %all-reduce.45.cloned.1.call-update) | async-done | bytes 3145744 | tf_op jit(solution)/shard_map/psum | solution.py:66
  339.9 8.9 multiply_convert_fusion.9
  353.9 9.1 multiply_convert_fusion.10
  369.0 86.1 %all-reduce.43.cloned.1.call-done = (f32[512,768]{1,0:T(8,128)}, f32[512,768]{1,0:T(8,128)}) async-done(((f32[512,768]{1,0:T(8,128)}, f32[512,768]{1,0:T(8,128)}), (f32[512,768]{1,0:T(8,128)}, f32[512,768]{1,0:T(8,128)})) %all-reduce.43.cloned.1.call-update) | async-done | bytes 3145744 | tf_op jit(solution)/shard_map/psum | solution.py:66
  455.1 4.2 multiply_reduce_fusion.6
  463.8 5.2 conditional.22
  473.1 10.4 conditional.20
  487.3 23.9 %collective-permute-done.10 = bf16[1024,768]{1,0:T(8,128)(2,1)} collective-permute-done((bf16[1024,768]{1,0:T(8,128)(2,1)}, bf16[1024,768]{1,0:T(8,128)(2,1)}, u32[]{:S(2)}, u32[]{:S(2)}) %collective-permute-start.10) | collective-permute-done | bytes 1572896 | tf_op jit(solution)/shard_map/ppermute | solution.py:19
  512.5 31.3 %collective-permute-done.8 = bf16[1024,768]{1,0:T(8,128)(2,1)} collective-permute-done((bf16[1024,768]{1,0:T(8,128)(2,1)}, bf16[1024,768]{1,0:T(8,128)(2,1)}, u32[]{:S(2)}, u32[]{:S(2)}) %collective-permute-start.8) | collective-permute-done | bytes 1572896 | tf_op jit(solution)/shard_map/ppermute | solution.py:19
  545.1 33.6 %collective-permute-done.11 = bf16[1024,768]{1,0:T(8,128)(2,1)} collective-permute-done((bf16[1024,768]{1,0:T(8,128)(2,1)}, bf16[1024,768]{1,0:T(8,128)(2,1)}, u32[]{:S(2)}, u32[]{:S(2)}) %collective-permute-start.11) | collective-permute-done | bytes 1572896 | tf_op jit(solution)/shard_map/ppermute | solution.py:19
  578.7 14.7 conditional.23
  596.6 22.6 %collective-permute-done.9 = bf16[1024,768]{1,0:T(8,128)(2,1)} collective-permute-done((bf16[1024,768]{1,0:T(8,128)(2,1)}, bf16[1024,768]{1,0:T(8,128)(2,1)}, u32[]{:S(2)}, u32[]{:S(2)}) %collective-permute-start.9) | collective-permute-done | bytes 1572896 | tf_op jit(solution)/shard_map/ppermute | solution.py:19
  619.2 14.3 conditional.21
  637.5 115.1 %all-reduce.41.cloned.1.call-done = (f32[512,768]{1,0:T(8,128)}, f32[512,768]{1,0:T(8,128)}) async-done(((f32[512,768]{1,0:T(8,128)}, f32[512,768]{1,0:T(8,128)}), (f32[512,768]{1,0:T(8,128)}, f32[512,768]{1,0:T(8,128)})) %all-reduce.41.cloned.1.call-update) | async-done | bytes 3145744 | tf_op jit(solution)/shard_map/psum | solution.py:66
  752.6 4.6 multiply_reduce_fusion.7
  793.9 4.2 fusion.208
  803.3 83.4 %all-reduce.39.cloned.1.call-done = (f32[512,768]{1,0:T(8,128)}, f32[512,768]{1,0:T(8,128)}) async-done(((f32[512,768]{1,0:T(8,128)}, f32[512,768]{1,0:T(8,128)}), (f32[512,768]{1,0:T(8,128)}, f32[512,768]{1,0:T(8,128)})) %all-reduce.39.cloned.1.call-update) | async-done | bytes 3145744 | tf_op jit(solution)/shard_map/psum | solution.py:66
  886.7 4.4 fusion.178
  901.4 51.6 %all-reduce.29.cloned.1.call-done = f32[512,768]{1,0:T(8,128)} async-done(((f32[512,768]{1,0:T(8,128)}), f32[512,768]{1,0:T(8,128)}) %all-reduce.29.cloned.1.call-update) | async-done | bytes 1572880 | tf_op jit(solution)/shard_map/psum | solution.py:66
  959.6 4.3 collective-permute-start
  964.4 15.7 collective-permute-done
  980.1 4.6 collective-permute-start.1
  984.8 4.8 fusion.105
  994.4 6.3 collective-permute-done.1
  1005.0 5.4 fusion.268
  1019.1 4.3 fusion.261
  1024.0 46.3 %all-reduce.31.cloned.1.call-done = f32[512,768]{1,0:T(8,128)} async-done(((f32[512,768]{1,0:T(8,128)}), f32[512,768]{1,0:T(8,128)}) %all-reduce.31.cloned.1.call-update) | async-done | bytes 1572880 | tf_op jit(solution)/shard_map/psum | solution.py:66
  1073.5 8.9 multiply_convert_fusion.11
  1096.4 5.9 fusion.400
  1106.2 35.0 %all-reduce.33.cloned.1.call-done = f32[512,768]{1,0:T(8,128)} async-done(((f32[512,768]{1,0:T(8,128)}), f32[512,768]{1,0:T(8,128)}) %all-reduce.33.cloned.1.call-update) | async-done | bytes 1572880 | tf_op jit(solution)/shard_map/psum | solution.py:66
  1147.3 5.2 conditional.18
  1156.5 9.4 fusion.399
  1177.2 16.1 %collective-permute-done.6 = bf16[1024,768]{1,0:T(8,128)(2,1)S(1)} collective-permute-done((bf16[1024,768]{1,0:T(8,128)(2,1)}, bf16[1024,768]{1,0:T(8,128)(2,1)S(1)}, u32[]{:S(2)}, u32[]{:S(2)}) %collective-permute-start.6) | collective-permute-done | bytes 1572896 | tf_op jit(solution)/shard_map/ppermute | solution.py:19
  1201.8 34.0 %collective-permute-start.29 = (bf16[384,768]{1,0:T(8,128)(2,1)}, bf16[384,768]{1,0:T(8,128)(2,1)}, u32[]{:S(2)}, u32[]{:S(2)}) collective-permute-start(bf16[384,768]{1,0:T(8,128)(2,1)} %fusion.315), channel_id=1, source_target_pairs={{0,8},{2,10},{4,12},{6,14},{8,0},{10,2},{12,4},{14,6},{16,24},{18,... | collective-permute-start | bytes 1769480 | tf_op jit(solution)/shard_map/ppermute | solution.py:29
  1237.0 9.3 collective-permute-start.26
  1246.3 17.7 %collective-permute-done.7 = bf16[1024,768]{1,0:T(8,128)(2,1)S(1)} collective-permute-done((bf16[1024,768]{1,0:T(8,128)(2,1)S(1)}, bf16[1024,768]{1,0:T(8,128)(2,1)S(1)}, u32[]{:S(2)}, u32[]{:S(2)}) %collective-permute-start.7) | collective-permute-done | bytes 1572896 | tf_op jit(solution)/shard_map/ppermute | solution.py:19
  1264.0 13.5 conditional.19
  1280.9 5.4 fusion.63
  1292.6 5.3 fusion.365
  1298.0 34.2 %all-reduce.35.cloned.1.call-done = f32[512,768]{1,0:T(8,128)} async-done(((f32[512,768]{1,0:T(8,128)}), f32[512,768]{1,0:T(8,128)}) %all-reduce.35.cloned.1.call-update) | async-done | bytes 1572880 | tf_op jit(solution)/shard_map/psum | solution.py:66
  1357.5 4.8 fusion.227
  1367.4 5.2 bitcast_convert_fusion
  1372.6 4.8 fusion.146
  1390.5 5.1 fusion.220
  1397.0 4.8 fusion.145
  1403.1 6.5 collective-permute-done.22
  1412.8 19.0 %collective-permute-done.35 = bf16[1536,768]{1,0:T(8,128)(2,1)} collective-permute-done((bf16[1536,768]{1,0:T(8,128)(2,1)}, bf16[1536,768]{1,0:T(8,128)(2,1)}, u32[]{:S(2)}, u32[]{:S(2)}) %collective-permute-start.35) | collective-permute-done | bytes 2359328 | tf_op jit(solution)/shard_map/ppermute | solution.py:29
  1431.8 6.7 fusion.61
  1438.5 8.8 collective-permute-done.16
  1450.1 9.0 collective-permute-done.19
  1459.9 22.5 %collective-permute-done.32 = bf16[768,1536]{1,0:T(8,128)(2,1)} collective-permute-done((bf16[768,1536]{1,0:T(8,128)(2,1)}, bf16[768,1536]{1,0:T(8,128)(2,1)}, u32[]{:S(2)}, u32[]{:S(2)}) %collective-permute-start.32) | collective-permute-done | bytes 2359328 | tf_op jit(solution)/shard_map/ppermute | solution.py:29
  1482.4 6.8 fusion.60
  1489.1 68.4 %collective-permute-done.20 = bf16[384,768]{1,0:T(8,128)(2,1)S(1)} collective-permute-done((bf16[384,768]{1,0:T(8,128)(2,1)S(1)}, bf16[384,768]{1,0:T(8,128)(2,1)S(1)}, u32[]{:S(2)}, u32[]{:S(2)}) %collective-permute-start.20) | collective-permute-done | bytes 589856 | tf_op jit(solution)/shard_map/ppermute | solution.py:29
  1562.5 4.1 fusion.62
  1566.6 5.4 copy.118
  1572.2 4.1 fusion.172
  (942 shorter events, 392.7 us)
Async XLA Ops:
  7.2 332.7 %copy-start = (bf16[1,768,1536]{2,1,0:T(8,128)(2,1)S(1)}, bf16[1,768,1536]{2,1,0:T(8,128)(2,1)}, u32[]{:S(2)}) copy-start(bf16[1,768,1536]{2,1,0:T(8,128)(2,1)} %param.44) | copy-start | bytes 7077892
  7.2 127.5 %all-reduce.47.cloned.1.call-start = ((), (), s32[]{:S(2)}) async-start(), calls=%async_computation.9 | async-start | bytes 6291456 | tf_op jit(solution)/shard_map/psum | solution.py:66
  9.8 206.7 %copy-start.177 = (s32[512]{0:T(512)}, s32[512]{0:T(512)S(1)}, u32[]{:S(2)}) copy-start(s32[512]{0:T(512)S(1)} %convert_reduce_fusion.9) | copy-start | bytes 6148
  15.6 123.0 %copy-start.143 = (f32[768]{0:T(1024)}, f32[768]{0:T(1024)S(1)}, u32[]{:S(2)}) copy-start(f32[768]{0:T(1024)S(1)} %get-tuple-element.436) | copy-start | bytes 9220
  45.2 291.0 %all-reduce.45.cloned.1.call-start = ((), (), s32[]{:S(2)}) async-start(), calls=%async_computation.8 | async-start | bytes 6291456 | tf_op jit(solution)/shard_map/psum | solution.py:66
  143.4 21.6 %collective-permute-start.2 = (bf16[512,768]{0,1:T(8,128)(2,1)}, bf16[512,768]{0,1:T(8,128)(2,1)}, u32[]{:S(2)}, u32[]{:S(2)}) collective-permute-start(bf16[512,768]{0,1:T(8,128)(2,1)} %get-tuple-element.662), channel_id=1, source_target_pairs={{0,8},{2,10},{4,12},{6,14},{8,16},{10,18},{12,20},{14,22},{16,24},... | collective-permute-start | bytes 2359304 | tf_op jit(solution)/shard_map/ppermute | solution.py:19
  151.1 30.8 %collective-permute-start.4 = (bf16[512,768]{0,1:T(8,128)(2,1)}, bf16[512,768]{0,1:T(8,128)(2,1)}, u32[]{:S(2)}, u32[]{:S(2)}) collective-permute-start(bf16[512,768]{0,1:T(8,128)(2,1)} %get-tuple-element.663), channel_id=1, source_target_pairs={{0,8},{2,10},{4,12},{6,14},{8,16},{10,18},{12,20},{14,22},{16,24},... | collective-permute-start | bytes 2359304 | tf_op jit(solution)/shard_map/ppermute | solution.py:19
  165.0 33.7 %collective-permute-start.3 = (bf16[512,768]{0,1:T(8,128)(2,1)}, bf16[512,768]{0,1:T(8,128)(2,1)}, u32[]{:S(2)}, u32[]{:S(2)}) collective-permute-start(bf16[512,768]{0,1:T(8,128)(2,1)} %collective-permute-done.2), channel_id=1, source_target_pairs={{0,8},{2,10},{4,12},{6,14},{8,16},{10,18},{12,20},{14,22},{16,24},... | collective-permute-start | bytes 2359304 | tf_op jit(solution)/shard_map/ppermute | solution.py:19
  181.9 32.6 %collective-permute-start.5 = (bf16[512,768]{0,1:T(8,128)(2,1)}, bf16[512,768]{0,1:T(8,128)(2,1)}, u32[]{:S(2)}, u32[]{:S(2)}) collective-permute-start(bf16[512,768]{0,1:T(8,128)(2,1)} %collective-permute-done.4), channel_id=1, source_target_pairs={{0,8},{2,10},{4,12},{6,14},{8,16},{10,18},{12,20},{14,22},{16,24},... | collective-permute-start | bytes 2359304 | tf_op jit(solution)/shard_map/ppermute | solution.py:19
  220.8 234.2 %all-reduce.43.cloned.1.call-start = ((), (), s32[]{:S(2)}) async-start(), calls=%async_computation.7 | async-start | bytes 6291456 | tf_op jit(solution)/shard_map/psum | solution.py:66
  339.5 119.8 %copy-start.171 = (f32[512]{0:T(512)}, f32[512]{0:T(512)S(1)}, u32[]{:S(2)}) copy-start(f32[512]{0:T(512)S(1)} %broadcast_multiply_fusion) | copy-start | bytes 6148
  339.8 119.4 %copy-start.194 = (f32[512]{0:T(512)}, f32[512]{0:T(512)S(1)}, u32[]{:S(2)}) copy-start(f32[512]{0:T(512)S(1)} %fusion.351) | copy-start | bytes 6148
  353.6 105.7 %copy-start.196 = (f32[512]{0:T(512)}, f32[512]{0:T(512)S(1)}, u32[]{:S(2)}) copy-start(f32[512]{0:T(512)S(1)} %broadcast_multiply_fusion.3) | copy-start | bytes 6148
  353.9 105.4 %copy-start.212 = (f32[512]{0:T(512)}, f32[512]{0:T(512)S(1)}, u32[]{:S(2)}) copy-start(f32[512]{0:T(512)S(1)} %fusion.348) | copy-start | bytes 6148
  369.0 383.6 %all-reduce.41.cloned.1.call-start = ((), (), s32[]{:S(2)}) async-start(), calls=%async_computation.6 | async-start | bytes 6291456 | tf_op jit(solution)/shard_map/psum | solution.py:66
  471.7 39.5 %collective-permute-start.10 = (bf16[1024,768]{1,0:T(8,128)(2,1)}, bf16[1024,768]{1,0:T(8,128)(2,1)}, u32[]{:S(2)}, u32[]{:S(2)}) collective-permute-start(bf16[1024,768]{1,0:T(8,128)(2,1)} %copy.102), channel_id=1, source_target_pairs={{8,0},{10,2},{12,4},{14,6},{16,8},{18,10},{20,12},{22,14},{24,16},... | collective-permute-start | bytes 4718600 | tf_op jit(solution)/shard_map/ppermute | solution.py:19
  486.0 57.7 %collective-permute-start.8 = (bf16[1024,768]{1,0:T(8,128)(2,1)}, bf16[1024,768]{1,0:T(8,128)(2,1)}, u32[]{:S(2)}, u32[]{:S(2)}) collective-permute-start(bf16[1024,768]{1,0:T(8,128)(2,1)} %copy.94), channel_id=1, source_target_pairs={{8,0},{10,2},{12,4},{14,6},{16,8},{18,10},{20,12},{22,14},{24,16},... | collective-permute-start | bytes 4718600 | tf_op jit(solution)/shard_map/ppermute | solution.py:19
  511.2 67.5 %collective-permute-start.11 = (bf16[1024,768]{1,0:T(8,128)(2,1)}, bf16[1024,768]{1,0:T(8,128)(2,1)}, u32[]{:S(2)}, u32[]{:S(2)}) collective-permute-start(bf16[1024,768]{1,0:T(8,128)(2,1)} %collective-permute-done.10), channel_id=1, source_target_pairs={{8,0},{10,2},{12,4},{14,6},{16,8},{18,10},{20,12},{22,14},{24,16},... | collective-permute-start | bytes 4718600 | tf_op jit(solution)/shard_map/ppermute | solution.py:19
  543.8 75.4 %collective-permute-start.9 = (bf16[1024,768]{1,0:T(8,128)(2,1)}, bf16[1024,768]{1,0:T(8,128)(2,1)}, u32[]{:S(2)}, u32[]{:S(2)}) collective-permute-start(bf16[1024,768]{1,0:T(8,128)(2,1)} %collective-permute-done.8), channel_id=1, source_target_pairs={{8,0},{10,2},{12,4},{14,6},{16,8},{18,10},{20,12},{22,14},{24,16},... | collective-permute-start | bytes 4718600 | tf_op jit(solution)/shard_map/ppermute | solution.py:19
  636.7 115.8 %copy-start.144 = (f32[768]{0:T(1024)S(1)}, f32[768]{0:T(1024)}, u32[]{:S(2)}) copy-start(f32[768]{0:T(1024)} %copy-done.143) | copy-start | bytes 9220
  636.7 115.8 %copy-start.174 = (f32[512]{0:T(512)S(1)}, f32[512]{0:T(512)}, u32[]{:S(2)}) copy-start(f32[512]{0:T(512)} %copy-done.173) | copy-start | bytes 6148
  636.7 115.8 %copy-start.176 = (f32[512]{0:T(512)S(1)}, f32[512]{0:T(512)}, u32[]{:S(2)}) copy-start(f32[512]{0:T(512)} %copy-done.175) | copy-start | bytes 6148
  636.7 115.8 %copy-start.199 = (f32[512]{0:T(512)S(1)}, f32[512]{0:T(512)}, u32[]{:S(2)}) copy-start(f32[512]{0:T(512)} %copy-done.198) | copy-start | bytes 6148
  636.8 115.8 %copy-start.201 = (f32[512]{0:T(512)S(1)}, f32[512]{0:T(512)}, u32[]{:S(2)}) copy-start(f32[512]{0:T(512)} %copy-done.200) | copy-start | bytes 6148
  636.8 249.9 %all-reduce.39.cloned.1.call-start = ((), (), s32[]{:S(2)}) async-start(), calls=%async_computation.5 | async-start | bytes 6291456 | tf_op jit(solution)/shard_map/psum | solution.py:66
  800.5 86.2 %copy-start.146 = (f32[768]{0:T(1024)S(1)}, f32[768]{0:T(1024)}, u32[]{:S(2)}) copy-start(f32[768]{0:T(1024)} %copy-done.145) | copy-start | bytes 9220
  800.6 86.2 %copy-start.163 = (f32[512]{0:T(512)S(1)}, f32[512]{0:T(512)}, u32[]{:S(2)}) copy-start(f32[512]{0:T(512)} %copy-done.162) | copy-start | bytes 6148
  800.6 86.2 %copy-start.183 = (f32[512]{0:T(512)S(1)}, f32[512]{0:T(512)}, u32[]{:S(2)}) copy-start(f32[512]{0:T(512)} %copy-done.182) | copy-start | bytes 6148
  800.6 152.4 %all-reduce.29.cloned.1.call-start = ((), (), s32[]{:S(2)}) async-start(), calls=%async_computation | async-start | bytes 3145728 | tf_op jit(solution)/shard_map/psum | solution.py:66
  802.9 198.8 %copy-start.179 = (s32[512]{0:T(512)}, s32[512]{0:T(512)S(1)}, u32[]{:S(2)}) copy-start(s32[512]{0:T(512)S(1)} %convert_reduce_fusion.13) | copy-start | bytes 6148
  803.0 88.1 %copy-start.185 = (f32[512]{0:T(512)}, f32[512]{0:T(512)S(1)}, u32[]{:S(2)}) copy-start(f32[512]{0:T(512)S(1)} %broadcast_multiply_fusion.8) | copy-start | bytes 6148
  901.3 168.9 %all-reduce.31.cloned.1.call-start = ((), (), s32[]{:S(2)}) async-start(), calls=%async_computation.1 | async-start | bytes 3145728 | tf_op jit(solution)/shard_map/psum | solution.py:66
  956.3 190.9 %copy-start.64 = (bf16[512,768]{1,0:T(8,128)(2,1)}, bf16[512,768]{1,0:T(8,128)(2,1)S(1)}, u32[]{:S(2)}) copy-start(bf16[512,768]{1,0:T(8,128)(2,1)S(1)} %add_convert_fusion.11) | copy-start | bytes 2359300
  959.6 20.5 %collective-permute-start = (bf16[512,768]{0,1:T(8,128)(2,1)}, bf16[512,768]{0,1:T(8,128)(2,1)}, u32[]{:S(2)}, u32[]{:S(2)}) collective-permute-start(bf16[512,768]{0,1:T(8,128)(2,1)} %get-tuple-element.661), channel_id=1, source_target_pairs={{0,8},{2,10},{4,12},{6,14},{8,16},{10,18},{12,20},{14,22},{16,24},... | collective-permute-start | bytes 2359304 | tf_op jit(solution)/shard_map/ppermute | solution.py:19
  980.1 20.6 %collective-permute-start.1 = (bf16[512,768]{0,1:T(8,128)(2,1)}, bf16[512,768]{0,1:T(8,128)(2,1)S(1)}, u32[]{:S(2)}, u32[]{:S(2)}) collective-permute-start(bf16[512,768]{0,1:T(8,128)(2,1)} %collective-permute-done), channel_id=1, source_target_pairs={{0,8},{2,10},{4,12},{6,14},{8,16},{10,18},{12,20},{14,22},{16,24},... | collective-permute-start | bytes 2359304 | tf_op jit(solution)/shard_map/ppermute | solution.py:19
  1004.4 136.8 %all-reduce.33.cloned.1.call-start = ((), (), s32[]{:S(2)}) async-start(), calls=%async_computation.2 | async-start | bytes 3145728 | tf_op jit(solution)/shard_map/psum | solution.py:66
  1089.6 242.6 %all-reduce.35.cloned.1.call-start = ((), (), s32[]{:S(2)}) async-start(), calls=%async_computation.3 | async-start | bytes 3145728 | tf_op jit(solution)/shard_map/psum | solution.py:66
  1102.3 94.0 %collective-permute-start.33 = (bf16[1536,768]{1,0:T(8,128)(2,1)}, bf16[1536,768]{1,0:T(8,128)(2,1)}, u32[]{:S(2)}, u32[]{:S(2)}) collective-permute-start(bf16[1536,768]{1,0:T(8,128)(2,1)} %get-tuple-element.579), channel_id=1, source_target_pairs={{0,2},{2,0},{4,6},{6,4},{8,10},{10,8},{12,14},{14,12},{16,18},{18,... | collective-permute-start | bytes 7077896 | tf_op jit(solution)/shard_map/ppermute | solution.py:29
  1155.1 38.2 %collective-permute-start.6 = (bf16[1024,768]{1,0:T(8,128)(2,1)}, bf16[1024,768]{1,0:T(8,128)(2,1)S(1)}, u32[]{:S(2)}, u32[]{:S(2)}) collective-permute-start(bf16[1024,768]{1,0:T(8,128)(2,1)} %copy.86), channel_id=1, source_target_pairs={{8,0},{10,2},{12,4},{14,6},{16,8},{18,10},{20,12},{22,14},{24,16},... | collective-permute-start | bytes 4718600 | tf_op jit(solution)/shard_map/ppermute | solution.py:19
  1165.8 115.0 %collective-permute-start.30 = (bf16[768,1536]{1,0:T(8,128)(2,1)}, bf16[768,1536]{1,0:T(8,128)(2,1)}, u32[]{:S(2)}, u32[]{:S(2)}) collective-permute-start(bf16[768,1536]{1,0:T(8,128)(2,1)} %get-tuple-element.577), channel_id=1, source_target_pairs={{0,2},{2,0},{4,6},{6,4},{8,10},{10,8},{12,14},{14,12},{16,18},{18,... | collective-permute-start | bytes 7077896 | tf_op jit(solution)/shard_map/ppermute | solution.py:29
  1168.1 7.5 collective-permute-start.27
  1171.0 23.6 %collective-permute-start.24 = (bf16[768,384]{1,0:T(8,128)(2,1)S(1)}, bf16[768,384]{1,0:T(8,128)(2,1)S(1)}, u32[]{:S(2)}, u32[]{:S(2)}) collective-permute-start(bf16[768,384]{1,0:T(8,128)(2,1)S(1)} %get-tuple-element.465), channel_id=1, source_target_pairs={{0,2},{2,0},{4,6},{6,4},{8,10},{10,8},{12,14},{14,12},{16,18},{18,... | collective-permute-start | bytes 1769480 | tf_op jit(solution)/shard_map/ppermute | solution.py:29
  1175.7 25.1 %collective-permute-start.28 = (bf16[384,768]{1,0:T(8,128)(2,1)S(1)}, bf16[384,768]{1,0:T(8,128)(2,1)S(1)}, u32[]{:S(2)}, u32[]{:S(2)}) collective-permute-start(bf16[384,768]{1,0:T(8,128)(2,1)S(1)} %fusion.248), channel_id=1, source_target_pairs={{0,4},{2,6},{4,0},{6,2},{8,12},{10,14},{12,8},{14,10},{16,20},{18,... | collective-permute-start | bytes 1769480 | tf_op jit(solution)/shard_map/ppermute | solution.py:29
  1193.4 70.6 %collective-permute-start.7 = (bf16[1024,768]{1,0:T(8,128)(2,1)S(1)}, bf16[1024,768]{1,0:T(8,128)(2,1)S(1)}, u32[]{:S(2)}, u32[]{:S(2)}) collective-permute-start(bf16[1024,768]{1,0:T(8,128)(2,1)S(1)} %collective-permute-done.6), channel_id=1, source_target_pairs={{8,0},{10,2},{12,4},{14,6},{16,8},{18,10},{20,12},{22,14},{24,16},... | collective-permute-start | bytes 4718600 | tf_op jit(solution)/shard_map/ppermute | solution.py:19
  1194.8 41.1 %collective-permute-start.25 = (bf16[768,384]{1,0:T(8,128)(2,1)S(1)}, bf16[768,384]{1,0:T(8,128)(2,1)S(1)}, u32[]{:S(2)}, u32[]{:S(2)}) collective-permute-start(bf16[768,384]{1,0:T(8,128)(2,1)S(1)} %fusion.247), channel_id=1, source_target_pairs={{0,4},{2,6},{4,0},{6,2},{8,12},{10,14},{12,8},{14,10},{16,20},{18,... | collective-permute-start | bytes 1769480 | tf_op jit(solution)/shard_map/ppermute | solution.py:29
  1200.2 172.4 %collective-permute-start.34 = (bf16[1536,768]{1,0:T(8,128)(2,1)}, bf16[1536,768]{1,0:T(8,128)(2,1)}, u32[]{:S(2)}, u32[]{:S(2)}) collective-permute-start(bf16[1536,768]{1,0:T(8,128)(2,1)} %fusion.64), channel_id=1, source_target_pairs={{0,4},{2,6},{4,0},{6,2},{8,12},{10,14},{12,8},{14,10},{16,20},{18,... | collective-permute-start | bytes 7077896 | tf_op jit(solution)/shard_map/ppermute | solution.py:29
  1201.8 86.0 %collective-permute-start.29 = (bf16[384,768]{1,0:T(8,128)(2,1)}, bf16[384,768]{1,0:T(8,128)(2,1)}, u32[]{:S(2)}, u32[]{:S(2)}) collective-permute-start(bf16[384,768]{1,0:T(8,128)(2,1)} %fusion.315), channel_id=1, source_target_pairs={{0,8},{2,10},{4,12},{6,14},{8,0},{10,2},{12,4},{14,6},{16,24},{18,... | collective-permute-start | bytes 1769480 | tf_op jit(solution)/shard_map/ppermute | solution.py:29
  1237.0 53.2 %collective-permute-start.26 = (bf16[768,384]{1,0:T(8,128)(2,1)}, bf16[768,384]{1,0:T(8,128)(2,1)}, u32[]{:S(2)}, u32[]{:S(2)}) collective-permute-start(bf16[768,384]{1,0:T(8,128)(2,1)} %fusion.314), channel_id=1, source_target_pairs={{0,8},{2,10},{4,12},{6,14},{8,0},{10,2},{12,4},{14,6},{16,24},{18,... | collective-permute-start | bytes 1769480 | tf_op jit(solution)/shard_map/ppermute | solution.py:29
  1280.6 291.4 %all-reduce.37.cloned.1.call-start = ((), (), s32[]{:S(2)}) async-start(), calls=%async_computation.4 | async-start | bytes 12582912 | tf_op jit(solution)/shard_map/psum | solution.py:66
  1286.3 110.6 %collective-permute-start.31 = (bf16[768,1536]{1,0:T(8,128)(2,1)}, bf16[768,1536]{1,0:T(8,128)(2,1)}, u32[]{:S(2)}, u32[]{:S(2)}) collective-permute-start(bf16[768,1536]{1,0:T(8,128)(2,1)} %fusion.63), channel_id=1, source_target_pairs={{0,4},{2,6},{4,0},{6,2},{8,12},{10,14},{12,8},{14,10},{16,20},{18,... | collective-permute-start | bytes 7077896 | tf_op jit(solution)/shard_map/ppermute | solution.py:29
  1298.0 81.0 %collective-permute-start.21 = (bf16[2,768,384]{2,1,0:T(8,128)(2,1)}, bf16[2,768,384]{2,1,0:T(8,128)(2,1)S(1)}, u32[]{:S(2)}, u32[]{:S(2)}) collective-permute-start(bf16[2,768,384]{2,1,0:T(8,128)(2,1)} %get-tuple-element.467), channel_id=1, source_target_pairs={{0,2},{2,0},{4,6},{6,4},{8,10},{10,8},{12,14},{14,12},{16,18},{18,... | collective-permute-start | bytes 3538952 | tf_op jit(solution)/shard_map/ppermute | solution.py:29
  1372.6 17.9 %collective-permute-start.15 = (bf16[3,768,384]{1,2,0:T(8,128)(2,1)}, bf16[3,768,384]{1,2,0:T(8,128)(2,1)}, u32[]{:S(2)}, u32[]{:S(2)}) collective-permute-start(bf16[3,768,384]{1,2,0:T(8,128)(2,1)} %get-tuple-element.573), channel_id=1, source_target_pairs={{0,2},{2,0},{4,6},{6,4},{8,10},{10,8},{12,14},{14,12},{16,18},{18,... | collective-permute-start | bytes 5308424 | tf_op jit(solution)/shard_map/ppermute | solution.py:29
  1377.4 54.4 %collective-permute-start.35 = (bf16[1536,768]{1,0:T(8,128)(2,1)}, bf16[1536,768]{1,0:T(8,128)(2,1)}, u32[]{:S(2)}, u32[]{:S(2)}) collective-permute-start(bf16[1536,768]{1,0:T(8,128)(2,1)} %fusion.146), channel_id=1, source_target_pairs={{0,8},{2,10},{4,12},{6,14},{8,0},{10,2},{12,4},{14,6},{16,24},{18,... | collective-permute-start | bytes 7077896 | tf_op jit(solution)/shard_map/ppermute | solution.py:29
  1380.4 29.1 %collective-permute-start.22 = (bf16[2,768,384]{2,1,0:T(8,128)(2,1)}, bf16[2,768,384]{2,1,0:T(8,128)(2,1)}, u32[]{:S(2)}, u32[]{:S(2)}) collective-permute-start(bf16[2,768,384]{2,1,0:T(8,128)(2,1)} %fusion.165), channel_id=1, source_target_pairs={{0,4},{2,6},{4,0},{6,2},{8,12},{10,14},{12,8},{14,10},{16,20},{18,... | collective-permute-start | bytes 3538952 | tf_op jit(solution)/shard_map/ppermute | solution.py:29
  1390.4 11.5 collective-permute-start.18
  1395.6 51.7 %collective-permute-start.16 = (bf16[3,768,384]{1,2,0:T(8,128)(2,1)}, bf16[3,768,384]{1,2,0:T(8,128)(2,1)S(1)}, u32[]{:S(2)}, u32[]{:S(2)}) collective-permute-start(bf16[3,768,384]{1,2,0:T(8,128)(2,1)} %fusion.220), channel_id=1, source_target_pairs={{0,4},{2,6},{4,0},{6,2},{8,12},{10,14},{12,8},{14,10},{16,20},{18,... | collective-permute-start | bytes 5308424 | tf_op jit(solution)/shard_map/ppermute | solution.py:29
  1401.8 80.6 %collective-permute-start.32 = (bf16[768,1536]{1,0:T(8,128)(2,1)}, bf16[768,1536]{1,0:T(8,128)(2,1)}, u32[]{:S(2)}, u32[]{:S(2)}) collective-permute-start(bf16[768,1536]{1,0:T(8,128)(2,1)} %fusion.145), channel_id=1, source_target_pairs={{0,8},{2,10},{4,12},{6,14},{8,0},{10,2},{12,4},{14,6},{16,24},{18,... | collective-permute-start | bytes 7077896 | tf_op jit(solution)/shard_map/ppermute | solution.py:29
  1402.0 57.1 %collective-permute-start.19 = (bf16[384,768]{1,0:T(8,128)(2,1)S(1)}, bf16[384,768]{1,0:T(8,128)(2,1)S(1)}, u32[]{:S(2)}, u32[]{:S(2)}) collective-permute-start(bf16[384,768]{1,0:T(8,128)(2,1)S(1)} %fusion.246), channel_id=1, source_target_pairs={{0,4},{2,6},{4,0},{6,2},{8,12},{10,14},{12,8},{14,10},{16,20},{18,... | collective-permute-start | bytes 1769480 | tf_op jit(solution)/shard_map/ppermute | solution.py:29
  1412.3 146.6 %collective-permute-start.23 = (bf16[2,768,384]{2,1,0:T(8,128)(2,1)}, bf16[2,768,384]{2,1,0:T(8,128)(2,1)}, u32[]{:S(2)}, u32[]{:S(2)}) collective-permute-start(bf16[2,768,384]{2,1,0:T(8,128)(2,1)} %fusion.245), channel_id=1, source_target_pairs={{0,8},{2,10},{4,12},{6,14},{8,0},{10,2},{12,4},{14,6},{16,24},{18,... | collective-permute-start | bytes 3538952 | tf_op jit(solution)/shard_map/ppermute | solution.py:29
  1449.5 113.0 %collective-permute-start.17 = (bf16[3,768,384]{1,2,0:T(8,128)(2,1)S(1)}, bf16[3,768,384]{1,2,0:T(8,128)(2,1)S(1)}, u32[]{:S(2)}, u32[]{:S(2)}) collective-permute-start(bf16[3,768,384]{1,2,0:T(8,128)(2,1)S(1)} %fusion.95), channel_id=1, source_target_pairs={{0,8},{2,10},{4,12},{6,14},{8,0},{10,2},{12,4},{14,6},{16,24},{18,... | collective-permute-start | bytes 5308424 | tf_op jit(solution)/shard_map/ppermute | solution.py:29
  1459.3 98.3 %collective-permute-start.20 = (bf16[384,768]{1,0:T(8,128)(2,1)S(1)}, bf16[384,768]{1,0:T(8,128)(2,1)S(1)}, u32[]{:S(2)}, u32[]{:S(2)}) collective-permute-start(bf16[384,768]{1,0:T(8,128)(2,1)S(1)} %fusion.313), channel_id=1, source_target_pairs={{0,8},{2,10},{4,12},{6,14},{8,0},{10,2},{12,4},{14,6},{16,24},{18,... | collective-permute-start | bytes 1769480 | tf_op jit(solution)/shard_map/ppermute | solution.py:29
  1580.0 8.0 collective-permute-start.12
  1588.0 4.0 collective-permute-start.13
  1592.1 3.8 collective-permute-start.14
  (270 other events, 1600.9 us)
Sparse Core Ops, SparseCore 0:
  45.4 89.2 all-reduce.46
  220.9 115.2 all-reduce.44
  369.1 85.9 all-reduce.42
  636.9 115.6 all-reduce.40
  800.7 85.9 all-reduce.38
  901.4 51.4 all-reduce.28
  1004.5 65.7 all-reduce.30
  1089.7 51.4 all-reduce.32
  1280.8 51.3 all-reduce.34
  1387.2 152.9 all-reduce.36
where the time goes:
time: 1620 us; the launch traced here: 1600 us
  waiting for transfers between devices  999 us (62%)
  matrix products  188 us (12%)
  other arithmetic  177 us (11%)
  local copies, waits for them, and re-layouts  120 us (7%)
  starting transfers between devices  96 us (6%)
  between operations  18.1 us (1%)
    psum x10, waiting for transfers between devices, head_total(): return lax.psum(partial_sum, 'head')  655 us
    ppermute x12, waiting for transfers between devices, shifted(): return lax.ppermute(block, axis, route)  208 us
    ppermute x24, waiting for transfers between devices, swapped(): return lax.ppermute(value, axis, pairs)  135 us
    ppermute x24, starting transfers between devices, swapped(): return lax.ppermute(value, axis, pairs)  59.5 us
    convert_element_type x20, other arithmetic, for_sending(): a.astype(jnp.bfloat16)  43 us
    dot_general x9, matrix products, product(): return jnp.dot(left, right, preferred_element_type=jnp.float32)  42 us
    unnamed x578, local copies, waits for them, and re-layouts  41.9 us
    dot_general x9, matrix products, contract_rows(): lax.dot_general(left, right, (((0,), (0,)), ((), ())), preferred_element_...  35.9 us
  transfers between devices with their start and end apart: 46, of which 28 were waited for; matrix products, arithmetic and copies ran while one was open for 16% of the time, Pallas kernels for 0%

commit v1 on v0

v1 whole, which is shorter than its diff:
```python
import jax
import jax.numpy as jnp
from jax import lax
from jax.experimental import pallas as pl
from jax.experimental.pallas import tpu as pltpu
from jax.sharding import PartitionSpec as P


HEAD_DIM = 64
EPSILON = 1e-06
SCORE_SCALE = 0.125
MASKED = -1e30
BF16 = jnp.bfloat16
F32 = jnp.float32
VMEM_BYTES = 24 * 1024 * 1024


def over_head(value):
    return lax.ppermute(value, "head", [(0, 1), (1, 0)])


def over_bit(value, bit, count=None):
    count = lax.axis_size("clip") if count is None else count
    return lax.ppermute(value, "clip", [(i, i ^ (1 << bit)) for i in range(count)])


def other_core(value):
    return over_bit(value, 0)


def in_core_order(core, mine, theirs, axis):
    first = jnp.where(core == 0, mine, theirs)
    second = jnp.where(core == 0, theirs, mine)
    return jnp.concatenate([first, second], axis=axis)


def core_piece(value, piece, axis):
    size = value.shape[axis] // 2
    return lax.dynamic_slice_in_dim(value, piece * size, size, axis)


def norm_stats(rows):
    mean = jnp.mean(rows, axis=-1, keepdims=True)
    centered = rows - mean
    variance = jnp.mean(centered * centered, axis=-1, keepdims=True)
    inverse = lax.rsqrt(variance + EPSILON)
    return centered * inverse, inverse


def norm_back(grad, normal, inverse, gain):
    scaled = grad * gain
    mean = jnp.mean(scaled, axis=-1, keepdims=True)
    along = jnp.mean(scaled * normal, axis=-1, keepdims=True)
    grad_rows = (scaled - mean - normal * along) * inverse
    return grad_rows, jnp.sum(grad * normal, axis=0), jnp.sum(grad, axis=0)


def attention_blocks(full, query_rows, key_rows):
    half = key_rows // 2
    if full:
        return [
            (slice(r, r + half), slice(0, key_rows), slice(r, r + half), slice(0, key_rows))
            for r in range(0, query_rows, half)
        ]
    blocks = []
    for s in range(2):
        part = slice(s * half, (s + 1) * half)
        if query_rows == key_rows:
            blocks.append((part, part, part, slice(0, half)))
        else:
            blocks.append((part, part, slice(0, half), part))
    return blocks


def dot_nt(left, right):
    return lax.dot_general(left, right, (((1,), (1,)), ((), ())), preferred_element_type=F32)


def dot_tn(left, right):
    return lax.dot_general(left, right, (((0,), (0,)), ((), ())), preferred_element_type=F32)


def dot_nn(left, right):
    return jnp.dot(left, right, preferred_element_type=F32)


def attend_kernel(query_rows, flag_ref, q_ref, k_ref, v_ref, idq_ref, idk_ref, mix_ref, p_ref, bias_ref):
    key_rows = k_ref.shape[0]
    first_head = lax.broadcasted_iota(jnp.int32, (1, 2 * HEAD_DIM), 1) < HEAD_DIM

    def run(full):
        blocks = attention_blocks(full, query_rows, key_rows)

        @pl.when(pl.program_id(0) == 0)
        def _():
            for rows, keys, p_rows, p_cols in blocks:
                same = idq_ref[rows, :] == idk_ref[:, keys]
                bias_ref[p_rows, p_cols] = jnp.where(same, 0.0, MASKED)

        for rows, keys, p_rows, p_cols in blocks:
            query = q_ref[rows, :] * jnp.asarray(SCORE_SCALE, BF16)
            mixes = []
            for h in range(2):
                wanted = first_head if h == 0 else jnp.logical_not(first_head)
                own = jnp.where(wanted, query, jnp.zeros_like(query))
                scores = dot_nt(own, k_ref[keys, :]) + bias_ref[p_rows, p_cols]
                top = jnp.max(scores, axis=-1, keepdims=True)
                exponent = jnp.exp(scores - top)
                total = jnp.sum(exponent, axis=-1, keepdims=True)
                probs = (exponent * (1.0 / total)).astype(BF16)
                p_ref[h, p_rows, p_cols] = probs
                mixes.append(dot_nn(probs, v_ref[keys, :]))
            mix_ref[rows, :] = jnp.where(first_head, mixes[0], mixes[1]).astype(BF16)

    @pl.when(flag_ref[0] != 0)
    def _():
        run(True)
        if query_rows < key_rows:
            mix_ref[query_rows:, :] = jnp.zeros((key_rows - query_rows, 2 * HEAD_DIM), BF16)

    @pl.when(flag_ref[0] == 0)
    def _():
        run(False)


def attend_back_kernel(query_rows, flag_ref, q_ref, k_ref, v_ref, p_ref, grad_ref, dq_ref, dk_ref, dv_ref):
    key_rows = k_ref.shape[0]
    first_head = lax.broadcasted_iota(jnp.int32, (1, 2 * HEAD_DIM), 1) < HEAD_DIM

    def run(full):
        blocks = attention_blocks(full, query_rows, key_rows)
        sums = {}
        for rows, keys, p_rows, p_cols in blocks:
            query = q_ref[rows, :]
            grad = grad_ref[rows, :]
            dq, dk, dv = [], [], []
            for h in range(2):
                wanted = first_head if h == 0 else jnp.logical_not(first_head)
                own = jnp.where(wanted, grad, jnp.zeros_like(grad))
                probs = p_ref[h, p_rows, p_cols]
                wide_probs = probs.astype(F32)
                grad_probs = dot_nt(own, v_ref[keys, :])
                delta = jnp.sum(wide_probs * grad_probs, axis=-1, keepdims=True)
                grad_scores = (wide_probs * (grad_probs - delta)).astype(BF16)
                dq.append(dot_nn(grad_scores, k_ref[keys, :]))
                dk.append(dot_tn(grad_scores, query))
                dv.append(dot_tn(probs, grad))
            dq_ref[rows, :] = (jnp.where(first_head, dq[0], dq[1]) * SCORE_SCALE).astype(BF16)
            both = (jnp.where(first_head, dk[0], dk[1]), jnp.where(first_head, dv[0], dv[1]))
            at = (keys.start, keys.stop)
            sums[at] = (sums[at][0] + both[0], sums[at][1] + both[1]) if at in sums else both
        for (start, stop), (dk, dv) in sums.items():
            dk_ref[start:stop, :] = (dk * SCORE_SCALE).astype(BF16)
            dv_ref[start:stop, :] = dv.astype(BF16)

    @pl.when(flag_ref[0] != 0)
    def _():
        run(True)
        if query_rows < key_rows:
            dq_ref[query_rows:, :] = jnp.zeros((key_rows - query_rows, 2 * HEAD_DIM), BF16)

    @pl.when(flag_ref[0] == 0)
    def _():
        run(False)


def pair_spec(array, rows, lead=None):
    if array.ndim == 3:
        return pl.BlockSpec((None, rows, 2 * HEAD_DIM), lambda j, flag, lead=lead: (lead, 0, j))
    return pl.BlockSpec((rows, 2 * HEAD_DIM), lambda j, flag: (0, j))


def attention_cost(heads, query_rows, key_rows, matmuls):
    return pl.CostEstimate(
        flops=2 * heads * query_rows * key_rows * 256 * matmuls,
        bytes_accessed=2 * heads * query_rows * key_rows + 8 * heads * key_rows * HEAD_DIM,
        transcendentals=heads * query_rows * key_rows,
    )


def attend(full, query, keys, values, ids, query_rows, heads):
    rows = 512
    id_query, id_keys = ids
    pairs = heads // 2
    return pl.pallas_call(
        lambda *refs: attend_kernel(query_rows, *refs),
        grid_spec=pltpu.PrefetchScalarGridSpec(
            num_scalar_prefetch=1,
            grid=(pairs,),
            in_specs=[pair_spec(a, rows, lead) for a, lead in (query, keys, values)]
            + [
                pl.BlockSpec((rows, 1), lambda j, flag: (0, 0)),
                pl.BlockSpec((1, rows), lambda j, flag: (0, 0)),
            ],
            out_specs=[
                pl.BlockSpec((rows, 2 * HEAD_DIM), lambda j, flag: (0, j)),
                pl.BlockSpec((2, query_rows, rows), lambda j, flag: (j, 0, 0)),
            ],
            scratch_shapes=[pltpu.VMEM((query_rows, rows), F32)],
        ),
        out_shape=[
            jax.ShapeDtypeStruct((rows, heads * HEAD_DIM), BF16),
            jax.ShapeDtypeStruct((heads, query_rows, rows), BF16),
        ],
        compiler_params=pltpu.CompilerParams(vmem_limit_bytes=VMEM_BYTES),
        cost_estimate=attention_cost(heads, query_rows, rows, 2),
        name="attend",
    )(full, query[0], keys[0], values[0], id_query, id_keys)


def attend_back(full, query, keys, values, probs, grad, query_rows, heads):
    rows = 512
    pairs = heads // 2
    out = jax.ShapeDtypeStruct((rows, heads * HEAD_DIM), BF16)
    out_spec = pl.BlockSpec((rows, 2 * HEAD_DIM), lambda j, flag: (0, j))
    return pl.pallas_call(
        lambda *refs: attend_back_kernel(query_rows, *refs),
        grid_spec=pltpu.PrefetchScalarGridSpec(
            num_scalar_prefetch=1,
            grid=(pairs,),
            in_specs=[pair_spec(a, rows, lead) for a, lead in (query, keys, values)]
            + [
                pl.BlockSpec((2, query_rows, rows), lambda j, flag: (j, 0, 0)),
                pair_spec(grad, rows),
            ],
            out_specs=[out_spec] * 3,
        ),
        out_shape=[out] * 3,
        compiler_params=pltpu.CompilerParams(vmem_limit_bytes=VMEM_BYTES),
        cost_estimate=attention_cost(heads, query_rows, rows, 4),
        name="attend_back",
    )(full, query[0], keys[0], values[0], probs, grad)


def to_slots(rows, exchange, core):
    received = other_core(core_piece(rows, 1 - core, 2))
    width = rows.shape[2] // 2
    left, right = rows[..., :width], rows[..., width:]
    first = jnp.where(jnp.logical_and(exchange, core == 1), received, left)
    second = jnp.where(jnp.logical_and(exchange, core == 0), received, right)
    return jnp.concatenate([first, second], axis=1)


def from_slots(slots, exchange, core):
    received = other_core(core_piece(slots, 1 - core, 1))
    height = slots.shape[1] // 2
    top, bottom = slots[:, :height], slots[:, height:]
    first = jnp.where(jnp.logical_and(exchange, core == 1), received, top)
    second = jnp.where(jnp.logical_and(exchange, core == 0), received, bottom)
    return jnp.concatenate([first, second], axis=2)


def clip_ids(lengths, row_count):
    ends = jnp.cumsum(lengths)
    places = jnp.arange(row_count, dtype=jnp.int32)
    return jnp.sum((places[:, None] >= ends[None, :]).astype(jnp.int32), axis=1)


def row_of(table, index):
    return lax.dynamic_index_in_dim(table, index, 0, keepdims=False)


def local(
    tokens,
    cotangent,
    clip_len,
    ln_params,
    w_self,
    w_self_out,
    w_offer,
    w_query,
    w_cross_out,
    w_up,
    w_down,
):
    index = lax.axis_index("clip")
    across = lax.axis_index("head")
    count = lax.axis_size("clip")
    quarter = count // 4
    view = jnp.where(index < 2 * quarter, 0, jnp.where(index < 3 * quarter, 1, 2))
    member = index % quarter
    core = index % 2
    own_micro2 = core == across
    is_big = view == 0
    is_mid = view == 1
    gains = ln_params[0]
    row_count = tokens.shape[1]
    half_rows = row_count // 2
    part_a = row_count

    def my_rows(array):
        first = row_of(array, across)
        kept = core_piece(array[2], core, 0)
        received = other_core(core_piece(array[2], 1 - core, 0))
        return jnp.concatenate([first, jnp.where(own_micro2, kept, received)], axis=0)

    def fetch(pieces):
        mine = over_head(pieces)
        return mine, other_core(mine)

    def assemble(mine, theirs, axis):
        return in_core_order(core, mine, theirs, axis)

    self_mine, self_theirs = fetch(core_piece(w_self[0], core, 1))
    bundle = [
        core_piece(w_self_out[0], core, 1),
        core_piece(w_query[0], core, 0),
        core_piece(w_offer[0, 0], core, 0),
        core_piece(w_offer[0, 1], core, 0),
        core_piece(w_cross_out[0], core, 1),
    ]
    mid_mine, mid_theirs = fetch(jnp.stack(bundle))
    up_mine, up_theirs = fetch(core_piece(w_up[0], core, 0))
    down_mine, down_theirs = fetch(core_piece(w_down[0], core, 0))

    full_self = jnp.concatenate([w_self[0], assemble(self_mine, self_theirs, 1)], axis=2)
    full_self_out = jnp.concatenate([w_self_out[0], assemble(mid_mine[0], mid_theirs[0], 1)], axis=0)
    full_query = jnp.concatenate([w_query[0], assemble(mid_mine[1], mid_theirs[1], 0)], axis=1)
    full_offer = jnp.concatenate([w_offer[0], assemble(mid_mine[2:4], mid_theirs[2:4], 1)], axis=2)
    full_cross_out = jnp.concatenate([w_cross_out[0], assemble(mid_mine[4], mid_theirs[4], 1)], axis=0)
    full_up = jnp.concatenate([w_up[0], assemble(up_mine, up_theirs, 0)], axis=1)
    full_down = jnp.concatenate([w_down[0], assemble(down_mine, down_theirs, 0)], axis=0)

    even_index = index - core + across
    even_member = even_index % quarter
    lens_a, lens_b = row_of(clip_len, across), clip_len[2]
    big_a = row_of(lens_a, jnp.minimum(index, 2 * quarter - 1))
    big_b = row_of(lens_b, jnp.minimum(even_index, 2 * quarter - 1))
    set_a = [clip_ids(row_of(lens_a, member + s * quarter), half_rows) for s in range(2)]
    set_b = clip_ids(row_of(lens_b, even_member + core * quarter), half_rows)
    keys_a = jnp.where(is_big, clip_ids(2 * big_a, row_count), jnp.concatenate(set_a))
    keys_b = jnp.where(is_big, clip_ids(2 * big_b, row_count), jnp.concatenate([set_b, set_b]))
    asks_a = jnp.where(is_big, jnp.concatenate([clip_ids(big_a, half_rows)] * 2), keys_a)
    asks_b = jnp.where(is_big, jnp.concatenate([clip_ids(big_b, half_rows)] * 2), keys_b)
    self_ids_a = (keys_a[:, None], keys_a[None, :])
    self_ids_b = (keys_b[:, None], keys_b[None, :])
    cross_ids_a = (asks_a[:, None], keys_a[None, :])
    cross_ids_b = (asks_b[:, None], keys_b[None, :])
    full_flag = is_big.astype(jnp.int32)[None]

    near = [(i, i - quarter) for i in range(2 * quarter, count)]
    far = [(i, i - 2 * quarter) for i in range(2 * quarter, 3 * quarter)]
    far += [(i, i - quarter) for i in range(3 * quarter, count)]

    def to_server(rows_a, slots_b):
        whole = jnp.concatenate([rows_a, slots_b], axis=1)
        second = lax.ppermute(whole[half_rows:], "clip", near)
        first = lax.ppermute(whole[:half_rows], "clip", far)
        second_plane = jnp.logical_and(is_big, index >= quarter)
        return jnp.concatenate([jnp.where(second_plane, second, first), second], axis=0)

    def to_reader(rows_a, slots_b):
        whole = jnp.concatenate([rows_a, slots_b], axis=1)
        top = whole[:half_rows]
        second = lax.ppermute(
            jnp.where(is_big, top, whole[half_rows:]), "clip", [(b, a) for a, b in near]
        )
        first = lax.ppermute(top, "clip", [(b, a) for a, b in far])
        both = jnp.concatenate([first, second], axis=0)
        width = rows_a.shape[1]
        return both[:, :width], both[:, width:]

    inputs = my_rows(tokens).astype(F32)
    grad_out_b = my_rows(cotangent)
    normal1, inverse1 = norm_stats(inputs)
    a1 = (normal1 * gains[0] + gains[1]).astype(BF16)
    qkv = jnp.einsum("rd,cde->cre", a1, full_self, preferred_element_type=F32).astype(BF16)
    qkv_b = to_slots(qkv[:, part_a:], is_big, core)
    self_a = [(qkv, 0), (qkv, 1), (qkv, 2)]
    self_b = [(qkv_b, 0), (qkv_b, 1), (qkv_b, 2)]
    heads = qkv.shape[2] // HEAD_DIM
    self_mix_a, self_p_a = attend(full_flag, *self_a, self_ids_a, row_count, heads)
    self_mix_b, self_p_b = attend(full_flag, *self_b, self_ids_b, row_count, heads // 2)
    self_mix = jnp.concatenate([self_mix_a, from_slots(self_mix_b[None], is_big, core)[0]], axis=0)
    hidden = inputs + dot_nn(self_mix, full_self_out)
    normal2, inverse2 = norm_stats(hidden)
    joined = (normal2 * gains[2] + gains[3]).astype(BF16)

    cross_q = dot_nn(joined, full_query).astype(BF16)
    cross_q_b = to_slots(cross_q[None, part_a:], is_mid, core)[0]
    asked = to_server(cross_q[:part_a], cross_q_b)
    offer_kv = jnp.einsum("rd,cde->cre", joined, full_offer, preferred_element_type=F32).astype(BF16)
    offer_b = to_slots(offer_kv[:, part_a:], is_big, core)
    wide = heads * HEAD_DIM
    asked_a, asked_b = asked[:, :wide], asked[:, wide:]
    cross_a = [(asked_a, None), (offer_kv, 0), (offer_kv, 1)]
    cross_b = [(asked_b, None), (offer_b, 0), (offer_b, 1)]
    served_a, cross_p_a = attend(full_flag, *cross_a, cross_ids_a, half_rows, heads)
    served_b, cross_p_b = attend(full_flag, *cross_b, cross_ids_b, half_rows, heads // 2)
    cross_mix_a, cross_mix_b = to_reader(served_a, served_b)
    cross_mix = jnp.concatenate([cross_mix_a, from_slots(cross_mix_b[None], is_mid, core)[0]], axis=0)
    second = hidden + dot_nn(cross_mix, full_cross_out)

    normal3, inverse3 = norm_stats(second)
    mlp_in = (normal3 * gains[4] + gains[5]).astype(BF16)
    mlp_pre = dot_nn(mlp_in, full_up)
    spread = lax.erf(mlp_pre * 0.7071067811865476) * 0.5 + 0.5
    density = jnp.exp(mlp_pre * mlp_pre * -0.5) * 0.3989422804014327
    activated = (mlp_pre * spread).astype(BF16)
    slope = spread + mlp_pre * density
    result = (second + dot_nn(activated, full_down)).astype(BF16)
    grad_up = (dot_nt(grad_out_b, full_down) * slope).astype(BF16)
    grad_mlp_in = dot_nt(grad_up, full_up)
    back3, gain3, shift3 = norm_back(grad_mlp_in, normal3, inverse3, gains[4])
    grad_second = grad_out_b.astype(F32) + back3
    grad_second_b = grad_second.astype(BF16)

    grad_cross_mix = dot_nt(grad_second_b, full_cross_out).astype(BF16)
    grad_cross_b = to_slots(grad_cross_mix[None, part_a:], is_mid, core)[0]
    grad_asked = to_server(grad_cross_mix[:part_a], grad_cross_b)
    g_down = dot_tn(activated, grad_out_b).astype(BF16)
    g_up = dot_tn(mlp_in, grad_up).astype(BF16)
    g_cross_out = dot_tn(cross_mix, grad_second_b).astype(BF16)
    dq_a, dk_a, dv_a = attend_back(
        full_flag, *cross_a, cross_p_a, grad_asked[:, :wide], half_rows, heads
    )
    dq_b, dk_b, dv_b = attend_back(
        full_flag, *cross_b, cross_p_b, grad_asked[:, wide:], half_rows, heads // 2
    )
    grad_q_a, grad_q_b = to_reader(dq_a, dq_b)
    grad_offer_b = from_slots(jnp.stack([dk_b, dv_b]), is_big, core)
    grad_offer = jnp.concatenate([jnp.stack([dk_a, dv_a]), grad_offer_b], axis=1)
    grad_q = jnp.concatenate([grad_q_a, from_slots(grad_q_b[None], is_mid, core)[0]], axis=0)
    g_offer = jnp.einsum("rd,cre->cde", joined, grad_offer, preferred_element_type=F32).astype(BF16)
    g_query = dot_tn(joined, grad_q).astype(BF16)
    grad_joined = dot_nt(grad_q, full_query) + jnp.einsum(
        "cre,cde->rd", grad_offer, full_offer, preferred_element_type=F32
    )
    back2, gain2, shift2 = norm_back(grad_joined, normal2, inverse2, gains[2])
    grad_hidden = grad_second + back2
    grad_hidden_b = grad_hidden.astype(BF16)

    grad_self_mix = dot_nt(grad_hidden_b, full_self_out).astype(BF16)
    g_self_out = dot_tn(self_mix, grad_hidden_b).astype(BF16)
    grad_mix_b = to_slots(grad_self_mix[None, part_a:], is_big, core)[0]
    dqkv_a = attend_back(
        full_flag, *self_a, self_p_a, grad_self_mix[:part_a], row_count, heads
    )
    dqkv_b = attend_back(full_flag, *self_b, self_p_b, grad_mix_b, row_count, heads // 2)
    grad_qkv_b = from_slots(jnp.stack(dqkv_b), is_big, core)
    grad_qkv = jnp.concatenate([jnp.stack(dqkv_a), grad_qkv_b], axis=1)
    g_self = jnp.einsum("rd,cre->cde", a1, grad_qkv, preferred_element_type=F32).astype(BF16)
    grad_a1 = jnp.einsum("cre,cde->rd", grad_qkv, full_self, preferred_element_type=F32)
    back1, gain1, shift1 = norm_back(grad_a1, normal1, inverse1, gains[0])
    grad_rows = (grad_hidden + back1).astype(BF16)

    def all_rows(mine):
        theirs = over_head(mine)
        a_mine, b_mine = mine[:part_a], mine[part_a:]
        a_theirs, b_theirs = theirs[:part_a], theirs[part_a:]
        kept = jnp.where(own_micro2, b_mine, b_theirs)
        received = other_core(jnp.where(own_micro2, b_theirs, b_mine))
        micro2 = in_core_order(core, kept, received, 0)
        micro0 = jnp.where(across == 0, a_mine, a_theirs)
        micro1 = jnp.where(across == 0, a_theirs, a_mine)
        return jnp.stack([micro0, micro1, micro2])

    levels = (2 * quarter).bit_length() - 1

    def view_sum(part):
        for bit in range(1, levels):
            members = 2 * quarter if bit == levels - 1 else None
            part = part + over_bit(part.astype(BF16), bit, members).astype(F32)
        return part

    def by_core(grad, axis):
        return core_piece(grad, core, axis).astype(F32) + other_core(
            core_piece(grad, 1 - core, axis)
        ).astype(F32)

    def reduce_pieces(mine, other):
        total = view_sum(mine + over_head(other.astype(BF16)).astype(F32))
        return total, other_core(total.astype(BF16)).astype(F32)

    width = w_query.shape[2]
    hidden_width = w_up.shape[2]
    down = by_core(g_down.reshape(2, hidden_width, -1), 1)
    down_sum = reduce_pieces(down[0], down[1])
    up = by_core(g_up, 0)
    up_sum = reduce_pieces(up[:, :hidden_width], up[:, hidden_width:])
    cross_out = by_core(g_cross_out, 1)
    query = by_core(g_query, 0)
    offer = by_core(g_offer, 1)
    cross_sum = reduce_pieces(
        jnp.concatenate([cross_out[None, :width], query[None, :, :width], offer[..., :width]]),
        jnp.concatenate([cross_out[None, width:], query[None, :, width:], offer[..., width:]]),
    )
    self_out = by_core(g_self_out, 1)
    self_in = by_core(g_self, 1)
    self_sum = reduce_pieces(
        jnp.concatenate([self_out[None, :width], self_in[..., :width]]),
        jnp.concatenate([self_out[None, width:], self_in[..., width:]]),
    )

    norms = jnp.stack([gain1, shift1, gain2, shift2, gain3, shift3])
    norms = norms + other_core(norms)
    for bit in range(1, levels):
        norms = norms + over_bit(norms, bit, 2 * quarter if bit == levels - 1 else None)
    norms = norms + over_head(norms)

    def whole(sums, axis, pick=slice(None)):
        return in_core_order(core, sums[0][pick], sums[1][pick], axis)

    return (
        all_rows(result),
        all_rows(grad_rows).astype(F32),
        norms[None],
        whole(self_sum, 1, slice(1, 4))[None],
        whole(self_sum, 1, 0)[None],
        whole(cross_sum, 1, slice(2, 4))[None],
        whole(cross_sum, 0, 1)[None],
        whole(cross_sum, 1, 0)[None],
        whole(up_sum, 0)[None],
        whole(down_sum, 0)[None],
    )


def solution(mesh):
    return jax.shard_map(
        local,
        mesh=mesh,
        in_specs=(
            P(None, "clip", None),
            P(None, "clip", None),
            P(),
            P("clip", None, None),
            P("clip", None, None, "head"),
            P("clip", "head", None),
            P("clip", None, None, "head"),
            P("clip", None, "head"),
            P("clip", "head", None),
            P("clip", None, "head"),
            P("clip", "head", None),
        ),
        out_specs=(
            P(None, "clip", None),
            P(None, "clip", None),
            P("clip", None, None),
            P("clip", None, None, "head"),
            P("clip", "head", None),
            P("clip", None, None, "head"),
            P("clip", None, "head"),
            P("clip", "head", None),
            P("clip", None, "head"),
            P("clip", "head", None),
        ),
        check_vma=False,
    )
```

time: 1620 us -> 694 us (0.43)
  waiting for transfers between devices: 999 us -> 251 us
  matrix products: 188 us -> 75.4 us
  other arithmetic: 177 us -> 82.8 us
  Pallas kernels: 0 us -> 63.3 us
  local copies, waits for them, and re-layouts: 120 us -> 91.6 us
  starting transfers between devices: 96 us -> 118 us
    psum x10 -> x0, waiting for transfers between devices: 655 us -> none  [head_total(): return lax.psum(partial_sum, 'head')]
    dot_general x63 -> x21, matrix products: 188 us -> 75.4 us  [the longest x5 23.2 us: dot_nt(): lax.dot_general(left, right, (((1,), (1,)), ((), ())), preferred_element_...]
    ppermute x36 -> x59, waiting for transfers between devices: 343 us -> 251 us  [the longest x11 119 us: over_head(): return lax.ppermute(value, 'head', [(0, 1), (1, 0)])]
    pallas_call x0 -> x8, Pallas kernels: none -> 63.3 us  [the longest x4 34.1 us: attend_back(): pl.pallas_call(lambda *refs: attend_back_kernel(query_rows, *refs), grid_...]
    reduce_sum x26 -> x6, other arithmetic: 50.6 us -> 7.49 us  [the longest x2 6.33 us: norm_back(): return (grad_rows, jnp.sum(grad * normal, axis=0), jnp.sum(grad, axis=0))]
    another operation x43 -> x8, local copies, waits for them, and re-layouts: 38.8 us -> 5.64 us  [the longest x7 4.89 us: local(): norms = jnp.stack([gain1, shift1, gain2, shift2, gain3, shift3])]
    convert_element_type x27 -> x17, other arithmetic: 53.5 us -> 28.4 us  [the longest x8 13.9 us: view_sum(): part = part + over_bit(part.astype(BF16), bit, members).astype(F32)]
    dynamic_slice x0 -> x31, local copies, waits for them, and re-layouts: none -> 24.9 us  [the longest x25 18 us: core_piece(): return lax.dynamic_slice_in_dim(value, piece * size, size, axis)]
  transfers between devices with their start and end apart: 46 -> 59, of which waited for: 28 -> 15; matrix products, arithmetic and copies ran while one was open for 16% -> 23% of each run, Pallas kernels for 0% -> 9%
where the time goes in v1:
time: 694 us; the launch traced here: 686 us
  waiting for transfers between devices  251 us (36%)
  starting transfers between devices  118 us (17%)
  local copies, waits for them, and re-layouts  91.6 us (13%)
  other arithmetic  82.8 us (12%)
  matrix products  75.4 us (11%)
  Pallas kernels  63.3 us (9%)
    ppermute x11, waiting for transfers between devices, over_head(): return lax.ppermute(value, 'head', [(0, 1), (1, 0)])  119 us
    ppermute x40, waiting for transfers between devices, over_bit(): lax.ppermute(value, 'clip', [(i, i ^ 1 << bit) for i in range(count)])  76.7 us
    ppermute x40, starting transfers between devices, over_bit(): lax.ppermute(value, 'clip', [(i, i ^ 1 << bit) for i in range(count)])  63.9 us
    ppermute x2, waiting for transfers between devices, to_server(): first = lax.ppermute(whole[:half_rows], 'clip', far)  40.7 us
    unnamed x322, local copies, waits for them, and re-layouts  39.7 us
    ppermute x2, starting transfers between devices, to_reader(): first = lax.ppermute(top, 'clip', [(b, a) for a, b in far])  37.4 us
    pallas_call x4, Pallas kernels, attend_back(): pl.pallas_call(lambda *refs: attend_back_kernel(query_rows, *refs), grid_...  34.1 us
    pallas_call x4, Pallas kernels, attend(): pl.pallas_call(lambda *refs: attend_kernel(query_rows, *refs), grid_spec=...  29.1 us
  transfers between devices with their start and end apart: 59, of which 15 were waited for; matrix products, arithmetic and copies ran while one was open for 23% of the time, Pallas kernels for 9%

profile of v1, /device:TPU:0, one launch (start us, length us, event | category | flops | bytes accessed | tf_op | source)
XLA Modules:
  0.0 685.6 jit_solution(2258388721030201078)
XLA Ops:
  0.7 2.3 dynamic-slice_bitcast_fusion.4
  3.0 2.9 collective-permute-start.1
  5.9 2.5 dynamic-slice_bitcast_fusion.2
  9.5 2.0 collective-permute-start.14
  19.7 2.4 constant_dynamic-slice_fusion.8
  29.4 2.0 collective-permute-done.2
  32.9 3.3 convert_bitcast_fusion.refs_1_.refs_2_.refs_3_
  40.6 2.3 copy.113
  45.9 62.2 %collective-permute-done.5 = bf16[5,384,384]{2,1,0:T(8,128)(2,1)} collective-permute-done((bf16[5,384,384]{2,1,0:T(8,128)(2,1)}, bf16[5,384,384]{2,1,0:T(8,128)(2,1)}, u32[]{:S(2)}, u32[]{:S(2)}) %collective-permute-start.5) | collective-permute-done | bytes 1474592 | tf_op jit(solution)/shard_map/ppermute | solution.py:19
  110.0 6.3 attend.5
  118.6 12.0 %attend.4 = (bf16[512,768]{1,0:T(8,128)(2,1)S(1)}, bf16[12,512,512]{2,1,0:T(8,128)(2,1)S(1)}) custom-call(s32[1]{0:T(128)} %bitcast.3.refs_0_, bf16[3,768,768]{2,1,0:T(8,128)(2,1)S(1)} %convert_bitcast_fusion.refs_1_.refs_2_.refs_3_, bf16[3,768,768]{2,1,0:T(8,128)(2,1)S(1)} %convert_bitcast_fusion.refs_1_.refs_2_.refs_3_, ...), custom_call_target="tpu_custom_call" | custom-call | flops 3221225472 | bytes 9437184 | tf_op jit(solution)/shard_map/attend/pallas_call | solution.py:185
  130.6 2.6 copy-done.20
  141.5 2.1 convert_bitcast_fusion.1.refs_2_.refs_3_
  149.0 15.4 %collective-permute-done.9 = bf16[256,1152]{1,0:T(8,128)(2,1)S(1)} collective-permute-done((bf16[256,1152]{1,0:T(8,128)(2,1)S(1)}, bf16[256,1152]{1,0:T(8,128)(2,1)S(1)}, u32[]{:S(2)}, u32[]{:S(2)}) %collective-permute-start.9) | collective-permute-done | bytes 589856 | tf_op jit(solution)/shard_map/ppermute | solution.py:348
  164.6 3.9 attend.7
  169.8 6.9 %attend.6 = (bf16[512,768]{1,0:T(8,128)(2,1)S(1)}, bf16[12,256,512]{2,1,0:T(8,128)(2,1)S(1)}) custom-call(s32[1]{0:T(128)} %bitcast.3.refs_0_, bf16[512,768]{1,0:T(8,128)(2,1)S(1)} %fusion.29.refs_1_, bf16[2,768,768]{2,1,0:T(8,128)(2,1)S(1)} %convert_bitcast_fusion.1.refs_2_.refs_3_, bf16[2,768,768]{2,1,0:T(8,128)(2,1)S(1)} %convert_bitcast_fusion.1.refs_2_.refs_3_, ...), custom_call_target="tpu_custom_call" | custom-call | flops 1610612736 | bytes 6291456 | tf_op jit(solution)/shard_map/attend/pallas_call | solution.py:185
  179.1 15.6 %collective-permute-start.11 = (bf16[256,1152]{1,0:T(8,128)(2,1)S(1)}, bf16[256,1152]{1,0:T(8,128)(2,1)S(1)}, u32[]{:S(2)}, u32[]{:S(2)}) collective-permute-start(bf16[256,1152]{1,0:T(8,128)(2,1)S(1)} %get-tuple-element.184), channel_id=1, source_target_pairs={{0,16},{2,18},{4,20},{6,22},{16,24},{18,26},{20,28},{22,30},{1,17}... | collective-permute-start | bytes 1769480 | tf_op jit(solution)/shard_map/ppermute | solution.py:358
  196.3 10.4 %collective-permute-done.11 = bf16[256,1152]{1,0:T(8,128)(2,1)S(1)} collective-permute-done((bf16[256,1152]{1,0:T(8,128)(2,1)S(1)}, bf16[256,1152]{1,0:T(8,128)(2,1)S(1)}, u32[]{:S(2)}, u32[]{:S(2)}) %collective-permute-start.11) | collective-permute-done | bytes 589856 | tf_op jit(solution)/shard_map/ppermute | solution.py:358
  211.5 2.2 copy-done.85
  213.7 8.8 %multiply_convert_fusion.1 = (bf16[768,3072]{1,0:T(8,128)(2,1)S(1)}, f32[768,3072]{1,0:T(8,128)}) fusion(bf16[384,1536]{1,0:T(8,128)(2,1)S(1)} %get-tuple-element.162, bf16[384,1536]{1,0:T(8,128)(2,1)S(1)} %get-tuple-element.161, bf16[768,1536]{1,0:T(8,128)(2,1)S(1)} %bitcast.252, f32[768,768]{0,1:T(8,128)S(1)} %get-tuple-element.210, ...), kind=kOutput, calls=%fused_computation.1 | convolution fusion | flops 3652780032 | bytes 21245952 | tf_op jit(solution)/shard_map/dot_general | solution.py:84
  222.5 5.8 convolution_convert_fusion
  228.3 7.5 %add_convert_fusion = bf16[768,768]{0,1:T(8,128)(2,1)} fusion(f32[768,768]{0,1:T(8,128)S(1)} %get-tuple-element.210, bf16[768,3072]{1,0:T(8,128)(2,1)} %copy-done.143, bf16[768,768]{1,0:T(8,128)(2,1)S(1)} %get-tuple-element.160, bf16[768,768]{1,0:T(8,128)(2,1)S(1)} %get-tuple-element.159, bf16[1536,768]{1,0:T(8,128)(2,1)S(1)} %bitcast.250), kind=kOutput, calls=%fused_computation.67 | convolution fusion | flops 3639214080 | bytes 12976128 | tf_op jit(solution)/shard_map/dot_general | solution.py:84
  235.8 13.3 %multiply_convert_fusion = bf16[768,3072]{1,0:T(8,128)(2,1)S(1)} fusion(f32[768,3072]{1,0:T(8,128)} %get-tuple-element.212, bf16[768,768]{1,0:T(8,128)(2,1)S(1)} %get-tuple-element.160, bf16[768,768]{1,0:T(8,128)(2,1)S(1)} %get-tuple-element.159, bf16[1536,768]{1,0:T(8,128)(2,1)S(1)} %bitcast.251, bf16[256,768]{0,1:T(8,128)(2,1)S(1)} %bitcast_select_fusion, ...), kind=kOutput, calls=%fused_computation | convolution fusion | flops 3663986688 | bytes 20054016 | tf_op jit(solution)/shard_map/dot_general | solution.py:76
  249.1 5.9 fusion.81
  254.9 5.8 convolution_convert_fusion.1
  260.7 3.0 copy.116
  263.7 3.3 multiply_reduce_fusion
  267.5 2.1 multiply_add_fusion.2
  285.1 25.3 %collective-permute-done.23 = bf16[256,1152]{1,0:T(8,128)(2,1)S(1)} collective-permute-done((bf16[256,1152]{1,0:T(8,128)(2,1)S(1)}, bf16[256,1152]{1,0:T(8,128)(2,1)S(1)}, u32[]{:S(2)}, u32[]{:S(2)}) %collective-permute-start.23) | collective-permute-done | bytes 589856 | tf_op jit(solution)/shard_map/ppermute | solution.py:348
  310.6 4.5 attend_back.5
  317.0 8.1 %attend_back.4 = (bf16[512,768]{1,0:T(8,128)(2,1)S(1)}, bf16[512,768]{1,0:T(8,128)(2,1)S(1)}, bf16[512,768]{1,0:T(8,128)(2,1)S(1)}) custom-call(s32[1]{0:T(128)} %bitcast.3.refs_0_, bf16[512,768]{1,0:T(8,128)(2,1)S(1)} %copy-done.7, bf16[2,768,768]{2,1,0:T(8,128)(2,1)S(1)} %copy-done.3, bf16[2,768,768]{2,1,0:T(8,128)(2,1)S(1)} %copy-done.3, ...), custom_call_target="tpu_custom_call" | custom-call | flops 3221225472 | bytes 6291456 | tf_op jit(solution)/shard_map/attend_back/pallas_call | solution.py:216
  326.2 21.8 %collective-permute-start.24 = (bf16[256,1152]{1,0:T(8,128)(2,1)S(1)}, bf16[256,1152]{1,0:T(8,128)(2,1)S(1)}, u32[]{:S(2)}, u32[]{:S(2)}) collective-permute-start(bf16[256,1152]{1,0:T(8,128)(2,1)S(1)} %get-tuple-element.174), channel_id=1, source_target_pairs={{0,16},{2,18},{4,20},{6,22},{16,24},{18,26},{20,28},{22,30},{1,17}... | collective-permute-start | bytes 1769480 | tf_op jit(solution)/shard_map/ppermute | solution.py:358
  353.7 2.0 fusion.27
  355.8 4.3 collective-permute-done.24
  361.1 2.1 collective-permute-done.26
  376.2 14.4 %attend_back.6 = (bf16[512,768]{1,0:T(8,128)(2,1)S(1)}, bf16[512,768]{1,0:T(8,128)(2,1)S(1)}, bf16[512,768]{1,0:T(8,128)(2,1)S(1)}) custom-call(s32[1]{0:T(128)} %bitcast.3.refs_0_, bf16[3,768,768]{2,1,0:T(8,128)(2,1)S(1)} %convert_bitcast_fusion.refs_1_.refs_2_.refs_3_, bf16[3,768,768]{2,1,0:T(8,128)(2,1)S(1)} %convert_bitcast_fusion.refs_1_.refs_2_.refs_3_, ...), custom_call_target="tpu_custom_call" | custom-call | flops 6442450944 | bytes 9437184 | tf_op jit(solution)/shard_map/attend_back/pallas_call | solution.py:216
  392.2 2.4 copy.125
  398.1 7.1 %attend_back.7 = (bf16[512,384]{1,0:T(8,128)(2,1)S(1)}, bf16[512,384]{1,0:T(8,128)(2,1)S(1)}, bf16[512,384]{1,0:T(8,128)(2,1)S(1)}) custom-call(s32[1]{0:T(128)} %bitcast.3.refs_0_, bf16[3,512,384]{2,1,0:T(8,128)(2,1)S(1)} %copy-done.1, bf16[3,512,384]{2,1,0:T(8,128)(2,1)S(1)} %copy-done.1, bf16[3,512,384]{2,1,0:T(8,128)(2,1)S(1)} %copy-done.1, ...), custom_call_target="tpu_custom_call" | custom-call | flops 3221225472 | bytes 4718592 | tf_op jit(solution)/shard_map/attend_back/pallas_call | solution.py:216
  416.5 4.9 fusion.80
  421.5 3.3 copy.119
  424.9 3.1 fusion.13
  431.3 3.1 fusion.12
  434.7 3.4 convert_add_fusion.1
  438.1 3.1 convolution_convert_fusion.2
  445.0 2.3 convert_add_fusion
  447.3 11.7 %collective-permute-start.34 = (f32[6,768]{1,0:T(8,128)S(1)}, f32[6,768]{1,0:T(8,128)S(1)}, u32[]{:S(2)}, u32[]{:S(2)}) collective-permute-start(f32[6,768]{1,0:T(8,128)S(1)} %add.290), channel_id=1, source_target_pairs={{0,8},{2,10},{4,12},{6,14},{8,0},{10,2},{12,4},{14,6},{1,9},{3,11}... | collective-permute-start | bytes 55304 | tf_op jit(solution)/shard_map/ppermute | solution.py:24
  461.6 56.4 %collective-permute-done.35 = f32[6,768]{1,0:T(8,128)S(1)} collective-permute-done((f32[6,768]{1,0:T(8,128)S(1)}, f32[6,768]{1,0:T(8,128)S(1)}, u32[]{:S(2)}, u32[]{:S(2)}) %collective-permute-start.35) | collective-permute-done | bytes 18464 | tf_op jit(solution)/shard_map/ppermute | solution.py:19
  530.2 18.9 %collective-permute-done.46 = bf16[4,384,384]{2,1,0:T(8,128)(2,1)S(1)} collective-permute-done((bf16[4,384,384]{2,1,0:T(8,128)(2,1)S(1)}, bf16[4,384,384]{2,1,0:T(8,128)(2,1)S(1)}, u32[]{:S(2)}, u32[]{:S(2)}) %collective-permute-start.46) | collective-permute-done | bytes 1179680 | tf_op jit(solution)/shard_map/ppermute | solution.py:24
  549.1 3.2 fusion.20
  552.3 11.7 %collective-permute-start.47 = (bf16[4,384,384]{2,1,0:T(8,128)(2,1)}, bf16[4,384,384]{2,1,0:T(8,128)(2,1)}, u32[]{:S(2)}, u32[]{:S(2)}) collective-permute-start(bf16[4,384,384]{2,1,0:T(8,128)(2,1)} %fusion.20), channel_id=1, source_target_pairs={{0,8},{2,10},{4,12},{6,14},{8,0},{10,2},{12,4},{14,6},{1,9},{3,11}... | collective-permute-start | bytes 3538952 | tf_op jit(solution)/shard_map/ppermute | solution.py:24
  564.0 10.4 %collective-permute-done.51 = bf16[384,1536]{1,0:T(8,128)(2,1)S(1)} collective-permute-done((bf16[384,1536]{1,0:T(8,128)(2,1)S(1)}, bf16[384,1536]{1,0:T(8,128)(2,1)S(1)}, u32[]{:S(2)}, u32[]{:S(2)}) %collective-permute-start.51) | collective-permute-done | bytes 1179680 | tf_op jit(solution)/shard_map/ppermute | solution.py:24
  576.0 11.7 %collective-permute-start.52 = (bf16[384,1536]{1,0:T(8,128)(2,1)}, bf16[384,1536]{1,0:T(8,128)(2,1)}, u32[]{:S(2)}, u32[]{:S(2)}) collective-permute-start(bf16[384,1536]{1,0:T(8,128)(2,1)} %fusion.21), channel_id=1, source_target_pairs={{0,8},{2,10},{4,12},{6,14},{8,0},{10,2},{12,4},{14,6},{1,9},{3,11}... | collective-permute-start | bytes 3538952 | tf_op jit(solution)/shard_map/ppermute | solution.py:24
  587.7 2.6 maximum_convert_fusion
  590.2 6.0 copy.126
  599.4 2.4 fusion.22
  601.8 12.1 %collective-permute-start.57 = (bf16[768,768]{1,0:T(8,128)(2,1)S(1)}, bf16[768,768]{1,0:T(8,128)(2,1)S(1)}, u32[]{:S(2)}, u32[]{:S(2)}) collective-permute-start(bf16[768,768]{1,0:T(8,128)(2,1)S(1)} %fusion.22), channel_id=1, source_target_pairs={{0,8},{2,10},{4,12},{6,14},{8,0},{10,2},{12,4},{14,6},{1,9},{3,11}... | collective-permute-start | bytes 3538952 | tf_op jit(solution)/shard_map/ppermute | solution.py:24
  617.3 2.2 fusion.75
  619.7 2.1 fusion.74
  622.2 18.1 %collective-permute-done.57 = bf16[768,768]{1,0:T(8,128)(2,1)S(1)} collective-permute-done((bf16[768,768]{1,0:T(8,128)(2,1)S(1)}, bf16[768,768]{1,0:T(8,128)(2,1)S(1)}, u32[]{:S(2)}, u32[]{:S(2)}) %collective-permute-start.57) | collective-permute-done | bytes 1179680 | tf_op jit(solution)/shard_map/ppermute | solution.py:24
  644.8 2.8 collective-permute-start.40
  652.5 21.7 %collective-permute-done.40 = bf16[4,384,384]{2,1,0:T(8,128)(2,1)S(1)} collective-permute-done((bf16[4,384,384]{2,1,0:T(8,128)(2,1)S(1)}, bf16[4,384,384]{2,1,0:T(8,128)(2,1)S(1)}, u32[]{:S(2)}, u32[]{:S(2)}) %collective-permute-start.40) | collective-permute-done | bytes 1179680 | tf_op jit(solution)/shard_map/ppermute | solution.py:24
  676.2 2.5 maximum_bitcast_fusion
  679.1 2.5 maximum_bitcast_fusion.1
  682.1 2.0 maximum_bitcast_fusion.2
  (623 shorter events, 150.5 us)
Async XLA Ops:
  3.0 25.7 %collective-permute-start.1 = (bf16[3,384,384]{2,1,0:T(8,128)(2,1)}, bf16[3,384,384]{2,1,0:T(8,128)(2,1)}, u32[]{:S(2)}, u32[]{:S(2)}) collective-permute-start(bf16[3,384,384]{2,1,0:T(8,128)(2,1)} %dynamic-slice_bitcast_fusion.4), channel_id=1, source_target_pairs={{0,1},{1,0},{2,3},{3,2},{4,5},{5,4},{6,7},{7,6},{8,9},{9,8},{10,11... | collective-permute-start | bytes 2654216 | tf_op jit(solution)/shard_map/ppermute | solution.py:19
  8.4 139.1 %collective-permute-start.16 = (bf16[768,768]{1,0:T(8,128)(2,1)}, bf16[768,768]{1,0:T(8,128)(2,1)}, u32[]{:S(2)}, u32[]{:S(2)}) collective-permute-start(bf16[768,768]{1,0:T(8,128)(2,1)} %dynamic-slice_bitcast_fusion.2), channel_id=1, source_target_pairs={{0,1},{1,0},{2,3},{3,2},{4,5},{5,4},{6,7},{7,6},{8,9},{9,8},{10,11... | collective-permute-start | bytes 3538952 | tf_op jit(solution)/shard_map/ppermute | solution.py:19
  9.5 139.2 %collective-permute-start.14 = (bf16[384,1536]{1,0:T(8,128)(2,1)}, bf16[384,1536]{1,0:T(8,128)(2,1)}, u32[]{:S(2)}, u32[]{:S(2)}) collective-permute-start(bf16[384,1536]{1,0:T(8,128)(2,1)} %dynamic-slice_bitcast_fusion.3), channel_id=1, source_target_pairs={{0,1},{1,0},{2,3},{3,2},{4,5},{5,4},{6,7},{7,6},{8,9},{9,8},{10,11... | collective-permute-start | bytes 3538952 | tf_op jit(solution)/shard_map/ppermute | solution.py:19
  15.4 92.7 %collective-permute-start.5 = (bf16[5,384,384]{2,1,0:T(8,128)(2,1)}, bf16[5,384,384]{2,1,0:T(8,128)(2,1)}, u32[]{:S(2)}, u32[]{:S(2)}) collective-permute-start(bf16[5,384,384]{2,1,0:T(8,128)(2,1)} %dynamic-slice_dynamic-update-slice_fusion), channel_id=1, source_target_pairs={{0,1},{1,0},{2,3},{3,2},{4,5},{5,4},{6,7},{7,6},{8,9},{9,8},{10,11... | collective-permute-start | bytes 4423688 | tf_op jit(solution)/shard_map/ppermute | solution.py:19
  17.2 11.1 %collective-permute-start = (bf16[256,768]{0,1:T(8,128)(2,1)S(1)}, bf16[256,768]{0,1:T(8,128)(2,1)}, u32[]{:S(2)}, u32[]{:S(2)}) collective-permute-start(bf16[256,768]{0,1:T(8,128)(2,1)S(1)} %bitcast.256), channel_id=1, source_target_pairs={{0,2},{2,0},{4,6},{6,4},{8,10},{10,8},{12,14},{14,12},{16,18},{18,... | collective-permute-start | bytes 1179656 | tf_op jit(solution)/shard_map/ppermute | solution.py:24
  28.2 118.5 %collective-permute-start.20 = (bf16[256,768]{0,1:T(8,128)(2,1)}, bf16[256,768]{0,1:T(8,128)(2,1)}, u32[]{:S(2)}, u32[]{:S(2)}) collective-permute-start(bf16[256,768]{0,1:T(8,128)(2,1)} %bitcast.59), channel_id=1, source_target_pairs={{0,2},{2,0},{4,6},{6,4},{8,10},{10,8},{12,14},{14,12},{16,18},{18,... | collective-permute-start | bytes 1179656 | tf_op jit(solution)/shard_map/ppermute | solution.py:24
  28.7 2.8 collective-permute-start.2
  37.2 71.5 %collective-permute-start.3 = (bf16[3,256,384]{2,1,0:T(8,128)(2,1)}, bf16[3,256,384]{2,1,0:T(8,128)(2,1)}, u32[]{:S(2)}, u32[]{:S(2)}) collective-permute-start(bf16[3,256,384]{2,1,0:T(8,128)(2,1)} %constant_dynamic-slice_fusion.12), channel_id=1, source_target_pairs={{0,2},{2,0},{4,6},{6,4},{8,10},{10,8},{12,14},{14,12},{16,18},{18,... | collective-permute-start | bytes 1769480 | tf_op jit(solution)/shard_map/ppermute | solution.py:24
  108.1 25.3 %collective-permute-start.6 = (bf16[5,384,384]{2,1,0:T(8,128)(2,1)}, bf16[5,384,384]{2,1,0:T(8,128)(2,1)S(1)}, u32[]{:S(2)}, u32[]{:S(2)}) collective-permute-start(bf16[5,384,384]{2,1,0:T(8,128)(2,1)} %collective-permute-done.5), channel_id=1, source_target_pairs={{0,2},{2,0},{4,6},{6,4},{8,10},{10,8},{12,14},{14,12},{16,18},{18,... | collective-permute-start | bytes 4423688 | tf_op jit(solution)/shard_map/ppermute | solution.py:24
  118.0 15.2 %collective-permute-start.4 = (bf16[1,256,384]{2,1,0:T(8,128)(2,1)S(1)}, bf16[1,256,384]{2,1,0:T(8,128)(2,1)S(1)}, u32[]{:S(2)}, u32[]{:S(2)}) collective-permute-start(bf16[1,256,384]{2,1,0:T(8,128)(2,1)S(1)} %dynamic-slice_bitcast_fusion.10), channel_id=1, source_target_pairs={{0,2},{2,0},{4,6},{6,4},{8,10},{10,8},{12,14},{14,12},{16,18},{18,... | collective-permute-start | bytes 589832 | tf_op jit(solution)/shard_map/ppermute | solution.py:24
  135.2 73.6 %copy-start.105 = (bf16[384,384]{1,0:T(8,128)(2,1)}, bf16[384,384]{1,0:T(8,128)(2,1)S(1)}, u32[]{:S(2)}) copy-start(bf16[384,384]{1,0:T(8,128)(2,1)S(1)} %get-tuple-element.139) | copy-start | bytes 884740
  135.2 73.6 %copy-start.107 = (bf16[384,384]{1,0:T(8,128)(2,1)}, bf16[384,384]{1,0:T(8,128)(2,1)S(1)}, u32[]{:S(2)}) copy-start(bf16[384,384]{1,0:T(8,128)(2,1)S(1)} %get-tuple-element.143) | copy-start | bytes 884740
  139.7 4.3 collective-permute-start.7
  143.8 5.0 collective-permute-start.10
  145.4 19.0 %collective-permute-start.9 = (bf16[256,1152]{1,0:T(8,128)(2,1)S(1)}, bf16[256,1152]{1,0:T(8,128)(2,1)S(1)}, u32[]{:S(2)}, u32[]{:S(2)}) collective-permute-start(bf16[256,1152]{1,0:T(8,128)(2,1)S(1)} %get-tuple-element.185), channel_id=1, source_target_pairs={{16,0},{18,2},{20,4},{22,6},{24,16},{26,18},{28,20},{30,22},{17,1}... | collective-permute-start | bytes 1769480 | tf_op jit(solution)/shard_map/ppermute | solution.py:348
  146.7 17.7 %collective-permute-start.8 = (bf16[256,1152]{1,0:T(8,128)(2,1)S(1)}, bf16[256,1152]{1,0:T(8,128)(2,1)S(1)}, u32[]{:S(2)}, u32[]{:S(2)}) collective-permute-start(bf16[256,1152]{1,0:T(8,128)(2,1)S(1)} %get-tuple-element.186), channel_id=1, source_target_pairs={{16,8},{18,10},{20,12},{22,14},{24,16},{26,18},{28,20},{30,22},{17... | collective-permute-start | bytes 1769480 | tf_op jit(solution)/shard_map/ppermute | solution.py:347
  147.5 88.2 %copy-start.60 = (bf16[256,768]{0,1:T(8,128)(2,1)}, bf16[256,768]{0,1:T(8,128)(2,1)S(1)}, u32[]{:S(2)}) copy-start(bf16[256,768]{0,1:T(8,128)(2,1)S(1)} %bitcast_select_fusion) | copy-start | bytes 1179652
  147.5 59.5 %collective-permute-start.17 = (bf16[768,768]{1,0:T(8,128)(2,1)}, bf16[768,768]{1,0:T(8,128)(2,1)S(1)}, u32[]{:S(2)}, u32[]{:S(2)}) collective-permute-start(bf16[768,768]{1,0:T(8,128)(2,1)} %collective-permute-done.16), channel_id=1, source_target_pairs={{0,2},{2,0},{4,6},{6,4},{8,10},{10,8},{12,14},{14,12},{16,18},{18,... | collective-permute-start | bytes 3538952 | tf_op jit(solution)/shard_map/ppermute | solution.py:24
  148.7 46.0 %collective-permute-start.15 = (bf16[384,1536]{1,0:T(8,128)(2,1)}, bf16[384,1536]{1,0:T(8,128)(2,1)S(1)}, u32[]{:S(2)}, u32[]{:S(2)}) collective-permute-start(bf16[384,1536]{1,0:T(8,128)(2,1)} %collective-permute-done.14), channel_id=1, source_target_pairs={{0,2},{2,0},{4,6},{6,4},{8,10},{10,8},{12,14},{14,12},{16,18},{18,... | collective-permute-start | bytes 3538952 | tf_op jit(solution)/shard_map/ppermute | solution.py:24
  178.4 28.4 %collective-permute-start.12 = (bf16[256,1152]{1,0:T(8,128)(2,1)S(1)}, bf16[256,1152]{1,0:T(8,128)(2,1)S(1)}, u32[]{:S(2)}, u32[]{:S(2)}) collective-permute-start(bf16[256,1152]{1,0:T(8,128)(2,1)S(1)} %get-tuple-element.183), channel_id=1, source_target_pairs={{8,16},{10,18},{12,20},{14,22},{16,24},{18,26},{20,28},{22,30},{9,... | collective-permute-start | bytes 1769480 | tf_op jit(solution)/shard_map/ppermute | solution.py:355
  179.1 27.6 %collective-permute-start.11 = (bf16[256,1152]{1,0:T(8,128)(2,1)S(1)}, bf16[256,1152]{1,0:T(8,128)(2,1)S(1)}, u32[]{:S(2)}, u32[]{:S(2)}) collective-permute-start(bf16[256,1152]{1,0:T(8,128)(2,1)S(1)} %get-tuple-element.184), channel_id=1, source_target_pairs={{0,16},{2,18},{4,20},{6,22},{16,24},{18,26},{20,28},{22,30},{1,17}... | collective-permute-start | bytes 1769480 | tf_op jit(solution)/shard_map/ppermute | solution.py:358
  206.9 1.8 collective-permute-start.13
  274.3 51.9 %collective-permute-start.18 = (bf16[768,768]{0,1:T(8,128)(2,1)S(1)}, bf16[768,768]{0,1:T(8,128)(2,1)S(1)}, u32[]{:S(2)}, u32[]{:S(2)}) collective-permute-start(bf16[768,768]{0,1:T(8,128)(2,1)S(1)} %copy-done.59), channel_id=1, source_target_pairs={{0,1},{1,0},{2,3},{3,2},{4,5},{5,4},{6,7},{7,6},{8,9},{9,8},{10,11... | collective-permute-start | bytes 3538952 | tf_op jit(solution)/shard_map/ppermute | solution.py:19
  276.7 6.0 collective-permute-start.42
  277.0 4.1 collective-permute-start.21
  279.0 155.7 %collective-permute-start.49 = (bf16[384,3072]{1,0:T(8,128)(2,1)}, bf16[384,3072]{1,0:T(8,128)(2,1)}, u32[]{:S(2)}, u32[]{:S(2)}) collective-permute-start(bf16[384,3072]{1,0:T(8,128)(2,1)} %constant_dynamic-slice_fusion.1), channel_id=1, source_target_pairs={{0,2},{2,0},{4,6},{6,4},{8,10},{10,8},{12,14},{14,12},{16,18},{18,... | collective-permute-start | bytes 7077896 | tf_op jit(solution)/shard_map/ppermute | solution.py:24
  280.8 164.1 %collective-permute-start.54 = (bf16[2,768,768]{2,1,0:T(8,128)(2,1)}, bf16[2,768,768]{2,1,0:T(8,128)(2,1)}, u32[]{:S(2)}, u32[]{:S(2)}) collective-permute-start(bf16[2,768,768]{2,1,0:T(8,128)(2,1)} %constant_dynamic-slice_fusion), channel_id=1, source_target_pairs={{0,2},{2,0},{4,6},{6,4},{8,10},{10,8},{12,14},{14,12},{16,18},{18,... | collective-permute-start | bytes 7077896 | tf_op jit(solution)/shard_map/ppermute | solution.py:24
  281.3 29.1 %collective-permute-start.23 = (bf16[256,1152]{1,0:T(8,128)(2,1)S(1)}, bf16[256,1152]{1,0:T(8,128)(2,1)S(1)}, u32[]{:S(2)}, u32[]{:S(2)}) collective-permute-start(bf16[256,1152]{1,0:T(8,128)(2,1)S(1)} %get-tuple-element.177), channel_id=1, source_target_pairs={{16,0},{18,2},{20,4},{22,6},{24,16},{26,18},{28,20},{30,22},{17,1}... | collective-permute-start | bytes 1769480 | tf_op jit(solution)/shard_map/ppermute | solution.py:348
  282.7 27.8 %collective-permute-start.22 = (bf16[256,1152]{1,0:T(8,128)(2,1)S(1)}, bf16[256,1152]{1,0:T(8,128)(2,1)S(1)}, u32[]{:S(2)}, u32[]{:S(2)}) collective-permute-start(bf16[256,1152]{1,0:T(8,128)(2,1)S(1)} %get-tuple-element.178), channel_id=1, source_target_pairs={{16,8},{18,10},{20,12},{22,14},{24,16},{26,18},{28,20},{30,22},{17... | collective-permute-start | bytes 1769480 | tf_op jit(solution)/shard_map/ppermute | solution.py:347
  315.2 32.8 %collective-permute-start.27 = (bf16[2,256,384]{2,1,0:T(8,128)(2,1)S(1)}, bf16[2,256,384]{2,1,0:T(8,128)(2,1)S(1)}, u32[]{:S(2)}, u32[]{:S(2)}) collective-permute-start(bf16[2,256,384]{2,1,0:T(8,128)(2,1)S(1)} %fusion.40), channel_id=1, source_target_pairs={{0,2},{2,0},{4,6},{6,4},{8,10},{10,8},{12,14},{14,12},{16,18},{18,... | collective-permute-start | bytes 1179656 | tf_op jit(solution)/shard_map/ppermute | solution.py:24
  325.4 34.8 %collective-permute-start.25 = (bf16[256,1152]{1,0:T(8,128)(2,1)S(1)}, bf16[256,1152]{1,0:T(8,128)(2,1)S(1)}, u32[]{:S(2)}, u32[]{:S(2)}) collective-permute-start(bf16[256,1152]{1,0:T(8,128)(2,1)S(1)} %get-tuple-element.173), channel_id=1, source_target_pairs={{8,16},{10,18},{12,20},{14,22},{16,24},{18,26},{20,28},{22,30},{9,... | collective-permute-start | bytes 1769480 | tf_op jit(solution)/shard_map/ppermute | solution.py:355
  326.2 33.9 %collective-permute-start.24 = (bf16[256,1152]{1,0:T(8,128)(2,1)S(1)}, bf16[256,1152]{1,0:T(8,128)(2,1)S(1)}, u32[]{:S(2)}, u32[]{:S(2)}) collective-permute-start(bf16[256,1152]{1,0:T(8,128)(2,1)S(1)} %get-tuple-element.174), channel_id=1, source_target_pairs={{0,16},{2,18},{4,20},{6,22},{16,24},{18,26},{20,28},{22,30},{1,17}... | collective-permute-start | bytes 1769480 | tf_op jit(solution)/shard_map/ppermute | solution.py:358
  348.0 42.6 %collective-permute-start.19 = (bf16[256,768]{0,1:T(8,128)(2,1)S(1)}, bf16[256,768]{0,1:T(8,128)(2,1)S(1)}, u32[]{:S(2)}, u32[]{:S(2)}) collective-permute-start(bf16[256,768]{0,1:T(8,128)(2,1)S(1)} %broadcast_select_fusion.16), channel_id=1, source_target_pairs={{0,2},{2,0},{4,6},{6,4},{8,10},{10,8},{12,14},{14,12},{16,18},{18,... | collective-permute-start | bytes 1179656 | tf_op jit(solution)/shard_map/ppermute | solution.py:24
  360.1 50.3 %collective-permute-start.44 = (bf16[2,384,768]{2,1,0:T(8,128)(2,1)}, bf16[2,384,768]{2,1,0:T(8,128)(2,1)}, u32[]{:S(2)}, u32[]{:S(2)}) collective-permute-start(bf16[2,384,768]{2,1,0:T(8,128)(2,1)} %dynamic-slice_bitcast_fusion.1), channel_id=1, source_target_pairs={{0,2},{2,0},{4,6},{6,4},{8,10},{10,8},{12,14},{14,12},{16,18},{18,... | collective-permute-start | bytes 3538952 | tf_op jit(solution)/shard_map/ppermute | solution.py:24
  360.3 2.9 collective-permute-start.26
  373.3 32.2 %collective-permute-start.43 = (bf16[384,768]{1,0:T(8,128)(2,1)}, bf16[384,768]{1,0:T(8,128)(2,1)}, u32[]{:S(2)}, u32[]{:S(2)}) collective-permute-start(bf16[384,768]{1,0:T(8,128)(2,1)} %constant_dynamic-slice_fusion.2), channel_id=1, source_target_pairs={{0,2},{2,0},{4,6},{6,4},{8,10},{10,8},{12,14},{14,12},{16,18},{18,... | collective-permute-start | bytes 1769480 | tf_op jit(solution)/shard_map/ppermute | solution.py:24
  390.6 4.0 collective-permute-start.28
  394.6 14.0 %collective-permute-start.36 = (bf16[768,384]{1,0:T(8,128)(2,1)}, bf16[768,384]{1,0:T(8,128)(2,1)S(1)}, u32[]{:S(2)}, u32[]{:S(2)}) collective-permute-start(bf16[768,384]{1,0:T(8,128)(2,1)} %constant_dynamic-slice_fusion.4), channel_id=1, source_target_pairs={{0,2},{2,0},{4,6},{6,4},{8,10},{10,8},{12,14},{14,12},{16,18},{18,... | collective-permute-start | bytes 1769480 | tf_op jit(solution)/shard_map/ppermute | solution.py:24
  405.5 8.2 %collective-permute-start.29 = (bf16[3,256,384]{2,1,0:T(8,128)(2,1)S(1)}, bf16[3,256,384]{2,1,0:T(8,128)(2,1)S(1)}, u32[]{:S(2)}, u32[]{:S(2)}) collective-permute-start(bf16[3,256,384]{2,1,0:T(8,128)(2,1)S(1)} %constant_dynamic-slice_fusion.5), channel_id=1, source_target_pairs={{0,2},{2,0},{4,6},{6,4},{8,10},{10,8},{12,14},{14,12},{16,18},{18,... | collective-permute-start | bytes 1769480 | tf_op jit(solution)/shard_map/ppermute | solution.py:24
  413.4 105.2 %collective-permute-start.45 = (bf16[4,384,384]{2,1,0:T(8,128)(2,1)}, bf16[4,384,384]{2,1,0:T(8,128)(2,1)}, u32[]{:S(2)}, u32[]{:S(2)}) collective-permute-start(bf16[4,384,384]{2,1,0:T(8,128)(2,1)} %pad_maximum_fusion.14), channel_id=1, source_target_pairs={{0,1},{1,0},{2,3},{3,2},{4,5},{5,4},{6,7},{7,6},{8,9},{9,8},{10,11... | collective-permute-start | bytes 3538952 | tf_op jit(solution)/shard_map/ppermute | solution.py:19
  430.5 12.9 %collective-permute-start.32 = (f32[6,768]{1,0:T(8,128)}, f32[6,768]{1,0:T(8,128)S(1)}, u32[]{:S(2)}, u32[]{:S(2)}) collective-permute-start(f32[6,768]{1,0:T(8,128)} %stack.130), channel_id=1, source_target_pairs={{0,2},{2,0},{4,6},{6,4},{8,10},{10,8},{12,14},{14,12},{16,18},{18,... | collective-permute-start | bytes 55304 | tf_op jit(solution)/shard_map/ppermute | solution.py:24
  434.4 87.4 %collective-permute-start.30 = (bf16[768,768]{0,1:T(8,128)(2,1)S(1)}, bf16[768,768]{0,1:T(8,128)(2,1)S(1)}, u32[]{:S(2)}, u32[]{:S(2)}) collective-permute-start(bf16[768,768]{0,1:T(8,128)(2,1)S(1)} %fusion.12), channel_id=1, source_target_pairs={{0,1},{1,0},{2,3},{3,2},{4,5},{5,4},{6,7},{7,6},{8,9},{9,8},{10,11... | collective-permute-start | bytes 3538952 | tf_op jit(solution)/shard_map/ppermute | solution.py:19
  438.1 136.3 %copy-start.27 = (f32[384,3072]{1,0:T(8,128)}, f32[384,3072]{1,0:T(8,128)S(1)}, u32[]{:S(2)}) copy-start(f32[384,3072]{1,0:T(8,128)S(1)} %convert_add_fusion.1) | copy-start | bytes 14155780
  441.4 80.7 %collective-permute-start.50 = (bf16[384,1536]{1,0:T(8,128)(2,1)S(1)}, bf16[384,1536]{1,0:T(8,128)(2,1)S(1)}, u32[]{:S(2)}, u32[]{:S(2)}) collective-permute-start(bf16[384,1536]{1,0:T(8,128)(2,1)S(1)} %slice.653), channel_id=1, source_target_pairs={{0,1},{1,0},{2,3},{3,2},{4,5},{5,4},{6,7},{7,6},{8,9},{9,8},{10,11... | collective-permute-start | bytes 3538952 | tf_op jit(solution)/shard_map/ppermute | solution.py:19
  443.4 3.9 collective-permute-start.33
  447.3 75.9 %copy-start.28 = (f32[2,768,768]{2,1,0:T(8,128)}, f32[2,768,768]{2,1,0:T(8,128)S(1)}, u32[]{:S(2)}) copy-start(f32[2,768,768]{2,1,0:T(8,128)S(1)} %convert_add_fusion) | copy-start | bytes 14155780
  447.3 13.5 %collective-permute-start.34 = (f32[6,768]{1,0:T(8,128)S(1)}, f32[6,768]{1,0:T(8,128)S(1)}, u32[]{:S(2)}, u32[]{:S(2)}) collective-permute-start(f32[6,768]{1,0:T(8,128)S(1)} %add.290), channel_id=1, source_target_pairs={{0,8},{2,10},{4,12},{6,14},{8,0},{10,2},{12,4},{14,6},{1,9},{3,11}... | collective-permute-start | bytes 55304 | tf_op jit(solution)/shard_map/ppermute | solution.py:24
  459.1 64.0 %collective-permute-start.55 = (bf16[768,768]{1,0:T(8,128)(2,1)S(1)}, bf16[768,768]{1,0:T(8,128)(2,1)S(1)}, u32[]{:S(2)}, u32[]{:S(2)}) collective-permute-start(bf16[768,768]{1,0:T(8,128)(2,1)S(1)} %fusion.23), channel_id=1, source_target_pairs={{0,1},{1,0},{2,3},{3,2},{4,5},{5,4},{6,7},{7,6},{8,9},{9,8},{10,11... | collective-permute-start | bytes 3538952 | tf_op jit(solution)/shard_map/ppermute | solution.py:19
  460.8 57.2 %collective-permute-start.35 = (f32[6,768]{1,0:T(8,128)S(1)}, f32[6,768]{1,0:T(8,128)S(1)}, u32[]{:S(2)}, u32[]{:S(2)}) collective-permute-start(f32[6,768]{1,0:T(8,128)S(1)} %add.291), channel_id=1, source_target_pairs={{0,1},{1,0},{2,3},{3,2},{4,5},{5,4},{6,7},{7,6},{8,9},{9,8},{10,11... | collective-permute-start | bytes 55304 | tf_op jit(solution)/shard_map/ppermute | solution.py:19
  518.0 8.2 %collective-permute-start.37 = (bf16[3,384,768]{2,1,0:T(8,128)(2,1)S(1)}, bf16[3,384,768]{2,1,0:T(8,128)(2,1)S(1)}, u32[]{:S(2)}, u32[]{:S(2)}) collective-permute-start(bf16[3,384,768]{2,1,0:T(8,128)(2,1)S(1)} %dynamic-slice_bitcast_fusion), channel_id=1, source_target_pairs={{0,2},{2,0},{4,6},{6,4},{8,10},{10,8},{12,14},{14,12},{16,18},{18,... | collective-permute-start | bytes 5308424 | tf_op jit(solution)/shard_map/ppermute | solution.py:24
  520.3 28.8 %collective-permute-start.46 = (bf16[4,384,384]{2,1,0:T(8,128)(2,1)S(1)}, bf16[4,384,384]{2,1,0:T(8,128)(2,1)S(1)}, u32[]{:S(2)}, u32[]{:S(2)}) collective-permute-start(bf16[4,384,384]{2,1,0:T(8,128)(2,1)S(1)} %fusion.72), channel_id=1, source_target_pairs={{0,4},{2,6},{4,0},{6,2},{8,12},{10,14},{12,8},{14,10},{16,20},{18,... | collective-permute-start | bytes 3538952 | tf_op jit(solution)/shard_map/ppermute | solution.py:24
  521.9 4.2 collective-permute-start.31
  522.6 51.8 %collective-permute-start.51 = (bf16[384,1536]{1,0:T(8,128)(2,1)S(1)}, bf16[384,1536]{1,0:T(8,128)(2,1)S(1)}, u32[]{:S(2)}, u32[]{:S(2)}) collective-permute-start(bf16[384,1536]{1,0:T(8,128)(2,1)S(1)} %fusion.30), channel_id=1, source_target_pairs={{0,4},{2,6},{4,0},{6,2},{8,12},{10,14},{12,8},{14,10},{16,20},{18,... | collective-permute-start | bytes 3538952 | tf_op jit(solution)/shard_map/ppermute | solution.py:24
  524.4 74.9 %collective-permute-start.56 = (bf16[768,768]{1,0:T(8,128)(2,1)}, bf16[768,768]{1,0:T(8,128)(2,1)}, u32[]{:S(2)}, u32[]{:S(2)}) collective-permute-start(bf16[768,768]{1,0:T(8,128)(2,1)} %fusion.31), channel_id=1, source_target_pairs={{0,4},{2,6},{4,0},{6,2},{8,12},{10,14},{12,8},{14,10},{16,20},{18,... | collective-permute-start | bytes 3538952 | tf_op jit(solution)/shard_map/ppermute | solution.py:24
  529.7 84.2 %collective-permute-start.38 = (bf16[4,384,384]{2,1,0:T(8,128)(2,1)}, bf16[4,384,384]{2,1,0:T(8,128)(2,1)}, u32[]{:S(2)}, u32[]{:S(2)}) collective-permute-start(bf16[4,384,384]{2,1,0:T(8,128)(2,1)} %pad_maximum_fusion.13), channel_id=1, source_target_pairs={{0,1},{1,0},{2,3},{3,2},{4,5},{5,4},{6,7},{7,6},{8,9},{9,8},{10,11... | collective-permute-start | bytes 3538952 | tf_op jit(solution)/shard_map/ppermute | solution.py:19
  552.3 65.0 %collective-permute-start.47 = (bf16[4,384,384]{2,1,0:T(8,128)(2,1)}, bf16[4,384,384]{2,1,0:T(8,128)(2,1)}, u32[]{:S(2)}, u32[]{:S(2)}) collective-permute-start(bf16[4,384,384]{2,1,0:T(8,128)(2,1)} %fusion.20), channel_id=1, source_target_pairs={{0,8},{2,10},{4,12},{6,14},{8,0},{10,2},{12,4},{14,6},{1,9},{3,11}... | collective-permute-start | bytes 3538952 | tf_op jit(solution)/shard_map/ppermute | solution.py:24
  576.0 43.7 %collective-permute-start.52 = (bf16[384,1536]{1,0:T(8,128)(2,1)}, bf16[384,1536]{1,0:T(8,128)(2,1)}, u32[]{:S(2)}, u32[]{:S(2)}) collective-permute-start(bf16[384,1536]{1,0:T(8,128)(2,1)} %fusion.21), channel_id=1, source_target_pairs={{0,8},{2,10},{4,12},{6,14},{8,0},{10,2},{12,4},{14,6},{1,9},{3,11}... | collective-permute-start | bytes 3538952 | tf_op jit(solution)/shard_map/ppermute | solution.py:24
  601.8 38.5 %collective-permute-start.57 = (bf16[768,768]{1,0:T(8,128)(2,1)S(1)}, bf16[768,768]{1,0:T(8,128)(2,1)S(1)}, u32[]{:S(2)}, u32[]{:S(2)}) collective-permute-start(bf16[768,768]{1,0:T(8,128)(2,1)S(1)} %fusion.22), channel_id=1, source_target_pairs={{0,8},{2,10},{4,12},{6,14},{8,0},{10,2},{12,4},{14,6},{1,9},{3,11}... | collective-permute-start | bytes 3538952 | tf_op jit(solution)/shard_map/ppermute | solution.py:24
  615.7 27.4 %collective-permute-start.39 = (bf16[4,384,384]{2,1,0:T(8,128)(2,1)S(1)}, bf16[4,384,384]{2,1,0:T(8,128)(2,1)S(1)}, u32[]{:S(2)}, u32[]{:S(2)}) collective-permute-start(bf16[4,384,384]{2,1,0:T(8,128)(2,1)S(1)} %fusion.47), channel_id=1, source_target_pairs={{0,4},{2,6},{4,0},{6,2},{8,12},{10,14},{12,8},{14,10},{16,20},{18,... | collective-permute-start | bytes 3538952 | tf_op jit(solution)/shard_map/ppermute | solution.py:24
  619.6 28.1 %collective-permute-start.48 = (bf16[4,384,384]{2,1,0:T(8,128)(2,1)S(1)}, bf16[4,384,384]{2,1,0:T(8,128)(2,1)S(1)}, u32[]{:S(2)}, u32[]{:S(2)}) collective-permute-start(bf16[4,384,384]{2,1,0:T(8,128)(2,1)S(1)} %get-tuple-element.115), channel_id=1, source_target_pairs={{0,2},{2,0},{4,6},{6,4},{8,10},{10,8},{12,14},{14,12},{16,18},{18,... | collective-permute-start | bytes 3538952 | tf_op jit(solution)/shard_map/ppermute | solution.py:24
  621.8 26.3 %collective-permute-start.53 = (bf16[384,1536]{1,0:T(8,128)(2,1)S(1)}, bf16[384,1536]{1,0:T(8,128)(2,1)S(1)}, u32[]{:S(2)}, u32[]{:S(2)}) collective-permute-start(bf16[384,1536]{1,0:T(8,128)(2,1)S(1)} %get-tuple-element.113), channel_id=1, source_target_pairs={{0,2},{2,0},{4,6},{6,4},{8,10},{10,8},{12,14},{14,12},{16,18},{18,... | collective-permute-start | bytes 3538952 | tf_op jit(solution)/shard_map/ppermute | solution.py:24
  642.2 36.5 %collective-permute-start.58 = (bf16[768,768]{1,0:T(8,128)(2,1)S(1)}, bf16[768,768]{1,0:T(8,128)(2,1)S(1)}, u32[]{:S(2)}, u32[]{:S(2)}) collective-permute-start(bf16[768,768]{1,0:T(8,128)(2,1)S(1)} %get-tuple-element.111), channel_id=1, source_target_pairs={{0,2},{2,0},{4,6},{6,4},{8,10},{10,8},{12,14},{14,12},{16,18},{18,... | collective-permute-start | bytes 3538952 | tf_op jit(solution)/shard_map/ppermute | solution.py:24
  644.8 29.4 %collective-permute-start.40 = (bf16[4,384,384]{2,1,0:T(8,128)(2,1)S(1)}, bf16[4,384,384]{2,1,0:T(8,128)(2,1)S(1)}, u32[]{:S(2)}, u32[]{:S(2)}) collective-permute-start(bf16[4,384,384]{2,1,0:T(8,128)(2,1)S(1)} %fusion.19), channel_id=1, source_target_pairs={{0,8},{2,10},{4,12},{6,14},{8,0},{10,2},{12,4},{14,6},{1,9},{3,11}... | collective-permute-start | bytes 3538952 | tf_op jit(solution)/shard_map/ppermute | solution.py:24
  676.1 5.5 collective-permute-start.41
  (154 other events, 1018.1 us)

commit v2 on v1

v2 whole, which is shorter than its diff:
```python
import functools

import jax
import jax.numpy as jnp
from jax import lax
from jax.experimental import pallas as pl
from jax.experimental.pallas import tpu as pltpu
from jax.sharding import PartitionSpec as P


HEAD_DIM = 64
EPSILON = 1e-06
SCORE_SCALE = 0.125
MASKED = -1e30
BF16 = jnp.bfloat16
F32 = jnp.float32
COST_BYTES = 1

FULL, CORE, ACROSS, SECOND_PLANE, TOP_BIG, BOTTOM_BIG, TOP_MID, BOTTOM_MID, ENDS = range(9)
SELF_A, SELF_B, CROSS_A, CROSS_B = range(4)


def over_head(value):
    return lax.ppermute(value, "head", [(0, 1), (1, 0)])


def over_bit(value, bit, count=None):
    count = lax.axis_size("clip") if count is None else count
    return lax.ppermute(value, "clip", [(i, i ^ (1 << bit)) for i in range(count)])


def other_core(value):
    return over_bit(value, 0)


def fence(*values):
    return lax.optimization_barrier(values)


def after(value, *others):
    return lax.optimization_barrier((value,) + others)[0]


def in_core_order(core, mine, theirs, axis):
    first = jnp.where(core == 0, mine, theirs)
    second = jnp.where(core == 0, theirs, mine)
    return jnp.concatenate([first, second], axis=axis)


def core_piece(value, piece, axis):
    size = value.shape[axis] // 2
    return lax.dynamic_slice_in_dim(value, piece * size, size, axis)


def dot_nt(left, right):
    return lax.dot_general(left, right, (((1,), (1,)), ((), ())), preferred_element_type=F32)


def dot_tn(left, right):
    return lax.dot_general(left, right, (((0,), (0,)), ((), ())), preferred_element_type=F32)


def dot_nn(left, right):
    return jnp.dot(left, right, preferred_element_type=F32)


def norm_stats(rows):
    mean = jnp.mean(rows, axis=-1, keepdims=True)
    centered = rows - mean
    variance = jnp.mean(centered * centered, axis=-1, keepdims=True)
    inverse = lax.rsqrt(variance + EPSILON)
    return centered * inverse, inverse


def norm_back(grad, normal, inverse, gain):
    scaled = grad * gain
    mean = jnp.mean(scaled, axis=-1, keepdims=True)
    along = jnp.mean(scaled * normal, axis=-1, keepdims=True)
    grad_rows = (scaled - mean - normal * along) * inverse
    gain_grad = jnp.sum(grad * normal, axis=0, keepdims=True)
    return grad_rows, gain_grad, jnp.sum(grad, axis=0, keepdims=True)


def pick(info, flag, yes, no):
    return jnp.where(info[flag] != 0, yes, no)


def core_order(info, mine, theirs):
    return pick(info, CORE, theirs, mine), pick(info, CORE, mine, theirs)


def joined_pieces(info, mine, theirs, axis):
    return jnp.concatenate(core_order(info, mine, theirs), axis=axis)


def exchanged(info, top_flag, first, second, received):
    return pick(info, top_flag, received, first), pick(info, top_flag + 1, received, second)


def to_send(info, first, second):
    return pick(info, CORE, first, second)


def put_pieces(info, keep_ref, send_ref, at, value, axis):
    size = value.shape[axis] // 2
    low, high = (value[:size], value[size:]) if axis == 0 else (value[:, :size], value[:, size:])
    mine, theirs = core_order(info, low.astype(BF16), high.astype(BF16))
    keep_ref[at] = mine
    send_ref[at] = theirs


def resident(shape, index=None):
    index = (lambda j, info: (0,) * len(shape)) if index is None else index
    return pl.BlockSpec(shape, index, pipeline_mode=pl.Buffered(1))


def whole_in(array):
    return (array, resident(array.shape))


def whole_out(*shape, kind=BF16):
    return (shape, kind, resident(shape))


def lead_spec(*shape):
    return pl.BlockSpec((None,) + shape, lambda j, info: (j,) + (0,) * len(shape))


def out_type(shape, kind, spec, in_hbm=False):
    return pltpu.HBM(shape, kind) if in_hbm else jax.ShapeDtypeStruct(shape, kind)


def call(kernel, info, steps, ins, outs, scratch, name, mebibytes, cost):
    return pl.pallas_call(
        kernel,
        grid_spec=pltpu.PrefetchScalarGridSpec(
            num_scalar_prefetch=1,
            grid=(steps,),
            in_specs=[spec for _, spec in ins],
            out_specs=[out[2] for out in outs],
            scratch_shapes=scratch,
        ),
        out_shape=[out_type(*out) for out in outs],
        compiler_params=pltpu.CompilerParams(vmem_limit_bytes=mebibytes * 1024 * 1024),
        cost_estimate=pl.CostEstimate(flops=0, bytes_accessed=cost * COST_BYTES, transcendentals=0),
        name=name,
    )(info, *[array for array, _ in ins])


def part_rows(array):
    _, count, width = array.shape
    return [
        (array, resident((None, count, width), lambda j, info: (info[ACROSS], 0, 0))),
        (array, resident((None, count // 2, width), lambda j, info: (2, info[CORE], 0))),
    ]


def joined_rows(info, a_ref, kept_ref, received_ref):
    own = info[CORE] == info[ACROSS]
    return jnp.concatenate([a_ref[...], jnp.where(own, kept_ref[...], received_ref[...])], axis=0)


def clip_bias(info, group, rows, cols, row_kind, col_kind):
    def clips(kind, places, shape, axis):
        base = ENDS + 16 * group + 4 * kind
        place = lax.broadcasted_iota(jnp.int32, shape, axis) + places.start
        return sum((place >= info[base + k]).astype(jnp.int32) for k in range(4))

    of_rows = clips(row_kind, rows, (rows.stop - rows.start, 128), 0)[:, :1]
    of_cols = clips(col_kind, cols, (8, cols.stop - cols.start), 1)[:1, :]
    return jnp.where(of_rows == of_cols, 0.0, MASKED)


def attention_blocks(full, cross, half):
    if full and cross:
        return [(None, (0, 1), slice(0, half), slice(0, 2 * half))]
    if full:
        return [(s, (0, 1), slice(s * half, (s + 1) * half), slice(0, 2 * half)) for s in range(2)]
    if cross:
        return [(s, (s,), slice(0, half), slice(s * half, (s + 1) * half)) for s in range(2)]
    return [(s, (s,), slice(s * half, (s + 1) * half), slice(0, half)) for s in range(2)]


def load_halves(info, refs, exchange):
    first, second = refs[0][...], refs[1][...]
    if exchange:
        first, second = exchanged(info, TOP_BIG, first, second, refs[2][...])
    return first, second


def query_half(info, halves, s):
    return pick(info, SECOND_PLANE, halves[1], halves[0]) if s is None else halves[s]


def head_lanes(h):
    first = lax.broadcasted_iota(jnp.int32, (1, 2 * HEAD_DIM), 1) < HEAD_DIM
    return first if h == 0 else jnp.logical_not(first)


def attend_kernel(group, counts, info, *refs):
    cross = group in (CROSS_A, CROSS_B)
    part_b = group in (SELF_B, CROSS_B)
    operands, at = [], 0
    for n in counts:
        operands.append(refs[at : at + n])
        at += n
    outs = refs[at:]
    bias_ref = outs[-1]
    p_ref = outs[-2]
    q, k, v = (load_halves(info, refs, len(refs) == 3) for refs in operands)
    half = q[0].shape[0]

    def run(full):
        blocks = attention_blocks(full, cross, half)

        @pl.when(pl.program_id(0) == 0)
        def _():
            for s, keys, rows, cols in blocks:
                at = rows if full else slice(0, half)
                kinds = (0, 1) if full else (2 + s, 2 + s)
                bias_ref[rows, cols] = clip_bias(info, group, at, slice(0, half * len(keys)), *kinds)

        mixes = []
        for s, keys, rows, cols in blocks:
            query = query_half(info, q, s) * jnp.asarray(SCORE_SCALE, BF16)
            key = jnp.concatenate([k[t] for t in keys], axis=0)
            value = jnp.concatenate([v[t] for t in keys], axis=0)
            pair = []
            for h in range(2):
                own = jnp.where(head_lanes(h), query, jnp.zeros_like(query))
                scores = dot_nt(own, key) + bias_ref[rows, cols]
                top = jnp.max(scores, axis=-1, keepdims=True)
                exponent = jnp.exp(scores - top)
                total = jnp.sum(exponent, axis=-1, keepdims=True)
                probs = (exponent * (1.0 / total)).astype(BF16)
                p_ref[h, rows, cols] = probs
                pair.append(dot_nn(probs, value))
            mixes.append(jnp.where(head_lanes(0), pair[0], pair[1]).astype(BF16))
        top, bottom = mixes[0], mixes[-1]
        if cross:
            outs[0][...] = top
            outs[1][...] = bottom
        else:
            outs[0][:half, :] = top
            outs[0][half:, :] = bottom
            if part_b:
                outs[1][...] = to_send(info, top, bottom)

    pl.when(info[FULL] != 0)(lambda: run(True))
    pl.when(info[FULL] == 0)(lambda: run(False))


def attend_back_kernel(group, counts, info, *refs):
    cross = group in (CROSS_A, CROSS_B)
    part_b = group in (SELF_B, CROSS_B)
    operands, at = [], 0
    for n in counts:
        operands.append(refs[at : at + n])
        at += n
    p_ref, outs = refs[at], refs[at + 1 :]
    q, k, v, g = (load_halves(info, refs, len(refs) == 3) for refs in operands)
    half = q[0].shape[0]

    def run(full):
        blocks = attention_blocks(full, cross, half)
        queries, sums = [], {}
        for s, keys, rows, cols in blocks:
            query = query_half(info, q, s)
            grad = query_half(info, g, s)
            key = jnp.concatenate([k[t] for t in keys], axis=0)
            value = jnp.concatenate([v[t] for t in keys], axis=0)
            dq, dk, dv = [], [], []
            for h in range(2):
                own = jnp.where(head_lanes(h), grad, jnp.zeros_like(grad))
                probs = p_ref[h, rows, cols]
                wide_probs = probs.astype(F32)
                grad_probs = dot_nt(own, value)
                delta = jnp.sum(wide_probs * grad_probs, axis=-1, keepdims=True)
                grad_scores = (wide_probs * (grad_probs - delta)).astype(BF16)
                dq.append(dot_nn(grad_scores, key))
                dk.append(dot_tn(grad_scores, query))
                dv.append(dot_tn(probs, grad))
            queries.append((jnp.where(head_lanes(0), dq[0], dq[1]) * SCORE_SCALE).astype(BF16))
            both = (jnp.where(head_lanes(0), dk[0], dk[1]), jnp.where(head_lanes(0), dv[0], dv[1]))
            sums[keys] = (sums[keys][0] + both[0], sums[keys][1] + both[1]) if keys in sums else both
        grads = []
        for t in range(2):
            dk, dv = (sums[(0, 1)] if full else sums[(t,)])
            rows = slice(t * half, (t + 1) * half) if full else slice(0, half)
            grads.append(((dk[rows] * SCORE_SCALE).astype(BF16), dv[rows].astype(BF16)))
        top, bottom = queries[0], queries[-1]
        if cross:
            outs[0][...] = top
            outs[1][...] = bottom
        parts = [(g0, g1) for g0, g1 in zip(*grads)]
        if not cross:
            parts = [(top, bottom)] + parts
        out_ref = outs[2] if cross else outs[0]
        for n, (first, second) in enumerate(parts):
            out_ref[n, :half, :] = first
            out_ref[n, half:, :] = second
            if part_b:
                outs[3 if cross else 1][n] = to_send(info, first, second)

    pl.when(info[FULL] != 0)(lambda: run(True))
    pl.when(info[FULL] == 0)(lambda: run(False))


def column_block(array, lead=None, row=0, column=0, rows=256):
    lanes = 2 * HEAD_DIM
    if array.ndim == 3:
        return (array, pl.BlockSpec((None, rows, lanes), lambda j, info: (lead, row, j + column)))
    return (array, pl.BlockSpec((rows, lanes), lambda j, info: (row, j + column)))


def halves_of(array, lead=None):
    return [column_block(array, lead, 0), column_block(array, lead, 1)]


def attend(info, group, operands, columns, rows=256):
    cross = group in (CROSS_A, CROSS_B)
    lanes = 2 * HEAD_DIM
    heads = columns // HEAD_DIM
    p_rows = rows if cross else 2 * rows
    half_out = ((rows, columns), BF16, pl.BlockSpec((rows, lanes), lambda j, info: (0, j)))
    mix_out = ((2 * rows, columns), BF16, pl.BlockSpec((2 * rows, lanes), lambda j, info: (0, j)))
    outs = [half_out, half_out] if cross else [mix_out] + ([half_out] if group == SELF_B else [])
    p_block = pl.BlockSpec((2, p_rows, 2 * rows), lambda j, info: (j, 0, 0))
    p_out = ((heads, p_rows, 2 * rows), BF16, p_block, True)
    return call(
        functools.partial(attend_kernel, group, [len(o) for o in operands]),
        info,
        heads // 2,
        sum(operands, []),
        outs + [p_out],
        [pltpu.VMEM((p_rows, 2 * rows), F32)],
        "attend",
        14,
        heads * 2 // 3,
    )


def attend_back(info, group, operands, probs, columns, rows=256):
    cross = group in (CROSS_A, CROSS_B)
    part_b = group in (SELF_B, CROSS_B)
    lanes = 2 * HEAD_DIM
    half_out = ((rows, columns), BF16, pl.BlockSpec((rows, lanes), lambda j, info: (0, j)))
    count = 2 if cross else 3

    def stacked(height):
        return ((count, height, columns), BF16, pl.BlockSpec((count, height, lanes), lambda j, info: (0, 0, j)))

    outs = [half_out, half_out] if cross else []
    outs = outs + [stacked(2 * rows)] + ([stacked(rows)] if part_b else [])
    p_block = pl.BlockSpec((2,) + probs.shape[1:], lambda j, info: (j, 0, 0))
    return call(
        functools.partial(attend_back_kernel, group, [len(o) for o in operands]),
        info,
        probs.shape[0] // 2,
        sum(operands, []) + [(probs, p_block)],
        outs,
        [],
        "attend_back",
        14,
        probs.shape[0],
    )


def first_project_kernel(info, a_ref, kept_ref, received_ref, norms_ref, w_ref, rows_ref, normed_ref, out_ref):
    @pl.when(pl.program_id(0) == 0)
    def _():
        rows = joined_rows(info, a_ref, kept_ref, received_ref)
        rows_ref[...] = rows
        normal, _ = norm_stats(rows.astype(F32))
        normed_ref[...] = (normal * norms_ref[0:1, :] + norms_ref[1:2, :]).astype(BF16)

    out_ref[...] = dot_nn(normed_ref[...], w_ref[...]).astype(BF16)


def first_project(info, tokens, received, norms, w_self):
    count, width, cols = w_self.shape
    rows = tokens.shape[1] + received.shape[0]
    return call(
        first_project_kernel,
        info,
        count,
        part_rows(tokens) + [whole_in(received), whole_in(norms), (w_self, lead_spec(width, cols))],
        [whole_out(rows, width), whole_out(rows, width), ((count, rows, cols), BF16, lead_spec(rows, cols))],
        [],
        "first_project",
        16,
        4,
    )


def other_project_kernel(info, normed_ref, own_b_ref, mine_ref, theirs_ref, out_ref, send_ref):
    weights = joined_pieces(info, mine_ref[...], theirs_ref[...], 0)
    out = dot_nn(normed_ref[...], weights).astype(BF16)
    out_ref[...] = out
    part_b = out.shape[0] - own_b_ref.shape[0]
    send_ref[...] = to_send(info, own_b_ref[...], out[part_b:])


def other_project(info, normed, qkv_own, mine, theirs, part_b):
    count, half, cols = mine.shape
    rows = normed.shape[0]
    own_b = pl.BlockSpec((None, part_b, cols), lambda j, info: (j, rows // part_b - 1, 0))
    return call(
        other_project_kernel,
        info,
        count,
        [whole_in(normed), (qkv_own, own_b), (mine, lead_spec(half, cols)), (theirs, lead_spec(half, cols))],
        [
            ((count, rows, cols), BF16, lead_spec(rows, cols)),
            ((count, part_b, cols), BF16, lead_spec(part_b, cols)),
        ],
        [],
        "other_project",
        12,
        3,
    )


def put_query_parts(info, value, far_ref, near_ref, left_ref, right_ref, send_ref):
    rows = left_ref.shape[0]
    cols = left_ref.shape[1]
    for h in range(2):
        at = slice(h * cols, (h + 1) * cols)
        far_ref[:, at] = value[h][:rows]
        near_ref[:, at] = value[h][rows : 2 * rows]
    left, right = value[0][2 * rows :], value[1][2 * rows :]
    left_ref[...] = left
    right_ref[...] = right
    send_ref[...] = to_send(info, left, right)


def query_outs(rows, width):
    whole, half = whole_out(rows, width), whole_out(rows, width // 2)
    return [whole, whole, half, half, half]


def self_mixes(info, mix0_ref, mix1_ref, slots_ref, received_ref):
    rows = received_ref.shape[0]
    parts = exchanged(info, TOP_BIG, slots_ref[:rows, :], slots_ref[rows:, :], received_ref[...])
    return [
        jnp.concatenate([ref[...], part], axis=0) for ref, part in zip((mix0_ref, mix1_ref), parts)
    ]


def second_project_kernel(
    info, rows_ref, norms_ref, mix0_ref, mix1_ref, slots_ref, received_ref, out_ref, query_ref, mine_ref, theirs_ref,
    hidden_ref, joined_ref, *query_refs,
):
    mixes = self_mixes(info, mix0_ref, mix1_ref, slots_ref, received_ref)
    other_out = joined_pieces(info, mine_ref[0], theirs_ref[0], 1)
    hidden = rows_ref[...].astype(F32) + dot_nn(mixes[0], out_ref[...]) + dot_nn(mixes[1], other_out)
    hidden_ref[...] = hidden
    normal, _ = norm_stats(hidden)
    joined = (normal * norms_ref[2:3, :] + norms_ref[3:4, :]).astype(BF16)
    joined_ref[...] = joined
    other_query = joined_pieces(info, mine_ref[1], theirs_ref[1], 0)
    queries = [dot_nn(joined, w).astype(BF16) for w in (query_ref[...], other_query)]
    put_query_parts(info, queries, *query_refs)


def second_project(info, rows, norms, mixes, w_self_out, w_query, mine, theirs, part_b):
    shape = rows.shape
    return call(
        second_project_kernel,
        info,
        1,
        [whole_in(a) for a in (rows, norms, *mixes, w_self_out, w_query, mine, theirs)],
        [whole_out(*shape, kind=F32), whole_out(*shape)] + query_outs(part_b, shape[1]),
        [],
        "second_project",
        20,
        5,
    )


def offer_project_kernel(info, rows_ref, own_ref, mine_ref, theirs_ref, out_ref, send_ref):
    cols = own_ref.shape[1]
    rows = send_ref.shape[0]
    other = joined_pieces(info, mine_ref[...], theirs_ref[...], 0)
    parts = [dot_nn(rows_ref[...], w).astype(BF16) for w in (own_ref[...], other)]
    for h in range(2):
        out_ref[:, h * cols : (h + 1) * cols] = parts[h]
    send_ref[...] = to_send(info, parts[0][-rows:], parts[1][-rows:])


def offer_project(info, joined, w_offer, mine, theirs, part_b):
    count, width, cols = w_offer.shape
    rows = joined.shape[0]
    piece = lead_spec(cols, cols)
    return call(
        offer_project_kernel,
        info,
        count,
        [whole_in(joined), (w_offer, lead_spec(width, cols)), (mine, piece), (theirs, piece)],
        [
            ((count, rows, 2 * cols), BF16, lead_spec(rows, 2 * cols)),
            ((count, part_b, cols), BF16, lead_spec(part_b, cols)),
        ],
        [],
        "offer_project",
        12,
        4,
    )


def reader_rows(info, far_ref, near_ref, far_b_ref, near_b_ref, received_ref):
    half = far_b_ref.shape[1]
    parts = exchanged(info, TOP_MID, far_b_ref[...], near_b_ref[...], received_ref[...])
    return [
        jnp.concatenate([ref[:, h * half : (h + 1) * half] for ref in (far_ref, near_ref)] + [parts[h]], axis=0)
        for h in range(2)
    ]


def mlp_kernel(
    info, hidden_ref, norms_ref, far_ref, near_ref, far_b_ref, near_b_ref, received_ref, w_cross_ref, mine_ref,
    theirs_ref, grad_a_ref, grad_kept_ref, grad_received_ref, up_ref, down_ref, result_ref, grad_second_ref, gm_far_ref, gm_near_ref, gm_left_ref, gm_right_ref,
    gm_send_ref, up_keep_ref, up_send_ref, down_keep_ref, down_send_ref, keep_ref, send_ref, g_norms_ref, second_ref,
    rows_ref, grad_ref, sum_ref, back_ref,
):
    step = pl.program_id(0)

    def mixes():
        return reader_rows(info, far_ref, near_ref, far_b_ref, near_b_ref, received_ref)

    def cross_weights():
        return w_cross_ref[...], joined_pieces(info, mine_ref[...], theirs_ref[...], 1)

    @pl.when(step == 0)
    def _():
        grad_ref[...] = joined_rows(info, grad_a_ref, grad_kept_ref, grad_received_ref)
        second = hidden_ref[...]
        for mix, weight in zip(mixes(), cross_weights()):
            second = second + dot_nn(mix, weight)
        second_ref[...] = second
        normal, _ = norm_stats(second)
        rows_ref[...] = (normal * norms_ref[4:5, :] + norms_ref[5:6, :]).astype(BF16)
        sum_ref[...] = second
        back_ref[...] = jnp.zeros_like(back_ref)

    rows, grad, up, down = rows_ref[...], grad_ref[...], up_ref[...], down_ref[...]
    pre = dot_nn(rows, up)
    spread = lax.erf(pre * 0.7071067811865476) * 0.5 + 0.5
    slope = spread + pre * (jnp.exp(pre * pre * -0.5) * 0.3989422804014327)
    activated = (pre * spread).astype(BF16)
    grad_up = (dot_nt(grad, down) * slope).astype(BF16)
    sum_ref[...] += dot_nn(activated, down)
    back_ref[...] += dot_nt(grad_up, up)
    g_up = dot_tn(rows, grad_up).astype(BF16)
    g_down = dot_tn(activated, grad).astype(BF16)

    @pl.when(step < 2)
    def _():
        up_keep_ref[...] = g_up
        down_keep_ref[...] = g_down

    @pl.when(step >= 2)
    def _():
        up_send_ref[...] = g_up
        down_send_ref[...] = g_down

    @pl.when(step == 3)
    def _():
        result_ref[...] = sum_ref[...].astype(BF16)
        normal, inverse = norm_stats(second_ref[...])
        back, gain, shift = norm_back(back_ref[...], normal, inverse, norms_ref[4:5, :])
        g_norms_ref[0:1, :] = gain
        g_norms_ref[1:2, :] = shift
        grad_second = grad_ref[...].astype(F32) + back
        grad_second_ref[...] = grad_second
        rounded = grad_second.astype(BF16)
        parts = []
        for h, (mix, weight) in enumerate(zip(mixes(), cross_weights())):
            parts.append(dot_nt(rounded, weight).astype(BF16))
            put_pieces(info, keep_ref, send_ref, h, dot_tn(mix, rounded), 1)
        put_query_parts(info, parts, gm_far_ref, gm_near_ref, gm_left_ref, gm_right_ref, gm_send_ref)


def mlp(info, hidden, norms, mixes, w_cross, mine, theirs, cotangent, received, up, down):
    rows, width = hidden.shape
    half = width // 2
    part_b = received.shape[0]

    def pieces(index):
        return ((2, width, width), BF16, pl.BlockSpec((None, width, width), lambda j, info: (index(j), 0, 0)))

    keep, send = pieces(lambda j: jnp.minimum(j, 1)), pieces(lambda j: jnp.maximum(j - 2, 0))
    wide = pltpu.VMEM((rows, width), F32)
    narrow = pltpu.VMEM((rows, width), BF16)
    return call(
        mlp_kernel,
        info,
        4,
        [whole_in(a) for a in (hidden, norms, *mixes, w_cross)]
        + [whole_in(mine), whole_in(theirs)]
        + part_rows(cotangent)
        + [whole_in(received), (up, lead_spec(width, width)), (down, lead_spec(width, width))],
        [whole_out(rows, width), whole_out(rows, width, kind=F32)]
        + query_outs(part_b, width)
        + [keep, send, keep, send, whole_out(2, half, half), whole_out(2, half, half)]
        + [whole_out(2, width, kind=F32)],
        [wide, narrow, narrow, wide, wide],
        "mlp",
        46,
        34,
    )


def second_back_kernel(
    info, far_ref, near_ref, far_b_ref, near_b_ref, received_ref, dkv_ref, slots_ref, slots_received_ref, joined_ref,
    hidden_ref, grad_second_ref, norms_ref, offer_ref, offer_mine_ref, offer_theirs_ref, query_ref, out_ref, mine_ref,
    theirs_ref, mix0_ref, mix1_ref, mix_slots_ref, mix_received_ref, cross_keep_ref, cross_send_ref, grad_hidden_ref,
    grad_mix_ref, mix_send_ref, keep_ref, send_ref, g_norms_ref, back_ref,
):
    step = pl.program_id(0)
    half = query_ref.shape[1]
    rows = received_ref.shape[0]

    def add(at, grads, weights, first):
        joined = joined_ref[...]
        total = dot_nt(grads[0], weights[0]) + dot_nt(grads[1], weights[1])
        back_ref[...] = total if first else back_ref[...] + total
        for h in range(2):
            put_pieces(info, keep_ref, send_ref, (h, at), dot_tn(joined, grads[h]), 0)

    def add_offer(at):
        parts = exchanged(info, TOP_BIG, slots_ref[:rows, :], slots_ref[rows:, :], slots_received_ref[...])
        grads = [
            jnp.concatenate([dkv_ref[:, h * half : (h + 1) * half], parts[h]], axis=0) for h in range(2)
        ]
        other = joined_pieces(info, offer_mine_ref[...], offer_theirs_ref[...], 0)
        add(at, grads, (offer_ref[...], other), at == 0)

    pl.when(step == 0)(lambda: add_offer(0))
    pl.when(step == 1)(lambda: add_offer(1))

    @pl.when(step == 2)
    def _():
        for h in range(2):
            keep_ref[h, 4] = cross_keep_ref[h]
            send_ref[h, 4] = cross_send_ref[h]
        grads = reader_rows(info, far_ref, near_ref, far_b_ref, near_b_ref, received_ref)
        add(2, grads, (query_ref[...], joined_pieces(info, mine_ref[1], theirs_ref[1], 0)), False)
        normal, inverse = norm_stats(hidden_ref[...])
        back, gain, shift = norm_back(back_ref[...], normal, inverse, norms_ref[2:3, :])
        g_norms_ref[0:1, :] = gain
        g_norms_ref[1:2, :] = shift
        grad_hidden = grad_second_ref[...] + back
        grad_hidden_ref[...] = grad_hidden
        rounded = grad_hidden.astype(BF16)
        mixes = self_mixes(info, mix0_ref, mix1_ref, mix_slots_ref, mix_received_ref)
        parts = []
        for h, weight in enumerate((out_ref[...], joined_pieces(info, mine_ref[0], theirs_ref[0], 1))):
            part = dot_nt(rounded, weight).astype(BF16)
            grad_mix_ref[h] = part
            parts.append(part[-rows:])
            put_pieces(info, keep_ref, send_ref, (h, 3), dot_tn(mixes[h], rounded), 1)
        mix_send_ref[...] = to_send(info, *parts)


def second_back(
    info, grad_q, dkv, slots, slots_received, joined, hidden, grad_second, norms, w_offer, offer_mine, offer_theirs,
    w_query, w_self_out, mine, theirs, mixes, cross_keep, cross_send,
):
    rows, width = hidden.shape
    half = width // 2
    part_b = slots_received.shape[1]

    def offered(array, *shape):
        return (array, pl.BlockSpec((None,) + shape, lambda j, info: (jnp.minimum(j, 1), 0, 0)))

    return call(
        second_back_kernel,
        info,
        3,
        [whole_in(a) for a in grad_q]
        + [offered(dkv, *dkv.shape[1:]), offered(slots, *slots.shape[1:])]
        + [offered(slots_received, *slots_received.shape[1:])]
        + [whole_in(a) for a in (joined, hidden, grad_second, norms)]
        + [offered(w_offer, width, half), offered(offer_mine, half, half), offered(offer_theirs, half, half)]
        + [whole_in(a) for a in (w_query, w_self_out, mine, theirs, *mixes, cross_keep, cross_send)],
        [whole_out(rows, width, kind=F32), whole_out(2, rows, half), whole_out(part_b, half)]
        + [whole_out(2, 5, half, half), whole_out(2, 5, half, half), whole_out(2, width, kind=F32)],
        [pltpu.VMEM((rows, width), F32)],
        "second_back",
        40,
        12,
    )


def first_back_kernel(
    info, own_ref, other_ref, slots_ref, received_ref, rows_ref, normed_ref, grad_hidden_ref, norms_ref, w_own_ref,
    mine_ref, theirs_ref, grad_rows_ref, keep_ref, send_ref, g_norms_ref, back_ref,
):
    step = pl.program_id(0)
    rows = received_ref.shape[0]
    parts = exchanged(info, TOP_BIG, slots_ref[:rows, :], slots_ref[rows:, :], received_ref[...])
    grads = [jnp.concatenate([ref[...], part], axis=0) for ref, part in zip((own_ref, other_ref), parts)]
    normed = normed_ref[...]
    for h in range(2):
        put_pieces(info, keep_ref, send_ref, (h, step), dot_tn(normed, grads[h]), 0)
    other = joined_pieces(info, mine_ref[...], theirs_ref[...], 0)
    total = dot_nt(grads[0], w_own_ref[...]) + dot_nt(grads[1], other)

    @pl.when(step == 0)
    def _():
        back_ref[...] = total

    @pl.when(step > 0)
    def _():
        back_ref[...] += total

    @pl.when(step == pl.num_programs(0) - 1)
    def _():
        normal, inverse = norm_stats(rows_ref[...].astype(F32))
        back, gain, shift = norm_back(back_ref[...], normal, inverse, norms_ref[0:1, :])
        g_norms_ref[0:1, :] = gain
        g_norms_ref[1:2, :] = shift
        grad_rows_ref[...] = (grad_hidden_ref[...] + back).astype(BF16)


def first_back(info, own, other, slots, received, rows, normed, grad_hidden, norms, w_self, mine, theirs):
    count, half = own.shape[0], own.shape[2]
    width = rows.shape[1]
    ins = [(a, lead_spec(*a.shape[1:])) for a in (own, other, slots, received)]
    ins += [whole_in(a) for a in (rows, normed, grad_hidden, norms)]
    ins += [(a, lead_spec(*a.shape[1:])) for a in (w_self, mine, theirs)]
    pieces = whole_out(2, count, half, half)
    return call(
        first_back_kernel,
        info,
        count,
        ins,
        [whole_out(*rows.shape), pieces, pieces, whole_out(2, width, kind=F32)],
        [pltpu.VMEM(rows.shape, F32)],
        "first_back",
        32,
        11,
    )


def row_of(table, index):
    return lax.dynamic_index_in_dim(table, index, 0, keepdims=False)


def scalars(clip_len, index, across, quarter):
    core = index % 2
    is_big = index < 2 * quarter
    is_mid = jnp.logical_and(index >= 2 * quarter, index < 3 * quarter)
    first, last = core == 0, core == 1
    flags = [
        is_big,
        core,
        across,
        jnp.logical_and(is_big, index >= quarter),
        jnp.logical_and(is_big, last),
        jnp.logical_and(is_big, first),
        jnp.logical_and(is_mid, last),
        jnp.logical_and(is_mid, first),
    ]
    shared = index - core + across
    lens_a, lens_b = row_of(clip_len, across), clip_len[2]
    big_a = row_of(lens_a, jnp.minimum(index, 2 * quarter - 1))
    big_b = row_of(lens_b, jnp.minimum(shared, 2 * quarter - 1))
    sets_a = [row_of(lens_a, index % quarter + s * quarter) for s in range(2)]
    sets_b = [row_of(lens_b, shared % quarter + core * quarter)] * 2
    table = jnp.stack(
        [2 * big_a, 2 * big_a, *sets_a, 2 * big_b, 2 * big_b, *sets_b]
        + [big_a, 2 * big_a, *sets_a, big_b, 2 * big_b, *sets_b]
    )
    ends = [table[:, 0]]
    for k in range(1, 4):
        ends.append(ends[-1] + table[:, k])
    flags = jnp.stack([flag.astype(jnp.int32) for flag in flags])
    return jnp.concatenate([flags, jnp.stack(ends, axis=1).reshape(-1)])


def local(
    tokens,
    cotangent,
    clip_len,
    ln_params,
    w_self,
    w_self_out,
    w_offer,
    w_query,
    w_cross_out,
    w_up,
    w_down,
):
    index = lax.axis_index("clip")
    across = lax.axis_index("head")
    count = lax.axis_size("clip")
    quarter = count // 4
    levels = (2 * quarter).bit_length() - 1
    core = index % 2
    is_big = index < 2 * quarter
    is_mid = jnp.logical_and(index >= 2 * quarter, index < 3 * quarter)
    own_micro2 = core == across
    norms = ln_params[0]
    w_self, w_self_out, w_offer, w_query = w_self[0], w_self_out[0], w_offer[0], w_query[0]
    w_cross_out, w_up, w_down = w_cross_out[0], w_up[0], w_down[0]
    half = w_query.shape[1]
    part_a = tokens.shape[1]
    part_b = part_a // 2
    wide = 2 * half

    near = [(i, i - quarter) for i in range(2 * quarter, count)]
    far = [(i, i - 2 * quarter) for i in range(2 * quarter, 3 * quarter)]
    far += [(i, i - quarter) for i in range(3 * quarter, count)]

    def to_server(far_rows, near_rows):
        second = lax.ppermute(near_rows, "clip", near)
        return lax.ppermute(far_rows, "clip", far), second

    def to_reader(far_rows, near_rows):
        second = lax.ppermute(near_rows, "clip", [(b, a) for a, b in near])
        return lax.ppermute(far_rows, "clip", [(b, a) for a, b in far]), second

    def reader_slots(left, right, received):
        top = jnp.where(jnp.logical_and(is_mid, core == 1), received, left)
        return top, jnp.where(jnp.logical_and(is_mid, core == 0), received, right)

    def from_server(top, bottom):
        return top, bottom, other_core(jnp.where(core == 0, bottom, top))

    def over_level(part, bit):
        return over_bit(part, bit, 2 * quarter if bit == levels - 1 else None)

    def add(left, right):
        return (left.astype(F32) + right.astype(F32)).astype(BF16)

    def view_sum(total, received):
        total = add(total, received)
        for bit in range(2, levels):
            total = add(total, over_level(total, bit))
        return total

    def all_rows(mine, theirs):
        a_mine, b_mine = mine[:part_a], mine[part_a:]
        a_theirs, b_theirs = theirs[:part_a], theirs[part_a:]
        kept = jnp.where(own_micro2, b_mine, b_theirs)
        received = other_core(jnp.where(own_micro2, b_theirs, b_mine))
        micro2 = in_core_order(core, kept, received, 0)
        micro0 = jnp.where(across == 0, a_mine, a_theirs)
        micro1 = jnp.where(across == 0, a_theirs, a_mine)
        return jnp.stack([micro0, micro1, micro2])


    def over_head_rows(array, start, stop, *others):
        return over_head(after(array[start:stop], *others) if others else array[start:stop])

    self_mine = over_head(core_piece(w_self, core, 1))
    tokens_received = other_core(core_piece(tokens[2], 1 - core, 0))
    info = scalars(clip_len, index, across, quarter)
    rows, normed, qkv_own = first_project(info, tokens, tokens_received, norms, w_self)
    self_0 = [halves_of(qkv_own, n) for n in range(3)]
    mix_0, p_0 = attend(info, SELF_A, self_0, half)
    first_piece = jnp.stack([core_piece(w_self_out, core, 1), core_piece(w_query, core, 0)])
    offer_piece, up_piece, down_piece = core_piece(w_offer, core, 1), core_piece(w_up, core, 1), core_piece(w_down, core, 0)
    cross_piece = core_piece(w_cross_out, core, 1)
    (self_mine, mix_0, first_piece) = fence(self_mine, mix_0, first_piece)

    first_mine = over_head(first_piece)
    self_theirs = other_core(self_mine)
    qkv_other, qkv_send = other_project(info, normed, qkv_own, self_mine, self_theirs, part_b)
    self_1 = [halves_of(qkv_other, n) for n in range(3)]
    mix_1, p_1 = attend(info, SELF_A, self_1, half)
    qkv_received, first_mine, mix_1, offer_piece = fence(other_core(qkv_send), first_mine, mix_1, offer_piece)

    offer_mine = over_head(offer_piece)
    self_b = [
        [column_block(qkv_own, n, 2), column_block(qkv_other, n, 2), column_block(qkv_received, n)] for n in range(3)
    ]
    mix_s, mix_send, p_s = attend(info, SELF_B, self_b, half)
    first_theirs = other_core(first_mine)
    mixes = (mix_0, mix_1, mix_s, other_core(mix_send))
    hidden, joined, q_far, q_near, q_left, q_right, q_send = second_project(
        info, rows, norms, mixes, w_self_out, w_query, first_mine, first_theirs, part_b
    )
    q_far, q_near, q_top, q_bottom, joined, offer_mine, cross_piece, up_piece, down_piece, cotangent = fence(
        q_far, q_near, *reader_slots(q_left, q_right, other_core(q_send)), joined, offer_mine, cross_piece, up_piece,
        down_piece, cotangent,
    )

    up_mine = over_head(up_piece)
    asked_a = to_server(q_far, q_near)
    asked_b = to_server(q_top, q_bottom)
    offer_theirs = other_core(offer_mine)
    offer, offer_send = offer_project(info, joined, w_offer, offer_mine, offer_theirs, part_b)
    cotangent_received = other_core(core_piece(cotangent[2], 1 - core, 0))
    offer_received = other_core(offer_send)
    *asked_a, asked_b_far, asked_b_near, offer_received, cotangent_received, up_mine, down_piece, cross_piece = fence(
        *asked_a, *asked_b, offer_received, cotangent_received, up_mine, down_piece, cross_piece
    )

    down_mine = [over_head(down_piece[:320])]
    cross_a = [[column_block(asked_a[0]), column_block(asked_a[1])]] + [halves_of(offer, n) for n in range(2)]
    far_a, near_a, cross_p_a = attend(info, CROSS_A, cross_a, wide)
    far_a, near_a, asked_b_far, asked_b_near, up_mine, down_mine[0], down_piece, cross_piece = fence(
        far_a, near_a, asked_b_far, asked_b_near, up_mine, down_mine[0], down_piece, cross_piece
    )

    back_a = to_reader(far_a, near_a)
    down_mine.append(over_head(down_piece[320:]))
    cross_mine = over_head(cross_piece)
    cross_b = [[column_block(asked_b_far), column_block(asked_b_near)]] + [
        [
            column_block(offer, n, 2),
            column_block(offer, n, 2, half // (2 * HEAD_DIM)),
            column_block(offer_received, n),
        ]
        for n in range(2)
    ]
    far_b, near_b, cross_p_b = attend(info, CROSS_B, cross_b, half)
    up_theirs = other_core(up_mine)
    *back_a, far_b, near_b, cross_mine, up_mine, up_theirs, down_mine[1] = fence(
        *back_a, far_b, near_b, cross_mine, up_mine, up_theirs, down_mine[1]
    )

    back_b = from_server(*to_reader(far_b, near_b))
    down_mine = jnp.concatenate(down_mine)
    down_theirs = other_core(down_mine)
    cross_theirs = other_core(cross_mine)
    up_pieces = jnp.stack([core_piece(w_up, core, 1), up_mine, core_piece(w_up, 1 - core, 1), up_theirs])
    down_pieces = jnp.stack([core_piece(w_down, core, 0), down_mine, core_piece(w_down, 1 - core, 0), down_theirs])

    (
        result, grad_second, gm_far, gm_near, gm_left, gm_right, gm_send,
        up_keep, up_send, down_keep, down_send, cross_keep, cross_send, norms_3,
    ) = mlp(
        info, hidden, norms, (*back_a, *back_b), w_cross_out, cross_mine, cross_theirs, cotangent, cotangent_received,
        up_pieces, down_pieces,
    )

    gm_far, gm_near, gm_top, gm_bottom, result, down_send, up_send = fence(
        gm_far, gm_near, *reader_slots(gm_left, gm_right, other_core(gm_send)), result, down_send, up_send
    )

    grad_a = to_server(gm_far, gm_near)
    grad_b = to_server(gm_top, gm_bottom)
    layer_x = over_head(result)
    down = add(down_keep, other_core(down_send))
    up = add(up_keep, other_core(up_send))
    *grad_a, grad_b_far, grad_b_near, layer_x, down, up = fence(*grad_a, *grad_b, layer_x, down, up)

    down_x = [over_head(down[1, :384])]
    grad_in = [column_block(grad_a[0]), column_block(grad_a[1])]
    dq_far, dq_near, dkv_a = attend_back(info, CROSS_A, cross_a + [grad_in], cross_p_a, wide)
    dq_far, dq_near, grad_b_far, grad_b_near, down_x[0], down, up = fence(
        dq_far, dq_near, grad_b_far, grad_b_near, down_x[0], down, up
    )

    dq_a = to_reader(dq_far, dq_near)
    down_x.append(over_head(down[1, 384:]))
    up_x = [over_head(up[1, :128])]
    grad_in = [column_block(grad_b_far), column_block(grad_b_near)]
    dq_b_far, dq_b_near, dkv_b, dkv_send = attend_back(info, CROSS_B, cross_b + [grad_in], cross_p_b, half)
    *dq_a, dq_b_far, dq_b_near, down_x[1], up_x[0], up = fence(*dq_a, dq_b_far, dq_b_near, down_x[1], up_x[0], up)

    dq_b = from_server(*to_reader(dq_b_far, dq_b_near))
    dkv_received = other_core(dkv_send)
    up_x.append(over_head(up[1, 128:448]))
    down_total = add(down[0], jnp.concatenate(down_x))
    *dq_b, dkv_received, up_x[1], down_total, up = fence(*dq_b, dkv_received, up_x[1], down_total, up)

    up_x.append(over_head(up[1, 448:]))
    down_y = over_level(down_total, 1)
    grad_hidden, grad_mix, grad_send, mid_keep, mid_send, norms_2 = second_back(
        info, (*dq_a, *dq_b), dkv_a, dkv_b, dkv_received, joined, hidden, grad_second, norms, w_offer,
        offer_mine, offer_theirs, w_query, w_self_out, first_mine, first_theirs, mixes, cross_keep, cross_send,
    )
    grad_hidden, grad_mix, grad_send, mid_keep, mid_send, up_x[2], down_y = fence(
        grad_hidden, grad_mix, grad_send, mid_keep, mid_send, up_x[2], down_y
    )

    mid = add(mid_keep, other_core(mid_send))
    grad_in = [column_block(grad_mix, 0, 2), column_block(grad_mix, 1, 2), column_block(other_core(grad_send))]
    (back_0,) = attend_back(info, SELF_A, self_0 + [halves_of(grad_mix, 0)], p_0, half)
    back_s, back_send = attend_back(info, SELF_B, self_b + [grad_in], p_s, half)
    up_total = add(up[0], jnp.concatenate(up_x))
    back_0, back_s, back_send, mid, up_total, grad_mix, down_total, down_y = fence(
        back_0, back_s, back_send, mid, up_total, grad_mix, down_total, down_y
    )

    mid_x = [over_head(mid[1, :1])]
    up_y = [over_level(up_total[:256], 1)]
    back_received = other_core(back_send)
    (back_1,) = attend_back(info, SELF_A, self_1 + [halves_of(grad_mix, 1)], p_1, half)
    back_1, back_received, mid_x[0], mid, up_y[0], up_total = fence(
        back_1, back_received, mid_x[0], mid, up_y[0], up_total
    )

    mid_x.append(over_head(mid[1, 1:3]))
    up_y.append(over_level(up_total[256:], 1))
    grad_rows, self_keep, self_send, norms_1 = first_back(
        info, back_0, back_1, back_s, back_received, rows, normed, grad_hidden, norms, w_self, self_mine, self_theirs
    )
    grad_rows, self_keep, self_send, mid_x[1], up_y[1], mid = fence(
        grad_rows, self_keep, self_send, mid_x[1], up_y[1], mid
    )
    mid_x.append(over_head(mid[1, 3:]))
    mid_total = [add(mid[0, :3], jnp.concatenate(mid_x[:2]))]
    mid_y = [over_level(mid_total[0], 1)]
    layer_out = all_rows(result, after(layer_x, grad_rows))
    norm_grads = jnp.concatenate([norms_1, norms_2, norms_3, jnp.zeros((2, wide), F32)], axis=0)
    norm_grads = norm_grads.reshape(-1, half).astype(BF16)
    norm_grads = add(norm_grads, other_core(norm_grads))
    last = add(self_keep, other_core(self_send))
    last, norm_grads, mid_x[2], mid, grad_rows = fence(last, norm_grads, mid_x[2], mid, grad_rows)

    end = jnp.concatenate([last[:, 2], jnp.stack([norm_grads, norm_grads])], axis=1)
    last_x = over_head(last[1, :2])
    mid_total.append(add(mid[0, 3:], mid_x[2]))
    mid_y.append(over_level(mid_total[1], 1))
    last_x, last, end, grad_rows = fence(last_x, last, end, grad_rows)

    end_x = over_head(end[1])
    rows_x = over_head(grad_rows)
    last_total = add(last[0, :2], last_x)
    last_y = over_level(last_total, 1)
    last_total, last_y, end_x = fence(last_total, last_y, end_x)

    end_total = add(end[0], end_x)
    end_total = view_sum(end_total, over_level(end_total, 1))
    last_total = view_sum(last_total, last_y)
    down_total = view_sum(down_total, down_y)
    up_total = view_sum(up_total, jnp.concatenate(up_y))
    mid_total = [n for total, received in zip(mid_total, mid_y) for n in view_sum(total, received)]
    norms_total = end_total[half:].reshape(-1, wide)[:6]

    def whole(mine, axis):
        return in_core_order(core, mine, other_core(mine), axis).astype(F32)[None]

    return (
        layer_out,
        all_rows(grad_rows, rows_x).astype(F32),
        norms_total.astype(F32)[None],
        whole(jnp.concatenate([last_total, end_total[None, :half]]), 1),
        whole(mid_total[3], 1),
        whole(jnp.stack(mid_total[:2]), 1),
        whole(mid_total[2], 0),
        whole(mid_total[4], 1),
        whole(up_total, 1),
        whole(down_total, 0),
    )


def solution(mesh):
    return jax.shard_map(
        local,
        mesh=mesh,
        in_specs=(
            P(None, "clip", None),
            P(None, "clip", None),
            P(),
            P("clip", None, None),
            P("clip", None, None, "head"),
            P("clip", "head", None),
            P("clip", None, None, "head"),
            P("clip", None, "head"),
            P("clip", "head", None),
            P("clip", None, "head"),
            P("clip", "head", None),
        ),
        out_specs=(
            P(None, "clip", None),
            P(None, "clip", None),
            P("clip", None, None),
            P("clip", None, None, "head"),
            P("clip", "head", None),
            P("clip", None, None, "head"),
            P("clip", None, "head"),
            P("clip", "head", None),
            P("clip", None, "head"),
            P("clip", "head", None),
        ),
        check_vma=False,
    )
```

time: 694 us -> 500 us (0.72)
  Pallas kernels: 63.3 us -> 161 us
  waiting for transfers between devices: 251 us -> 169 us
  matrix products: 75.4 us -> 0 us
  local copies, waits for them, and re-layouts: 91.6 us -> 28.3 us
  other arithmetic: 82.8 us -> 43.2 us
  starting transfers between devices: 118 us -> 87.1 us
    pallas_call x8 -> x17, Pallas kernels: 63.3 us -> 161 us  [call(): pl.pallas_call(kernel, grid_spec=pltpu.PrefetchScalarGridSpec(num_scalar_...]
    ppermute x11 -> x19, waiting for transfers between devices: 119 us -> 40.6 us  [over_head(): return lax.ppermute(value, 'head', [(0, 1), (1, 0)])]
    dot_general x21 -> x0, matrix products: 75.4 us -> none  [the longest x5 23.2 us: dot_nt(): lax.dot_general(left, right, (((1,), (1,)), ((), ())), preferred_element_...]
    ppermute x40 -> x45, starting transfers between devices: 63.9 us -> 32.6 us  [over_bit(): lax.ppermute(value, 'clip', [(i, i ^ 1 << bit) for i in range(count)])]
    unnamed x322 -> x182, local copies, waits for them, and re-layouts: 39.7 us -> 16.5 us
    dynamic_slice x25 -> x9, local copies, waits for them, and re-layouts: 18 us -> 5.9 us  [core_piece(): return lax.dynamic_slice_in_dim(value, piece * size, size, axis)]
    broadcast_in_dim x7 -> x0, other arithmetic: 11.9 us -> none  [the longest x1 2.51 us: local(): whole(up_sum, 0)[None]]
    add x13 -> x1, other arithmetic: 11.9 us -> 0.01 us  [scalars(): ends.append(ends[-1] + table[:, k])]
  transfers between devices with their start and end apart: 59 -> 80, of which waited for: 15 -> 29; matrix products, arithmetic and copies ran while one was open for 23% -> 10% of each run, Pallas kernels for 9% -> 25%
where the time goes in v2:
time: 500 us; the launch traced here: 491 us
  waiting for transfers between devices  169 us (34%)
  Pallas kernels  161 us (32%)
  starting transfers between devices  87.1 us (17%)
  other arithmetic  43.2 us (9%)
  local copies, waits for them, and re-layouts  28.3 us (6%)
    pallas_call x17, Pallas kernels, call(): pl.pallas_call(kernel, grid_spec=pltpu.PrefetchScalarGridSpec(num_scalar_...  161 us
    ppermute x45, waiting for transfers between devices, over_bit(): lax.ppermute(value, 'clip', [(i, i ^ 1 << bit) for i in range(count)])  79.3 us
    ppermute x4, waiting for transfers between devices, to_server(): return (lax.ppermute(far_rows, 'clip', far), second)  45.6 us
    ppermute x19, waiting for transfers between devices, over_head(): return lax.ppermute(value, 'head', [(0, 1), (1, 0)])  40.6 us
    ppermute x45, starting transfers between devices, over_bit(): lax.ppermute(value, 'clip', [(i, i ^ 1 << bit) for i in range(count)])  32.6 us
    ppermute x4, starting transfers between devices, to_reader(): return (lax.ppermute(far_rows, 'clip', [(b, a) for a, b in far]), second)  22.4 us
    ppermute x19, starting transfers between devices, over_head(): return lax.ppermute(value, 'head', [(0, 1), (1, 0)])  20.9 us
    unnamed x182, local copies, waits for them, and re-layouts  16.5 us
  transfers between devices with their start and end apart: 80, of which 29 were waited for; matrix products, arithmetic and copies ran while one was open for 10% of the time, Pallas kernels for 25%

profile of v2, /device:TPU:0, one launch (start us, length us, event | category | flops | bytes accessed | tf_op | source)
XLA Modules:
  0.0 491.2 jit_solution(4641843102516646843)
XLA Ops:
  3.0 2.2 dynamic-slice_bitcast_fusion
  5.2 2.5 collective-permute-start.1
  12.9 3.9 first_project.1
  16.8 7.9 %attend.5 = (bf16[512,384]{1,0:T(8,128)(2,1)S(1)}, bf16[6,512,512]{2,1,0:T(8,128)(2,1)}) custom-call(s32[72]{0:T(128)S(1)} %concatenate.132.info, bf16[3,768,384]{2,1,0:T(8,128)(2,1)S(1)} %get-tuple-element.188.refs_0_.refs_1_.refs_2_.refs_3_.refs_4_.refs_5_.own_b_ref.refs_6_, ...), custom_call_target="tpu_custom_call" | custom-call | bytes 4 | tf_op jit(solution)/shard_map/attend/pallas_call | solution.py:134
  25.5 2.8 collective-permute-done.1.mine_ref
  28.3 1.7 collective-permute-start.4
  30.9 4.2 other_project.1
  36.3 7.9 %attend.6 = (bf16[512,384]{1,0:T(8,128)(2,1)S(1)}, bf16[6,512,512]{2,1,0:T(8,128)(2,1)}) custom-call(s32[72]{0:T(128)S(1)} %concatenate.132.info, bf16[3,768,384]{2,1,0:T(8,128)(2,1)S(1)} %get-tuple-element.195.refs_0_.refs_1_.refs_2_.refs_3_.refs_4_.refs_5_.refs_7_, ...), custom_call_target="tpu_custom_call" | custom-call | bytes 4 | tf_op jit(solution)/shard_map/attend/pallas_call | solution.py:134
  44.6 8.6 %attend.7 = (bf16[512,384]{1,0:T(8,128)(2,1)S(1)}, bf16[256,384]{1,0:T(8,128)(2,1)}, bf16[6,512,512]{2,1,0:T(8,128)(2,1)}) custom-call(s32[72]{0:T(128)S(1)} %concatenate.132.info, bf16[3,768,384]{2,1,0:T(8,128)(2,1)S(1)} %get-tuple-element.188.refs_0_.refs_1_.refs_2_.refs_3_.refs_4_.refs_5_.own_b_ref.refs_6_, ...), custom_call_target="tpu_custom_call" | custom-call | bytes 4 | tf_op jit(solution)/shard_map/attend/pallas_call | solution.py:134
  54.2 1.8 collective-permute-start.8
  56.0 1.8 constant_dynamic-slice_fusion.1
  57.9 6.4 %second_project.1 = (f32[768,768]{1,0:T(8,128)S(1)}, bf16[768,768]{1,0:T(8,128)(2,1)S(1)}, bf16[256,768]{1,0:T(8,128)(2,1)S(1)}, bf16[256,768]{1,0:T(8,128)(2,1)...) custom-call(s32[72]{0:T(128)S(1)} %concatenate.132.info, ...), custom_call_target="tpu_custom_call" | custom-call | bytes 5 | tf_op jit(solution)/shard_map/second_project/pallas_call | solution.py:134
  65.9 4.2 collective-permute-done.8.mine_ref.offer_mine_ref
  70.1 1.7 collective-permute-start.16
  75.1 3.4 offer_project.1
  78.5 3.8 collective-permute-done.11.refs_0_
  84.5 18.5 %collective-permute-done.9.refs_0_ = bf16[256,768]{1,0:T(8,128)(2,1)S(1)} collective-permute-done((bf16[256,768]{1,0:T(8,128)(2,1)S(1)}, bf16[256,768]{1,0:T(8,128)(2,1)S(1)}, u32[]{:S(2)}, u32[]{:S(2)}) %collective-permute-start.9) | collective-permute-done | bytes 393248 | tf_op jit(solution)/shard_map/ppermute | solution.py:819
  103.4 8.6 %attend.8 = (bf16[256,768]{1,0:T(8,128)(2,1)S(1)}, bf16[256,768]{1,0:T(8,128)(2,1)S(1)}, bf16[12,256,512]{2,1,0:T(8,128)(2,1)}) custom-call(s32[72]{0:T(128)S(1)} %concatenate.132.info, bf16[256,768]{1,0:T(8,128)(2,1)S(1)} %collective-permute-done.9.refs_0_, bf16[256,768]{1,0:T(8,128)(2,1)S(1)} %collective-permute-done.10.refs_1_, ...), custom_call_target="tpu_custom_call" | custom-call | bytes 8 | tf_op jit(solution)/shard_map/attend/pallas_call | solution.py:134
  112.0 4.0 collective-permute-done.17
  118.5 1.8 collective-permute-start.20
  120.3 5.2 %attend.9 = (bf16[256,384]{1,0:T(8,128)(2,1)S(1)}, bf16[256,384]{1,0:T(8,128)(2,1)S(1)}, bf16[6,256,512]{2,1,0:T(8,128)(2,1)}) custom-call(s32[72]{0:T(128)S(1)} %concatenate.132.info, bf16[256,384]{1,0:T(8,128)(2,1)S(1)} %collective-permute-done.11.refs_0_, bf16[256,384]{1,0:T(8,128)(2,1)S(1)} %collective-permute-done.12.refs_1_, ...), custom_call_target="tpu_custom_call" | custom-call | bytes 4 | tf_op jit(solution)/shard_map/attend/pallas_call | solution.py:134
  125.6 14.7 %collective-permute-done.20.mine_ref = bf16[384,384]{1,0:T(8,128)(2,1)S(1)} collective-permute-done((bf16[384,384]{1,0:T(8,128)(2,1)S(1)}, bf16[384,384]{1,0:T(8,128)(2,1)S(1)}, u32[]{:S(2)}, u32[]{:S(2)}) %collective-permute-start.20) | collective-permute-done | bytes 294944 | tf_op jit(solution)/shard_map/ppermute | solution.py:24
  143.2 2.7 pad_maximum_fusion.up_ref
  147.0 2.5 pad_maximum_fusion.1.down_ref
  153.0 36.5 %mlp.1 = (bf16[768,768]{1,0:T(8,128)(2,1)S(1)}, f32[768,768]{1,0:T(8,128)}, bf16[256,768]{1,0:T(8,128)(2,1)}, bf16[256,768]{1,0:T(8,128)(2,1)S(1)}, bf16[256,384...) custom-call(s32[72]{0:T(128)S(1)} %concatenate.132.info, ...), custom_call_target="tpu_custom_call" | custom-call | bytes 34 | tf_op jit(solution)/shard_map/mlp/pallas_call | solution.py:134
  197.9 2.4 add_convert_fusion.1
  201.6 23.3 %collective-permute-done.31.refs_8_ = bf16[256,384]{1,0:T(8,128)(2,1)S(1)} collective-permute-done((bf16[256,384]{1,0:T(8,128)(2,1)S(1)}, bf16[256,384]{1,0:T(8,128)(2,1)S(1)}, u32[]{:S(2)}, u32[]{:S(2)}) %collective-permute-start.31) | collective-permute-done | bytes 196640 | tf_op jit(solution)/shard_map/ppermute | solution.py:819
  224.9 1.8 collective-permute-start.36
  226.8 9.1 %attend_back.5 = (bf16[256,768]{1,0:T(8,128)(2,1)S(1)}, bf16[256,768]{1,0:T(8,128)(2,1)S(1)}, bf16[2,512,768]{2,1,0:T(8,128)(2,1)S(1)}) custom-call(s32[72]{0:T(128)S(1)} %concatenate.132.info, bf16[256,768]{1,0:T(8,128)(2,1)S(1)} %copy-done.28, bf16[256,768]{1,0:T(8,128)(2,1)S(1)} %collective-permute-done.10.refs_1_, ...), custom_call_target="tpu_custom_call" | custom-call | bytes 12 | tf_op jit(solution)/shard_map/attend_back/pallas_call | solution.py:134
  235.9 3.4 collective-permute-done.36
  239.3 1.8 collective-permute-start.39
  241.1 7.5 %collective-permute-start.37 = (bf16[256,768]{1,0:T(8,128)(2,1)S(1)}, bf16[256,768]{1,0:T(8,128)(2,1)S(1)}, u32[]{:S(2)}, u32[]{:S(2)}) collective-permute-start(bf16[256,768]{1,0:T(8,128)(2,1)S(1)} %get-tuple-element.278), channel_id=1, source_target_pairs={{0,16},{2,18},{4,20},{6,22},{16,24},{18,26},{20,28},{22,30},{1,17}... | collective-permute-start | bytes 1179656 | tf_op jit(solution)/shard_map/ppermute | solution.py:823
  249.7 5.1 %attend_back.6 = (bf16[256,384]{1,0:T(8,128)(2,1)S(1)}, bf16[256,384]{1,0:T(8,128)(2,1)S(1)}, bf16[2,512,384]{2,1,0:T(8,128)(2,1)S(1)}, bf16[2,256,384]{2,1,0:T(8,128)(2,1)S(1)}) custom-call(s32[72]{0:T(128)S(1)} %concatenate.132.info, bf16[256,384]{1,0:T(8,128)(2,1)S(1)} %copy-done.48, bf16[256,384]{1,0:T(8,128)(2,1)S(1)} %copy-done.50, ...), custom_call_target="tpu_custom_call" | custom-call | bytes 6 | tf_op jit(solution)/shard_map/attend_back/pallas_call | solution.py:134
  254.9 2.0 collective-permute-done.40
  256.9 12.0 %collective-permute-start.41 = (bf16[256,384]{1,0:T(8,128)(2,1)S(1)}, bf16[256,384]{1,0:T(8,128)(2,1)S(1)}, u32[]{:S(2)}, u32[]{:S(2)}) collective-permute-start(bf16[256,384]{1,0:T(8,128)(2,1)S(1)} %get-tuple-element.289), channel_id=1, source_target_pairs={{0,16},{2,18},{4,20},{6,22},{16,24},{18,26},{20,28},{22,30},{1,17}... | collective-permute-start | bytes 589832 | tf_op jit(solution)/shard_map/ppermute | solution.py:823
  270.5 2.7 collective-permute-done.41.far_b_ref
  274.9 8.1 %collective-permute-done.45 = bf16[320,768]{1,0:T(8,128)(2,1)S(1)} collective-permute-done((bf16[320,768]{1,0:T(8,128)(2,1)S(1)}, bf16[320,768]{1,0:T(8,128)(2,1)S(1)}, u32[]{:S(2)}, u32[]{:S(2)}) %collective-permute-start.45) | collective-permute-done | bytes 491552 | tf_op jit(solution)/shard_map/ppermute | solution.py:24
  285.9 17.5 %second_back.1 = (f32[768,768]{1,0:T(8,128)}, bf16[2,768,384]{2,1,0:T(8,128)(2,1)S(1)}, bf16[256,384]{1,0:T(8,128)(2,1)S(1)}, bf16[2,5,384,384]{3,2,1,0:T(8,128)...) custom-call(s32[72]{0:T(128)S(1)} %concatenate.132.info, ...), custom_call_target="tpu_custom_call" | custom-call | bytes 12 | tf_op jit(solution)/shard_map/second_back/pallas_call | solution.py:134
  303.4 6.4 %collective-permute-done.47 = bf16[768,768]{1,0:T(8,128)(2,1)} collective-permute-done((bf16[768,768]{1,0:T(8,128)(2,1)S(1)}, bf16[768,768]{1,0:T(8,128)(2,1)}, u32[]{:S(2)}, u32[]{:S(2)}) %collective-permute-start.47) | collective-permute-done | bytes 1179680 | tf_op jit(solution)/shard_map/ppermute | solution.py:29
  310.3 1.9 copy-done.19
  312.2 8.0 %attend_back.7.own_ref = bf16[3,512,384]{2,1,0:T(8,128)(2,1)S(1)} custom-call(s32[72]{0:T(128)S(1)} %concatenate.132.info, bf16[3,768,384]{2,1,0:T(8,128)(2,1)S(1)} %get-tuple-element.188.refs_0_.refs_1_.refs_2_.refs_3_.refs_4_.refs_5_.own_b_ref.refs_6_, ...), custom_call_target="tpu_custom_call" | custom-call | bytes 6 | tf_op jit(solution)/shard_map/attend_back/pallas_call | solution.py:134
  321.3 8.2 %attend_back.8 = (bf16[3,512,384]{2,1,0:T(8,128)(2,1)S(1)}, bf16[3,256,384]{2,1,0:T(8,128)(2,1)S(1)}) custom-call(s32[72]{0:T(128)S(1)} %concatenate.132.info, bf16[3,768,384]{2,1,0:T(8,128)(2,1)S(1)} %get-tuple-element.188.refs_0_.refs_1_.refs_2_.refs_3_.refs_4_.refs_5_.own_b_ref.refs_6_, ...), custom_call_target="tpu_custom_call" | custom-call | bytes 6 | tf_op jit(solution)/shard_map/attend_back/pallas_call | solution.py:134
  332.0 3.0 add_convert_fusion.5
  335.0 3.7 collective-permute-start.78
  339.4 8.0 %attend_back.9.other_ref = bf16[3,512,384]{2,1,0:T(8,128)(2,1)S(1)} custom-call(s32[72]{0:T(128)S(1)} %concatenate.132.info, bf16[3,768,384]{2,1,0:T(8,128)(2,1)S(1)} %get-tuple-element.195.refs_0_.refs_1_.refs_2_.refs_3_.refs_4_.refs_5_.refs_7_, bf16[3,768,384]{2,1,0:T(8,128)(2,1)S(1)} %get-tuple-element.195.refs_0_.refs_1_.refs_2_.refs_3_.refs_4_.refs_5_.refs_7_, ...), custom_call_target="tpu_custom_call" | custom-call | bytes 6 | tf_op jit(solution)/shard_map/attend_back/pallas_call | solution.py:134
  351.6 12.1 %first_back.1 = (bf16[768,768]{1,0:T(8,128)(2,1)S(1)}, bf16[2,3,384,384]{3,2,1,0:T(8,128)(2,1)S(1)}, bf16[2,3,384,384]{3,2,1,0:T(8,128)(2,1)S(1)}, f32[2,768]{1,0:T(2,128)S(1)}) custom-call(s32[72]{0:T(128)S(1)} %concatenate.132.info, bf16[3,512,384]{2,1,0:T(8,128)(2,1)S(1)} %attend_back.7.own_ref, bf16[3,512,384]{2,1,0:T(8,128)(2,1)S(1)} %attend_back.9.other_ref, ...), custom_call_target="tpu_custom_call" | custom-call | bytes 11 | tf_op jit(solution)/shard_map/first_back/pallas_call | solution.py:134
  368.4 2.1 add_convert_fusion.4
  374.5 2.1 collective-permute-start.76
  377.7 16.5 %collective-permute-done.71 = bf16[3,384,384]{2,1,0:T(8,128)(2,1)S(1)} collective-permute-done((bf16[3,384,384]{2,1,0:T(8,128)(2,1)S(1)}, bf16[3,384,384]{2,1,0:T(8,128)(2,1)S(1)}, u32[]{:S(2)}, u32[]{:S(2)}) %collective-permute-start.71) | collective-permute-done | bytes 884768 | tf_op jit(solution)/shard_map/ppermute | solution.py:29
  394.9 2.4 collective-permute-start.72
  399.2 6.1 %collective-permute-done.76 = bf16[768,768]{1,0:T(8,128)(2,1)S(1)} collective-permute-done((bf16[768,768]{1,0:T(8,128)(2,1)S(1)}, bf16[768,768]{1,0:T(8,128)(2,1)S(1)}, u32[]{:S(2)}, u32[]{:S(2)}) %collective-permute-start.76) | collective-permute-done | bytes 1179680 | tf_op jit(solution)/shard_map/ppermute | solution.py:29
  405.7 17.5 %collective-permute-done.72 = bf16[3,384,384]{2,1,0:T(8,128)(2,1)S(1)} collective-permute-done((bf16[3,384,384]{2,1,0:T(8,128)(2,1)S(1)}, bf16[3,384,384]{2,1,0:T(8,128)(2,1)S(1)}, u32[]{:S(2)}, u32[]{:S(2)}) %collective-permute-start.72) | collective-permute-done | bytes 884768 | tf_op jit(solution)/shard_map/ppermute | solution.py:29
  428.1 12.1 %collective-permute-done.68 = bf16[2,384,384]{2,1,0:T(8,128)(2,1)S(1)} collective-permute-done((bf16[2,384,384]{2,1,0:T(8,128)(2,1)S(1)}, bf16[2,384,384]{2,1,0:T(8,128)(2,1)S(1)}, u32[]{:S(2)}, u32[]{:S(2)}) %collective-permute-start.68) | collective-permute-done | bytes 589856 | tf_op jit(solution)/shard_map/ppermute | solution.py:29
  440.3 2.2 collective-permute-start.69
  448.2 2.5 maximum_convert_fusion.2
  450.8 2.8 maximum_convert_fusion.1
  453.6 3.1 collective-permute-done.69
  457.7 3.1 collective-permute-start.66
  463.9 5.1 %collective-permute-done.64 = bf16[400,384]{1,0:T(8,128)(2,1)S(1)} collective-permute-done((bf16[400,384]{1,0:T(8,128)(2,1)S(1)}, bf16[400,384]{1,0:T(8,128)(2,1)S(1)}, u32[]{:S(2)}, u32[]{:S(2)}) %collective-permute-start.64) | collective-permute-done | bytes 307232 | tf_op jit(solution)/shard_map/ppermute | solution.py:29
  469.1 3.6 collective-permute-start.65
  472.7 3.0 collective-permute-done.66
  478.2 3.3 collective-permute-done.65
  484.7 2.6 maximum_convert_fusion
  488.7 2.0 maximum_convert_fusion.3
  (404 shorter events, 89.1 us)
Async XLA Ops:
  2.6 7.0 %collective-permute-start = (bf16[256,768]{1,0:T(8,128)(2,1)}, bf16[256,768]{1,0:T(8,128)(2,1)S(1)}, u32[]{:S(2)}, u32[]{:S(2)}) collective-permute-start(bf16[256,768]{1,0:T(8,128)(2,1)} %dynamic-slice_bitcast_fusion.3), channel_id=1, source_target_pairs={{0,2},{2,0},{4,6},{6,4},{8,10},{10,8},{12,14},{14,12},{16,18},{18,... | collective-permute-start | bytes 1179656 | tf_op jit(solution)/shard_map/ppermute | solution.py:29
  5.2 23.1 %collective-permute-start.1 = (bf16[3,384,384]{2,1,0:T(8,128)(2,1)}, bf16[3,384,384]{2,1,0:T(8,128)(2,1)}, u32[]{:S(2)}, u32[]{:S(2)}) collective-permute-start(bf16[3,384,384]{2,1,0:T(8,128)(2,1)} %dynamic-slice_bitcast_fusion), channel_id=1, source_target_pairs={{0,1},{1,0},{2,3},{3,2},{4,5},{5,4},{6,7},{7,6},{8,9},{9,8},{10,11... | collective-permute-start | bytes 2654216 | tf_op jit(solution)/shard_map/ppermute | solution.py:24
  28.3 15.8 %collective-permute-start.4 = (bf16[2,384,384]{2,1,0:T(8,128)(2,1)S(1)}, bf16[2,384,384]{2,1,0:T(8,128)(2,1)}, u32[]{:S(2)}, u32[]{:S(2)}) collective-permute-start(bf16[2,384,384]{2,1,0:T(8,128)(2,1)S(1)} %pad_maximum_fusion.4), channel_id=1, source_target_pairs={{0,1},{1,0},{2,3},{3,2},{4,5},{5,4},{6,7},{7,6},{8,9},{9,8},{10,11... | collective-permute-start | bytes 1769480 | tf_op jit(solution)/shard_map/ppermute | solution.py:24
  35.2 8.9 %collective-permute-start.3 = (bf16[3,256,384]{2,1,0:T(8,128)(2,1)S(1)}, bf16[3,256,384]{2,1,0:T(8,128)(2,1)S(1)}, u32[]{:S(2)}, u32[]{:S(2)}) collective-permute-start(bf16[3,256,384]{2,1,0:T(8,128)(2,1)S(1)} %get-tuple-element.193), channel_id=1, source_target_pairs={{0,2},{2,0},{4,6},{6,4},{8,10},{10,8},{12,14},{14,12},{16,18},{18,... | collective-permute-start | bytes 1769480 | tf_op jit(solution)/shard_map/ppermute | solution.py:29
  44.2 13.7 %collective-permute-start.6 = (bf16[2,384,384]{2,1,0:T(8,128)(2,1)}, bf16[2,384,384]{2,1,0:T(8,128)(2,1)}, u32[]{:S(2)}, u32[]{:S(2)}) collective-permute-start(bf16[2,384,384]{2,1,0:T(8,128)(2,1)} %collective-permute-done.4.mine_ref), channel_id=1, source_target_pairs={{0,2},{2,0},{4,6},{6,4},{8,10},{10,8},{12,14},{14,12},{16,18},{18,... | collective-permute-start | bytes 1769480 | tf_op jit(solution)/shard_map/ppermute | solution.py:29
  54.2 15.9 %collective-permute-start.8 = (bf16[2,384,384]{2,1,0:T(8,128)(2,1)}, bf16[2,384,384]{2,1,0:T(8,128)(2,1)S(1)}, u32[]{:S(2)}, u32[]{:S(2)}) collective-permute-start(bf16[2,384,384]{2,1,0:T(8,128)(2,1)} %dynamic-slice_bitcast_fusion.1), channel_id=1, source_target_pairs={{0,1},{1,0},{2,3},{3,2},{4,5},{5,4},{6,7},{7,6},{8,9},{9,8},{10,11... | collective-permute-start | bytes 1769480 | tf_op jit(solution)/shard_map/ppermute | solution.py:24
  70.1 32.9 %collective-permute-start.16 = (bf16[768,768]{1,0:T(8,128)(2,1)S(1)}, bf16[768,768]{1,0:T(8,128)(2,1)S(1)}, u32[]{:S(2)}, u32[]{:S(2)}) collective-permute-start(bf16[768,768]{1,0:T(8,128)(2,1)S(1)} %bitcast.163), channel_id=1, source_target_pairs={{0,1},{1,0},{2,3},{3,2},{4,5},{5,4},{6,7},{7,6},{8,9},{9,8},{10,11... | collective-permute-start | bytes 3538952 | tf_op jit(solution)/shard_map/ppermute | solution.py:24
  71.8 10.5 %collective-permute-start.11 = (bf16[256,384]{1,0:T(8,128)(2,1)S(1)}, bf16[256,384]{1,0:T(8,128)(2,1)S(1)}, u32[]{:S(2)}, u32[]{:S(2)}) collective-permute-start(bf16[256,384]{1,0:T(8,128)(2,1)S(1)} %get-tuple-element.212), channel_id=1, source_target_pairs={{16,0},{18,2},{20,4},{22,6},{24,16},{26,18},{28,20},{30,22},{17,1}... | collective-permute-start | bytes 589832 | tf_op jit(solution)/shard_map/ppermute | solution.py:819
  73.1 10.5 %collective-permute-start.12 = (bf16[256,384]{1,0:T(8,128)(2,1)S(1)}, bf16[256,384]{1,0:T(8,128)(2,1)S(1)}, u32[]{:S(2)}, u32[]{:S(2)}) collective-permute-start(bf16[256,384]{1,0:T(8,128)(2,1)S(1)} %get-tuple-element.213), channel_id=1, source_target_pairs={{16,8},{18,10},{20,12},{22,14},{24,16},{26,18},{28,20},{30,22},{17... | collective-permute-start | bytes 589832 | tf_op jit(solution)/shard_map/ppermute | solution.py:818
  73.8 9.8 %collective-permute-start.15 = (bf16[256,768]{1,0:T(8,128)(2,1)S(1)}, bf16[256,768]{1,0:T(8,128)(2,1)S(1)}, u32[]{:S(2)}, u32[]{:S(2)}) collective-permute-start(bf16[256,768]{1,0:T(8,128)(2,1)S(1)} %dynamic-slice_bitcast_fusion.2), channel_id=1, source_target_pairs={{0,2},{2,0},{4,6},{6,4},{8,10},{10,8},{12,14},{14,12},{16,18},{18,... | collective-permute-start | bytes 1179656 | tf_op jit(solution)/shard_map/ppermute | solution.py:29
  74.4 10.0 %collective-permute-start.10 = (bf16[256,768]{1,0:T(8,128)(2,1)S(1)}, bf16[256,768]{1,0:T(8,128)(2,1)S(1)}, u32[]{:S(2)}, u32[]{:S(2)}) collective-permute-start(bf16[256,768]{1,0:T(8,128)(2,1)S(1)} %get-tuple-element.211), channel_id=1, source_target_pairs={{16,8},{18,10},{20,12},{22,14},{24,16},{26,18},{28,20},{30,22},{17... | collective-permute-start | bytes 1179656 | tf_op jit(solution)/shard_map/ppermute | solution.py:818
  82.3 20.7 %collective-permute-start.9 = (bf16[256,768]{1,0:T(8,128)(2,1)S(1)}, bf16[256,768]{1,0:T(8,128)(2,1)S(1)}, u32[]{:S(2)}, u32[]{:S(2)}) collective-permute-start(bf16[256,768]{1,0:T(8,128)(2,1)S(1)} %get-tuple-element.210), channel_id=1, source_target_pairs={{16,0},{18,2},{20,4},{22,6},{24,16},{26,18},{28,20},{30,22},{17,1}... | collective-permute-start | bytes 1179656 | tf_op jit(solution)/shard_map/ppermute | solution.py:819
  83.6 19.4 %collective-permute-start.14 = (bf16[2,256,384]{2,1,0:T(8,128)(2,1)S(1)}, bf16[2,256,384]{2,1,0:T(8,128)(2,1)S(1)}, u32[]{:S(2)}, u32[]{:S(2)}) collective-permute-start(bf16[2,256,384]{2,1,0:T(8,128)(2,1)S(1)} %get-tuple-element.216), channel_id=1, source_target_pairs={{0,2},{2,0},{4,6},{6,4},{8,10},{10,8},{12,14},{14,12},{16,18},{18,... | collective-permute-start | bytes 1179656 | tf_op jit(solution)/shard_map/ppermute | solution.py:29
  103.0 12.9 %collective-permute-start.17 = (bf16[320,768]{1,0:T(8,128)(2,1)S(1)}, bf16[320,768]{1,0:T(8,128)(2,1)S(1)}, u32[]{:S(2)}, u32[]{:S(2)}) collective-permute-start(bf16[320,768]{1,0:T(8,128)(2,1)S(1)} %slice.125), channel_id=1, source_target_pairs={{0,1},{1,0},{2,3},{3,2},{4,5},{5,4},{6,7},{7,6},{8,9},{9,8},{10,11... | collective-permute-start | bytes 1474568 | tf_op jit(solution)/shard_map/ppermute | solution.py:24
  116.0 24.3 %collective-permute-start.21 = (bf16[768,768]{1,0:T(8,128)(2,1)S(1)}, bf16[768,768]{1,0:T(8,128)(2,1)S(1)}, u32[]{:S(2)}, u32[]{:S(2)}) collective-permute-start(bf16[768,768]{1,0:T(8,128)(2,1)S(1)} %collective-permute-done.16), channel_id=1, source_target_pairs={{0,2},{2,0},{4,6},{6,4},{8,10},{10,8},{12,14},{14,12},{16,18},{18,... | collective-permute-start | bytes 3538952 | tf_op jit(solution)/shard_map/ppermute | solution.py:29
  116.0 24.3 %collective-permute-start.22 = (bf16[448,768]{1,0:T(8,128)(2,1)S(1)}, bf16[448,768]{1,0:T(8,128)(2,1)S(1)}, u32[]{:S(2)}, u32[]{:S(2)}) collective-permute-start(bf16[448,768]{1,0:T(8,128)(2,1)S(1)} %slice.126), channel_id=1, source_target_pairs={{0,1},{1,0},{2,3},{3,2},{4,5},{5,4},{6,7},{7,6},{8,9},{9,8},{10,11... | collective-permute-start | bytes 2064392 | tf_op jit(solution)/shard_map/ppermute | solution.py:24
  116.4 23.9 %collective-permute-start.18 = (bf16[256,768]{1,0:T(8,128)(2,1)S(1)}, bf16[256,768]{1,0:T(8,128)(2,1)S(1)}, u32[]{:S(2)}, u32[]{:S(2)}) collective-permute-start(bf16[256,768]{1,0:T(8,128)(2,1)S(1)} %get-tuple-element.231), channel_id=1, source_target_pairs={{0,16},{2,18},{4,20},{6,22},{16,24},{18,26},{20,28},{22,30},{1,17}... | collective-permute-start | bytes 1179656 | tf_op jit(solution)/shard_map/ppermute | solution.py:823
  117.8 22.4 %collective-permute-start.19 = (bf16[256,768]{1,0:T(8,128)(2,1)S(1)}, bf16[256,768]{1,0:T(8,128)(2,1)S(1)}, u32[]{:S(2)}, u32[]{:S(2)}) collective-permute-start(bf16[256,768]{1,0:T(8,128)(2,1)S(1)} %get-tuple-element.232), channel_id=1, source_target_pairs={{8,16},{10,18},{12,20},{14,22},{16,24},{18,26},{20,28},{22,30},{9,... | collective-permute-start | bytes 1179656 | tf_op jit(solution)/shard_map/ppermute | solution.py:822
  118.5 21.7 %collective-permute-start.20 = (bf16[384,384]{1,0:T(8,128)(2,1)S(1)}, bf16[384,384]{1,0:T(8,128)(2,1)S(1)}, u32[]{:S(2)}, u32[]{:S(2)}) collective-permute-start(bf16[384,384]{1,0:T(8,128)(2,1)S(1)} %dynamic-slice_bitcast_fusion.4), channel_id=1, source_target_pairs={{0,1},{1,0},{2,3},{3,2},{4,5},{5,4},{6,7},{7,6},{8,9},{9,8},{10,11... | collective-permute-start | bytes 884744 | tf_op jit(solution)/shard_map/ppermute | solution.py:24
  140.3 6.6 %collective-permute-start.27 = (bf16[768,768]{1,0:T(8,128)(2,1)S(1)}, bf16[768,768]{1,0:T(8,128)(2,1)S(1)}, u32[]{:S(2)}, u32[]{:S(2)}) collective-permute-start(bf16[768,768]{1,0:T(8,128)(2,1)S(1)} %constant_dynamic-update-slice_fusion), channel_id=1, source_target_pairs={{0,2},{2,0},{4,6},{6,4},{8,10},{10,8},{12,14},{14,12},{16,18},{18,... | collective-permute-start | bytes 3538952 | tf_op jit(solution)/shard_map/ppermute | solution.py:29
  141.0 5.8 %collective-permute-start.23 = (bf16[256,384]{1,0:T(8,128)(2,1)S(1)}, bf16[256,384]{1,0:T(8,128)(2,1)S(1)}, u32[]{:S(2)}, u32[]{:S(2)}) collective-permute-start(bf16[256,384]{1,0:T(8,128)(2,1)S(1)} %get-tuple-element.243), channel_id=1, source_target_pairs={{0,16},{2,18},{4,20},{6,22},{16,24},{18,26},{20,28},{22,30},{1,17}... | collective-permute-start | bytes 589832 | tf_op jit(solution)/shard_map/ppermute | solution.py:823
  143.1 6.4 %collective-permute-start.26 = (bf16[384,384]{1,0:T(8,128)(2,1)S(1)}, bf16[384,384]{1,0:T(8,128)(2,1)S(1)}, u32[]{:S(2)}, u32[]{:S(2)}) collective-permute-start(bf16[384,384]{1,0:T(8,128)(2,1)S(1)} %collective-permute-done.20.mine_ref), channel_id=1, source_target_pairs={{0,2},{2,0},{4,6},{6,4},{8,10},{10,8},{12,14},{14,12},{16,18},{18,... | collective-permute-start | bytes 884744 | tf_op jit(solution)/shard_map/ppermute | solution.py:29
  192.2 8.1 %collective-permute-start.34 = (bf16[2,768,768]{2,1,0:T(8,128)(2,1)}, bf16[2,768,768]{2,1,0:T(8,128)(2,1)S(1)}, u32[]{:S(2)}, u32[]{:S(2)}) collective-permute-start(bf16[2,768,768]{2,1,0:T(8,128)(2,1)} %get-tuple-element.265), channel_id=1, source_target_pairs={{0,2},{2,0},{4,6},{6,4},{8,10},{10,8},{12,14},{14,12},{16,18},{18,... | collective-permute-start | bytes 7077896 | tf_op jit(solution)/shard_map/ppermute | solution.py:29
  192.4 32.5 %collective-permute-start.33 = (bf16[768,768]{1,0:T(8,128)(2,1)S(1)}, bf16[768,768]{1,0:T(8,128)(2,1)S(1)}, u32[]{:S(2)}, u32[]{:S(2)}) collective-permute-start(bf16[768,768]{1,0:T(8,128)(2,1)S(1)} %get-tuple-element.259), channel_id=1, source_target_pairs={{0,1},{1,0},{2,3},{3,2},{4,5},{5,4},{6,7},{7,6},{8,9},{9,8},{10,11... | collective-permute-start | bytes 3538952 | tf_op jit(solution)/shard_map/ppermute | solution.py:24
  192.7 32.2 %collective-permute-start.29 = (bf16[256,768]{1,0:T(8,128)(2,1)}, bf16[256,768]{1,0:T(8,128)(2,1)S(1)}, u32[]{:S(2)}, u32[]{:S(2)}) collective-permute-start(bf16[256,768]{1,0:T(8,128)(2,1)} %get-tuple-element.260), channel_id=1, source_target_pairs={{16,0},{18,2},{20,4},{22,6},{24,16},{26,18},{28,20},{30,22},{17,1}... | collective-permute-start | bytes 1179656 | tf_op jit(solution)/shard_map/ppermute | solution.py:819
  194.0 30.9 %collective-permute-start.30 = (bf16[256,768]{1,0:T(8,128)(2,1)}, bf16[256,768]{1,0:T(8,128)(2,1)S(1)}, u32[]{:S(2)}, u32[]{:S(2)}) collective-permute-start(bf16[256,768]{1,0:T(8,128)(2,1)} %copy-done.67), channel_id=1, source_target_pairs={{16,8},{18,10},{20,12},{22,14},{24,16},{26,18},{28,20},{30,22},{17... | collective-permute-start | bytes 1179656 | tf_op jit(solution)/shard_map/ppermute | solution.py:818
  196.6 28.3 %collective-permute-start.31 = (bf16[256,384]{1,0:T(8,128)(2,1)S(1)}, bf16[256,384]{1,0:T(8,128)(2,1)S(1)}, u32[]{:S(2)}, u32[]{:S(2)}) collective-permute-start(bf16[256,384]{1,0:T(8,128)(2,1)S(1)} %get-tuple-element.262), channel_id=1, source_target_pairs={{16,0},{18,2},{20,4},{22,6},{24,16},{26,18},{28,20},{30,22},{17,1}... | collective-permute-start | bytes 589832 | tf_op jit(solution)/shard_map/ppermute | solution.py:819
  200.3 24.5 %collective-permute-start.32 = (bf16[256,384]{1,0:T(8,128)(2,1)S(1)}, bf16[256,384]{1,0:T(8,128)(2,1)S(1)}, u32[]{:S(2)}, u32[]{:S(2)}) collective-permute-start(bf16[256,384]{1,0:T(8,128)(2,1)S(1)} %get-tuple-element.263), channel_id=1, source_target_pairs={{16,8},{18,10},{20,12},{22,14},{24,16},{26,18},{28,20},{30,22},{17... | collective-permute-start | bytes 589832 | tf_op jit(solution)/shard_map/ppermute | solution.py:818
  224.9 14.3 %collective-permute-start.36 = (bf16[384,768]{1,0:T(8,128)(2,1)S(1)}, bf16[384,768]{1,0:T(8,128)(2,1)S(1)}, u32[]{:S(2)}, u32[]{:S(2)}) collective-permute-start(bf16[384,768]{1,0:T(8,128)(2,1)S(1)} %slice_bitcast_fusion.5), channel_id=1, source_target_pairs={{0,1},{1,0},{2,3},{3,2},{4,5},{5,4},{6,7},{7,6},{8,9},{9,8},{10,11... | collective-permute-start | bytes 1769480 | tf_op jit(solution)/shard_map/ppermute | solution.py:24
  239.3 17.6 %collective-permute-start.39 = (bf16[384,768]{1,0:T(8,128)(2,1)S(1)}, bf16[384,768]{1,0:T(8,128)(2,1)S(1)}, u32[]{:S(2)}, u32[]{:S(2)}) collective-permute-start(bf16[384,768]{1,0:T(8,128)(2,1)S(1)} %slice_bitcast_fusion.4), channel_id=1, source_target_pairs={{0,1},{1,0},{2,3},{3,2},{4,5},{5,4},{6,7},{7,6},{8,9},{9,8},{10,11... | collective-permute-start | bytes 1769480 | tf_op jit(solution)/shard_map/ppermute | solution.py:24
  241.1 15.8 %collective-permute-start.37 = (bf16[256,768]{1,0:T(8,128)(2,1)S(1)}, bf16[256,768]{1,0:T(8,128)(2,1)S(1)}, u32[]{:S(2)}, u32[]{:S(2)}) collective-permute-start(bf16[256,768]{1,0:T(8,128)(2,1)S(1)} %get-tuple-element.278), channel_id=1, source_target_pairs={{0,16},{2,18},{4,20},{6,22},{16,24},{18,26},{20,28},{22,30},{1,17}... | collective-permute-start | bytes 1179656 | tf_op jit(solution)/shard_map/ppermute | solution.py:823
  248.6 8.2 %collective-permute-start.38 = (bf16[256,768]{1,0:T(8,128)(2,1)S(1)}, bf16[256,768]{1,0:T(8,128)(2,1)S(1)}, u32[]{:S(2)}, u32[]{:S(2)}) collective-permute-start(bf16[256,768]{1,0:T(8,128)(2,1)S(1)} %get-tuple-element.279), channel_id=1, source_target_pairs={{8,16},{10,18},{12,20},{14,22},{16,24},{18,26},{20,28},{22,30},{9,... | collective-permute-start | bytes 1179656 | tf_op jit(solution)/shard_map/ppermute | solution.py:822
  249.3 7.5 %collective-permute-start.40 = (bf16[128,768]{1,0:T(8,128)(2,1)S(1)}, bf16[128,768]{1,0:T(8,128)(2,1)S(1)}, u32[]{:S(2)}, u32[]{:S(2)}) collective-permute-start(bf16[128,768]{1,0:T(8,128)(2,1)S(1)} %slice_bitcast_fusion.14), channel_id=1, source_target_pairs={{0,1},{1,0},{2,3},{3,2},{4,5},{5,4},{6,7},{7,6},{8,9},{9,8},{10,11... | collective-permute-start | bytes 589832 | tf_op jit(solution)/shard_map/ppermute | solution.py:24
  254.8 18.9 %collective-permute-start.44 = (bf16[2,256,384]{2,1,0:T(8,128)(2,1)S(1)}, bf16[2,256,384]{2,1,0:T(8,128)(2,1)S(1)}, u32[]{:S(2)}, u32[]{:S(2)}) collective-permute-start(bf16[2,256,384]{2,1,0:T(8,128)(2,1)S(1)} %get-tuple-element.291), channel_id=1, source_target_pairs={{0,2},{2,0},{4,6},{6,4},{8,10},{10,8},{12,14},{14,12},{16,18},{18,... | collective-permute-start | bytes 1179656 | tf_op jit(solution)/shard_map/ppermute | solution.py:29
  256.9 16.4 %collective-permute-start.41 = (bf16[256,384]{1,0:T(8,128)(2,1)S(1)}, bf16[256,384]{1,0:T(8,128)(2,1)S(1)}, u32[]{:S(2)}, u32[]{:S(2)}) collective-permute-start(bf16[256,384]{1,0:T(8,128)(2,1)S(1)} %get-tuple-element.289), channel_id=1, source_target_pairs={{0,16},{2,18},{4,20},{6,22},{16,24},{18,26},{20,28},{22,30},{1,17}... | collective-permute-start | bytes 589832 | tf_op jit(solution)/shard_map/ppermute | solution.py:823
  270.0 12.9 %collective-permute-start.45 = (bf16[320,768]{1,0:T(8,128)(2,1)S(1)}, bf16[320,768]{1,0:T(8,128)(2,1)S(1)}, u32[]{:S(2)}, u32[]{:S(2)}) collective-permute-start(bf16[320,768]{1,0:T(8,128)(2,1)S(1)} %slice_bitcast_fusion.7), channel_id=1, source_target_pairs={{0,1},{1,0},{2,3},{3,2},{4,5},{5,4},{6,7},{7,6},{8,9},{9,8},{10,11... | collective-permute-start | bytes 1474568 | tf_op jit(solution)/shard_map/ppermute | solution.py:24
  282.9 26.8 %collective-permute-start.47 = (bf16[768,768]{1,0:T(8,128)(2,1)S(1)}, bf16[768,768]{1,0:T(8,128)(2,1)}, u32[]{:S(2)}, u32[]{:S(2)}) collective-permute-start(bf16[768,768]{1,0:T(8,128)(2,1)S(1)} %fusion.1), channel_id=1, source_target_pairs={{0,4},{2,6},{4,0},{6,2},{8,12},{10,14},{12,8},{14,10},{16,20},{18,... | collective-permute-start | bytes 3538952 | tf_op jit(solution)/shard_map/ppermute | solution.py:29
  285.3 18.1 %collective-permute-start.46 = (bf16[320,768]{1,0:T(8,128)(2,1)}, bf16[320,768]{1,0:T(8,128)(2,1)S(1)}, u32[]{:S(2)}, u32[]{:S(2)}) collective-permute-start(bf16[320,768]{1,0:T(8,128)(2,1)} %slice_bitcast_fusion.6), channel_id=1, source_target_pairs={{0,1},{1,0},{2,3},{3,2},{4,5},{5,4},{6,7},{7,6},{8,9},{9,8},{10,11... | collective-permute-start | bytes 1474568 | tf_op jit(solution)/shard_map/ppermute | solution.py:24
  309.8 19.7 %collective-permute-start.49 = (bf16[2,5,384,384]{3,2,1,0:T(8,128)(2,1)}, bf16[2,5,384,384]{3,2,1,0:T(8,128)(2,1)S(1)}, u32[]{:S(2)}, u32[]{:S(2)}) collective-permute-start(bf16[2,5,384,384]{3,2,1,0:T(8,128)(2,1)} %get-tuple-element.318), channel_id=1, source_target_pairs={{0,2},{2,0},{4,6},{6,4},{8,10},{10,8},{12,14},{14,12},{16,18},{18,... | collective-permute-start | bytes 8847368 | tf_op jit(solution)/shard_map/ppermute | solution.py:29
  309.8 10.7 %collective-permute-start.48 = (bf16[256,384]{1,0:T(8,128)(2,1)S(1)}, bf16[256,384]{1,0:T(8,128)(2,1)S(1)}, u32[]{:S(2)}, u32[]{:S(2)}) collective-permute-start(bf16[256,384]{1,0:T(8,128)(2,1)S(1)} %get-tuple-element.313), channel_id=1, source_target_pairs={{0,2},{2,0},{4,6},{6,4},{8,10},{10,8},{12,14},{14,12},{16,18},{18,... | collective-permute-start | bytes 589832 | tf_op jit(solution)/shard_map/ppermute | solution.py:29
  330.4 17.2 %collective-permute-start.52 = (bf16[256,768]{1,0:T(8,128)(2,1)S(1)}, bf16[256,768]{1,0:T(8,128)(2,1)S(1)}, u32[]{:S(2)}, u32[]{:S(2)}) collective-permute-start(bf16[256,768]{1,0:T(8,128)(2,1)S(1)} %slice.136), channel_id=1, source_target_pairs={{0,4},{2,6},{4,0},{6,2},{8,12},{10,14},{12,8},{14,10},{16,20},{18,... | collective-permute-start | bytes 1179656 | tf_op jit(solution)/shard_map/ppermute | solution.py:29
  332.0 15.6 %collective-permute-start.50 = (bf16[3,256,384]{2,1,0:T(8,128)(2,1)S(1)}, bf16[3,256,384]{2,1,0:T(8,128)(2,1)S(1)}, u32[]{:S(2)}, u32[]{:S(2)}) collective-permute-start(bf16[3,256,384]{2,1,0:T(8,128)(2,1)S(1)} %get-tuple-element.326), channel_id=1, source_target_pairs={{0,2},{2,0},{4,6},{6,4},{8,10},{10,8},{12,14},{14,12},{16,18},{18,... | collective-permute-start | bytes 1769480 | tf_op jit(solution)/shard_map/ppermute | solution.py:29
  335.0 33.4 %collective-permute-start.78 = (bf16[768,768]{1,0:T(8,128)(2,1)}, bf16[768,768]{1,0:T(8,128)(2,1)}, u32[]{:S(2)}, u32[]{:S(2)}) collective-permute-start(bf16[768,768]{1,0:T(8,128)(2,1)} %add_convert_fusion.5), channel_id=1, source_target_pairs={{0,8},{2,10},{4,12},{6,14},{8,0},{10,2},{12,4},{14,6},{1,9},{3,11}... | collective-permute-start | bytes 3538952 | tf_op jit(solution)/shard_map/ppermute | solution.py:29
  338.7 8.8 %collective-permute-start.51 = (bf16[1,384,384]{2,1,0:T(8,128)(2,1)S(1)}, bf16[1,384,384]{2,1,0:T(8,128)(2,1)S(1)}, u32[]{:S(2)}, u32[]{:S(2)}) collective-permute-start(bf16[1,384,384]{2,1,0:T(8,128)(2,1)S(1)} %slice_bitcast_fusion.13), channel_id=1, source_target_pairs={{0,1},{1,0},{2,3},{3,2},{4,5},{5,4},{6,7},{7,6},{8,9},{9,8},{10,11... | collective-permute-start | bytes 884744 | tf_op jit(solution)/shard_map/ppermute | solution.py:24
  348.5 22.2 %collective-permute-start.54 = (bf16[512,768]{1,0:T(8,128)(2,1)}, bf16[512,768]{1,0:T(8,128)(2,1)}, u32[]{:S(2)}, u32[]{:S(2)}) collective-permute-start(bf16[512,768]{1,0:T(8,128)(2,1)} %slice.138), channel_id=1, source_target_pairs={{0,4},{2,6},{4,0},{6,2},{8,12},{10,14},{12,8},{14,10},{16,20},{18,... | collective-permute-start | bytes 2359304 | tf_op jit(solution)/shard_map/ppermute | solution.py:29
  350.0 20.7 %collective-permute-start.53 = (bf16[2,384,384]{2,1,0:T(8,128)(2,1)S(1)}, bf16[2,384,384]{2,1,0:T(8,128)(2,1)}, u32[]{:S(2)}, u32[]{:S(2)}) collective-permute-start(bf16[2,384,384]{2,1,0:T(8,128)(2,1)S(1)} %slice_bitcast_fusion.3), channel_id=1, source_target_pairs={{0,1},{1,0},{2,3},{3,2},{4,5},{5,4},{6,7},{7,6},{8,9},{9,8},{10,11... | collective-permute-start | bytes 1769480 | tf_op jit(solution)/shard_map/ppermute | solution.py:24
  370.5 75.9 %collective-permute-start.79 = (bf16[768,768]{1,0:T(8,128)(2,1)S(1)}, bf16[768,768]{1,0:T(8,128)(2,1)S(1)}, u32[]{:S(2)}, u32[]{:S(2)}) collective-permute-start(bf16[768,768]{1,0:T(8,128)(2,1)S(1)} %add_convert_fusion.4), channel_id=1, source_target_pairs={{0,2},{2,0},{4,6},{6,4},{8,10},{10,8},{12,14},{14,12},{16,18},{18,... | collective-permute-start | bytes 3538952 | tf_op jit(solution)/shard_map/ppermute | solution.py:29
  372.4 21.8 %collective-permute-start.71 = (bf16[3,384,384]{2,1,0:T(8,128)(2,1)S(1)}, bf16[3,384,384]{2,1,0:T(8,128)(2,1)S(1)}, u32[]{:S(2)}, u32[]{:S(2)}) collective-permute-start(bf16[3,384,384]{2,1,0:T(8,128)(2,1)S(1)} %fusion.2), channel_id=1, source_target_pairs={{0,4},{2,6},{4,0},{6,2},{8,12},{10,14},{12,8},{14,10},{16,20},{18,... | collective-permute-start | bytes 2654216 | tf_op jit(solution)/shard_map/ppermute | solution.py:29
  374.5 30.7 %collective-permute-start.76 = (bf16[768,768]{1,0:T(8,128)(2,1)S(1)}, bf16[768,768]{1,0:T(8,128)(2,1)S(1)}, u32[]{:S(2)}, u32[]{:S(2)}) collective-permute-start(bf16[768,768]{1,0:T(8,128)(2,1)S(1)} %add_convert_fusion.7), channel_id=1, source_target_pairs={{0,8},{2,10},{4,12},{6,14},{8,0},{10,2},{12,4},{14,6},{1,9},{3,11}... | collective-permute-start | bytes 3538952 | tf_op jit(solution)/shard_map/ppermute | solution.py:29
  376.7 47.0 %collective-permute-start.56 = (bf16[2,3,384,384]{3,2,1,0:T(8,128)(2,1)S(1)}, bf16[2,3,384,384]{3,2,1,0:T(8,128)(2,1)S(1)}, u32[]{:S(2)}, u32[]{:S(2)}) collective-permute-start(bf16[2,3,384,384]{3,2,1,0:T(8,128)(2,1)S(1)} %copy-done.66), channel_id=1, source_target_pairs={{0,2},{2,0},{4,6},{6,4},{8,10},{10,8},{12,14},{14,12},{16,18},{18,... | collective-permute-start | bytes 5308424 | tf_op jit(solution)/shard_map/ppermute | solution.py:29
  377.1 17.8 %collective-permute-start.55 = (bf16[256,768]{1,0:T(8,128)(2,1)S(1)}, bf16[256,768]{1,0:T(8,128)(2,1)S(1)}, u32[]{:S(2)}, u32[]{:S(2)}) collective-permute-start(bf16[256,768]{1,0:T(8,128)(2,1)S(1)} %broadcast_select_fusion.2), channel_id=1, source_target_pairs={{0,2},{2,0},{4,6},{6,4},{8,10},{10,8},{12,14},{14,12},{16,18},{18,... | collective-permute-start | bytes 1179656 | tf_op jit(solution)/shard_map/ppermute | solution.py:29
  394.1 30.5 %collective-permute-start.58 = (bf16[2,384,384]{2,1,0:T(8,128)(2,1)S(1)}, bf16[2,384,384]{2,1,0:T(8,128)(2,1)S(1)}, u32[]{:S(2)}, u32[]{:S(2)}) collective-permute-start(bf16[2,384,384]{2,1,0:T(8,128)(2,1)S(1)} %slice_bitcast_fusion.2), channel_id=1, source_target_pairs={{0,1},{1,0},{2,3},{3,2},{4,5},{5,4},{6,7},{7,6},{8,9},{9,8},{10,11... | collective-permute-start | bytes 1769480 | tf_op jit(solution)/shard_map/ppermute | solution.py:24
  394.9 28.3 %collective-permute-start.72 = (bf16[3,384,384]{2,1,0:T(8,128)(2,1)S(1)}, bf16[3,384,384]{2,1,0:T(8,128)(2,1)S(1)}, u32[]{:S(2)}, u32[]{:S(2)}) collective-permute-start(bf16[3,384,384]{2,1,0:T(8,128)(2,1)S(1)} %add_convert_fusion.9), channel_id=1, source_target_pairs={{0,8},{2,10},{4,12},{6,14},{8,0},{10,2},{12,4},{14,6},{1,9},{3,11}... | collective-permute-start | bytes 2654216 | tf_op jit(solution)/shard_map/ppermute | solution.py:29
  405.6 42.3 %collective-permute-start.77 = (bf16[768,768]{1,0:T(8,128)(2,1)S(1)}, bf16[768,768]{1,0:T(8,128)(2,1)S(1)}, u32[]{:S(2)}, u32[]{:S(2)}) collective-permute-start(bf16[768,768]{1,0:T(8,128)(2,1)S(1)} %add_convert_fusion.6), channel_id=1, source_target_pairs={{0,2},{2,0},{4,6},{6,4},{8,10},{10,8},{12,14},{14,12},{16,18},{18,... | collective-permute-start | bytes 3538952 | tf_op jit(solution)/shard_map/ppermute | solution.py:29
  423.7 20.5 %collective-permute-start.73 = (bf16[2,384,384]{2,1,0:T(8,128)(2,1)S(1)}, bf16[2,384,384]{2,1,0:T(8,128)(2,1)S(1)}, u32[]{:S(2)}, u32[]{:S(2)}) collective-permute-start(bf16[2,384,384]{2,1,0:T(8,128)(2,1)S(1)} %stack.168), channel_id=1, source_target_pairs={{0,2},{2,0},{4,6},{6,4},{8,10},{10,8},{12,14},{14,12},{16,18},{18,... | collective-permute-start | bytes 1769480 | tf_op jit(solution)/shard_map/ppermute | solution.py:29
  424.8 15.4 %collective-permute-start.68 = (bf16[2,384,384]{2,1,0:T(8,128)(2,1)S(1)}, bf16[2,384,384]{2,1,0:T(8,128)(2,1)S(1)}, u32[]{:S(2)}, u32[]{:S(2)}) collective-permute-start(bf16[2,384,384]{2,1,0:T(8,128)(2,1)S(1)} %fusion.3), channel_id=1, source_target_pairs={{0,4},{2,6},{4,0},{6,2},{8,12},{10,14},{12,8},{14,10},{16,20},{18,... | collective-permute-start | bytes 1769480 | tf_op jit(solution)/shard_map/ppermute | solution.py:29
  426.4 16.2 %collective-permute-start.59 = (bf16[2,384,384]{2,1,0:T(8,128)(2,1)S(1)}, bf16[2,384,384]{2,1,0:T(8,128)(2,1)S(1)}, u32[]{:S(2)}, u32[]{:S(2)}) collective-permute-start(bf16[2,384,384]{2,1,0:T(8,128)(2,1)S(1)} %slice_bitcast_fusion.1), channel_id=1, source_target_pairs={{0,1},{1,0},{2,3},{3,2},{4,5},{5,4},{6,7},{7,6},{8,9},{9,8},{10,11... | collective-permute-start | bytes 1769480 | tf_op jit(solution)/shard_map/ppermute | solution.py:24
  440.3 16.4 %collective-permute-start.69 = (bf16[2,384,384]{2,1,0:T(8,128)(2,1)S(1)}, bf16[2,384,384]{2,1,0:T(8,128)(2,1)S(1)}, u32[]{:S(2)}, u32[]{:S(2)}) collective-permute-start(bf16[2,384,384]{2,1,0:T(8,128)(2,1)S(1)} %add_convert_fusion.11), channel_id=1, source_target_pairs={{0,8},{2,10},{4,12},{6,14},{8,0},{10,2},{12,4},{14,6},{1,9},{3,11}... | collective-permute-start | bytes 1769480 | tf_op jit(solution)/shard_map/ppermute | solution.py:29
  442.7 14.8 %collective-permute-start.62 = (bf16[2,384,384]{2,1,0:T(8,128)(2,1)S(1)}, bf16[2,384,384]{2,1,0:T(8,128)(2,1)S(1)}, u32[]{:S(2)}, u32[]{:S(2)}) collective-permute-start(bf16[2,384,384]{2,1,0:T(8,128)(2,1)S(1)} %fusion.4), channel_id=1, source_target_pairs={{0,4},{2,6},{4,0},{6,2},{8,12},{10,14},{12,8},{14,10},{16,20},{18,... | collective-permute-start | bytes 1769480 | tf_op jit(solution)/shard_map/ppermute | solution.py:29
  444.1 13.4 %collective-permute-start.63 = (bf16[400,384]{1,0:T(8,128)(2,1)S(1)}, bf16[400,384]{1,0:T(8,128)(2,1)S(1)}, u32[]{:S(2)}, u32[]{:S(2)}) collective-permute-start(bf16[400,384]{1,0:T(8,128)(2,1)S(1)} %slice_bitcast_fusion.8), channel_id=1, source_target_pairs={{0,1},{1,0},{2,3},{3,2},{4,5},{5,4},{6,7},{7,6},{8,9},{9,8},{10,11... | collective-permute-start | bytes 921608 | tf_op jit(solution)/shard_map/ppermute | solution.py:24
  446.4 30.9 %collective-permute-start.60 = (bf16[768,768]{1,0:T(8,128)(2,1)S(1)}, bf16[768,768]{1,0:T(8,128)(2,1)S(1)}, u32[]{:S(2)}, u32[]{:S(2)}) collective-permute-start(bf16[768,768]{1,0:T(8,128)(2,1)S(1)} %get-tuple-element.349), channel_id=1, source_target_pairs={{0,1},{1,0},{2,3},{3,2},{4,5},{5,4},{6,7},{7,6},{8,9},{9,8},{10,11... | collective-permute-start | bytes 3538952 | tf_op jit(solution)/shard_map/ppermute | solution.py:24
  457.7 18.1 %collective-permute-start.66 = (bf16[2,384,384]{2,1,0:T(8,128)(2,1)S(1)}, bf16[2,384,384]{2,1,0:T(8,128)(2,1)S(1)}, u32[]{:S(2)}, u32[]{:S(2)}) collective-permute-start(bf16[2,384,384]{2,1,0:T(8,128)(2,1)S(1)} %add_convert_fusion.13), channel_id=1, source_target_pairs={{0,8},{2,10},{4,12},{6,14},{8,0},{10,2},{12,4},{14,6},{1,9},{3,11}... | collective-permute-start | bytes 1769480 | tf_op jit(solution)/shard_map/ppermute | solution.py:29
  460.9 8.1 %collective-permute-start.64 = (bf16[400,384]{1,0:T(8,128)(2,1)S(1)}, bf16[400,384]{1,0:T(8,128)(2,1)S(1)}, u32[]{:S(2)}, u32[]{:S(2)}) collective-permute-start(bf16[400,384]{1,0:T(8,128)(2,1)S(1)} %fusion.5), channel_id=1, source_target_pairs={{0,4},{2,6},{4,0},{6,2},{8,12},{10,14},{12,8},{14,10},{16,20},{18,... | collective-permute-start | bytes 921608 | tf_op jit(solution)/shard_map/ppermute | solution.py:29
  469.1 12.4 %collective-permute-start.65 = (bf16[400,384]{1,0:T(8,128)(2,1)S(1)}, bf16[400,384]{1,0:T(8,128)(2,1)S(1)}, u32[]{:S(2)}, u32[]{:S(2)}) collective-permute-start(bf16[400,384]{1,0:T(8,128)(2,1)S(1)} %add_convert_fusion.15), channel_id=1, source_target_pairs={{0,8},{2,10},{4,12},{6,14},{8,0},{10,2},{12,4},{14,6},{1,9},{3,11}... | collective-permute-start | bytes 921608 | tf_op jit(solution)/shard_map/ppermute | solution.py:29
  (109 other events, 762.3 us)

commit v3 on v2

--- a/solution.py
+++ b/solution.py
@@ -335,7 +335,7 @@
         outs + [p_out],
         [pltpu.VMEM((p_rows, 2 * rows), F32)],
         "attend",
-        14,
+        10,
         heads * 2 // 3,
     )
 
@@ -361,7 +361,7 @@
         outs,
         [],
         "attend_back",
-        14,
+        11,
         probs.shape[0],
     )
 
@@ -388,7 +388,7 @@
         [whole_out(rows, width), whole_out(rows, width), ((count, rows, cols), BF16, lead_spec(rows, cols))],
         [],
         "first_project",
-        16,
+        12,
         4,
     )
 
@@ -416,7 +416,7 @@
         ],
         [],
         "other_project",
-        12,
+        9,
         3,
     )
 
@@ -473,7 +473,7 @@
         [whole_out(*shape, kind=F32), whole_out(*shape)] + query_outs(part_b, shape[1]),
         [],
         "second_project",
-        20,
+        17,
         5,
     )
 
@@ -503,7 +503,7 @@
         ],
         [],
         "offer_project",
-        12,
+        9,
         4,
     )
 
@@ -688,7 +688,7 @@
         + [whole_out(2, 5, half, half), whole_out(2, 5, half, half), whole_out(2, width, kind=F32)],
         [pltpu.VMEM((rows, width), F32)],
         "second_back",
-        40,
+        35,
         12,
     )
 
@@ -739,7 +739,7 @@
         [whole_out(*rows.shape), pieces, pieces, whole_out(2, width, kind=F32)],
         [pltpu.VMEM(rows.shape, F32)],
         "first_back",
-        32,
+        24,
         11,
     )
 
@@ -835,15 +835,14 @@
     def add(left, right):
         return (left.astype(F32) + right.astype(F32)).astype(BF16)
 
-    def view_sum(total, received):
+    def last_levels(total, received):
         total = add(total, received)
-        for bit in range(2, levels):
+        for bit in range(3, levels):
             total = add(total, over_level(total, bit))
         return total
 
-    def all_rows(mine, theirs):
+    def all_rows(mine, a_theirs, b_theirs):
         a_mine, b_mine = mine[:part_a], mine[part_a:]
-        a_theirs, b_theirs = theirs[:part_a], theirs[part_a:]
         kept = jnp.where(own_micro2, b_mine, b_theirs)
         received = other_core(jnp.where(own_micro2, b_theirs, b_mine))
         micro2 = in_core_order(core, kept, received, 0)
@@ -967,16 +966,19 @@
     dkv_received = other_core(dkv_send)
     up_x.append(over_head(up[1, 128:448]))
     down_total = add(down[0], jnp.concatenate(down_x))
-    *dq_b, dkv_received, up_x[1], down_total, up = fence(*dq_b, dkv_received, up_x[1], down_total, up)
+    down_y = [over_level(down_total[:384], 1)]
+    *dq_b, dkv_received, up_x[1], down_total, up, down_y[0] = fence(
+        *dq_b, dkv_received, up_x[1], down_total, up, down_y[0]
+    )
 
     up_x.append(over_head(up[1, 448:]))
-    down_y = over_level(down_total, 1)
+    down_y.append(over_level(down_total[384:], 1))
     grad_hidden, grad_mix, grad_send, mid_keep, mid_send, norms_2 = second_back(
         info, (*dq_a, *dq_b), dkv_a, dkv_b, dkv_received, joined, hidden, grad_second, norms, w_offer,
         offer_mine, offer_theirs, w_query, w_self_out, first_mine, first_theirs, mixes, cross_keep, cross_send,
     )
-    grad_hidden, grad_mix, grad_send, mid_keep, mid_send, up_x[2], down_y = fence(
-        grad_hidden, grad_mix, grad_send, mid_keep, mid_send, up_x[2], down_y
+    grad_hidden, grad_mix, grad_send, mid_keep, mid_send, up_x[2], up, down_total, down_y[1] = fence(
+        grad_hidden, grad_mix, grad_send, mid_keep, mid_send, up_x[2], up, down_total, down_y[1]
     )
 
     mid = add(mid_keep, other_core(mid_send))
@@ -984,54 +986,74 @@
     (back_0,) = attend_back(info, SELF_A, self_0 + [halves_of(grad_mix, 0)], p_0, half)
     back_s, back_send = attend_back(info, SELF_B, self_b + [grad_in], p_s, half)
     up_total = add(up[0], jnp.concatenate(up_x))
-    back_0, back_s, back_send, mid, up_total, grad_mix, down_total, down_y = fence(
-        back_0, back_s, back_send, mid, up_total, grad_mix, down_total, down_y
+    up_y = over_level(up_total, 1)
+    down_total = add(down_total, jnp.concatenate(down_y))
+    down_z = over_level(down_total, 2)
+    back_0, back_s, back_send, mid, up_total, grad_mix, up_y, down_total, down_z = fence(
+        back_0, back_s, back_send, mid, up_total, grad_mix, up_y, down_total, down_z
     )
 
     mid_x = [over_head(mid[1, :1])]
-    up_y = [over_level(up_total[:256], 1)]
+    up_total = add(up_total, up_y)
+    up_z = over_level(up_total, 2)
     back_received = other_core(back_send)
     (back_1,) = attend_back(info, SELF_A, self_1 + [halves_of(grad_mix, 1)], p_1, half)
-    back_1, back_received, mid_x[0], mid, up_y[0], up_total = fence(
-        back_1, back_received, mid_x[0], mid, up_y[0], up_total
-    )
+    back_1, back_received, mid_x[0], mid = fence(back_1, back_received, mid_x[0], mid)
 
     mid_x.append(over_head(mid[1, 1:3]))
-    up_y.append(over_level(up_total[256:], 1))
+    mid_total = [add(mid[0, :1], mid_x[0])]
+    mid_y = [over_level(mid_total[0], 1)]
     grad_rows, self_keep, self_send, norms_1 = first_back(
         info, back_0, back_1, back_s, back_received, rows, normed, grad_hidden, norms, w_self, self_mine, self_theirs
     )
-    grad_rows, self_keep, self_send, mid_x[1], up_y[1], mid = fence(
-        grad_rows, self_keep, self_send, mid_x[1], up_y[1], mid
-    )
+    grad_rows, self_keep, self_send, mid_x[1], mid, mid_y[0], mid_total[0], up_z = fence(
+        grad_rows, self_keep, self_send, mid_x[1], mid, mid_y[0], mid_total[0], up_z
+    )
+
     mid_x.append(over_head(mid[1, 3:]))
-    mid_total = [add(mid[0, :3], jnp.concatenate(mid_x[:2]))]
-    mid_y = [over_level(mid_total[0], 1)]
-    layer_out = all_rows(result, after(layer_x, grad_rows))
+    mid_total.append(add(mid[0, 1:3], mid_x[1]))
+    mid_y.append(over_level(mid_total[1], 1))
+    mid_total[0] = add(mid_total[0], mid_y[0])
+    mid_z = [over_level(mid_total[0], 2)]
     norm_grads = jnp.concatenate([norms_1, norms_2, norms_3, jnp.zeros((2, wide), F32)], axis=0)
     norm_grads = norm_grads.reshape(-1, half).astype(BF16)
     norm_grads = add(norm_grads, other_core(norm_grads))
     last = add(self_keep, other_core(self_send))
-    last, norm_grads, mid_x[2], mid, grad_rows = fence(last, norm_grads, mid_x[2], mid, grad_rows)
+    last, norm_grads, mid_x[2], mid, grad_rows, mid_y[1], mid_total[1], mid_z[0] = fence(
+        last, norm_grads, mid_x[2], mid, grad_rows, mid_y[1], mid_total[1], mid_z[0]
+    )
 
     end = jnp.concatenate([last[:, 2], jnp.stack([norm_grads, norm_grads])], axis=1)
     last_x = over_head(last[1, :2])
     mid_total.append(add(mid[0, 3:], mid_x[2]))
-    mid_y.append(over_level(mid_total[1], 1))
-    last_x, last, end, grad_rows = fence(last_x, last, end, grad_rows)
+    mid_y.append(over_level(mid_total[2], 1))
+    mid_total[1] = add(mid_total[1], mid_y[1])
+    mid_z.append(over_level(mid_total[1], 2))
+    layer_x = after(layer_x, last)
+    layer_out = all_rows(result, layer_x[:part_a], layer_x[part_a:])
+    last_x, last, end, grad_rows, mid_y[2], mid_total[2], mid_z[1] = fence(
+        last_x, last, end, grad_rows, mid_y[2], mid_total[2], mid_z[1]
+    )
 
     end_x = over_head(end[1])
-    rows_x = over_head(grad_rows)
+    rows_b_x = over_head(grad_rows[part_a:])
     last_total = add(last[0, :2], last_x)
     last_y = over_level(last_total, 1)
-    last_total, last_y, end_x = fence(last_total, last_y, end_x)
-
+    mid_total[2] = add(mid_total[2], mid_y[2])
+    mid_z.append(over_level(mid_total[2], 2))
+    last_total, last_y, end_x, rows_b_x, grad_rows, end, mid_z[2] = fence(
+        last_total, last_y, end_x, rows_b_x, grad_rows, end, mid_z[2]
+    )
+
+    rows_a_x = over_head(grad_rows[:part_a])
     end_total = add(end[0], end_x)
-    end_total = view_sum(end_total, over_level(end_total, 1))
-    last_total = view_sum(last_total, last_y)
-    down_total = view_sum(down_total, down_y)
-    up_total = view_sum(up_total, jnp.concatenate(up_y))
-    mid_total = [n for total, received in zip(mid_total, mid_y) for n in view_sum(total, received)]
+    end_total = add(end_total, over_level(end_total, 1))
+    last_total = add(last_total, last_y)
+    end_total = last_levels(end_total, over_level(end_total, 2))
+    last_total = last_levels(last_total, over_level(last_total, 2))
+    down_total = last_levels(down_total, down_z)
+    up_total = last_levels(up_total, up_z)
+    mid_total = [n for total, received in zip(mid_total, mid_z) for n in last_levels(total, received)]
     norms_total = end_total[half:].reshape(-1, wide)[:6]
 
     def whole(mine, axis):
@@ -1039,7 +1061,7 @@
 
     return (
         layer_out,
-        all_rows(grad_rows, rows_x).astype(F32),
+        all_rows(grad_rows, rows_a_x, rows_b_x).astype(F32),
         norms_total.astype(F32)[None],
         whole(jnp.concatenate([last_total, end_total[None, :half]]), 1),
         whole(mid_total[3], 1),

time: 500 us -> 479 us (0.958)
  waiting for transfers between devices: 169 us -> 143 us
  starting transfers between devices: 87.1 us -> 94.2 us
    ppermute x45 -> x47, waiting for transfers between devices: 79.3 us -> 39.1 us  [over_bit(): lax.ppermute(value, 'clip', [(i, i ^ 1 << bit) for i in range(count)])]
    ppermute x19 -> x20, waiting for transfers between devices: 40.6 us -> 54.7 us  [over_head(): return lax.ppermute(value, 'head', [(0, 1), (1, 0)])]
    ppermute x19 -> x20, starting transfers between devices: 20.9 us -> 25.5 us  [over_head(): return lax.ppermute(value, 'head', [(0, 1), (1, 0)])]
    ppermute x45 -> x47, starting transfers between devices: 32.6 us -> 35.6 us  [over_bit(): lax.ppermute(value, 'clip', [(i, i ^ 1 << bit) for i in range(count)])]
    convert_element_type x23 -> x26, other arithmetic: 15.5 us -> 14.3 us  [add(): return (left.astype(F32) + right.astype(F32)).astype(BF16)]
    unnamed x182 -> x168, local copies, waits for them, and re-layouts: 16.5 us -> 15.3 us
    convert_element_type x6 -> x7, other arithmetic: 11.6 us -> 12.2 us  [whole(): return in_core_order(core, mine, other_core(mine), axis).astype(F32)[None]]
  transfers between devices with their start and end apart: 80 -> 83, of which waited for: 29 -> 32; matrix products, arithmetic and copies ran while one was open for 10% -> 11% of each run, Pallas kernels for 25% -> 26%
where the time goes in v3:
time: 479 us; the launch traced here: 470 us
  Pallas kernels  159 us (33%)
  waiting for transfers between devices  143 us (30%)
  starting transfers between devices  94.2 us (20%)
  other arithmetic  44.1 us (9%)
  local copies, waits for them, and re-layouts  27.5 us (6%)
    pallas_call x17, Pallas kernels, call(): pl.pallas_call(kernel, grid_spec=pltpu.PrefetchScalarGridSpec(num_scalar_...  159 us
    ppermute x20, waiting for transfers between devices, over_head(): return lax.ppermute(value, 'head', [(0, 1), (1, 0)])  54.7 us
    ppermute x4, waiting for transfers between devices, to_server(): return (lax.ppermute(far_rows, 'clip', far), second)  45.5 us
    ppermute x47, waiting for transfers between devices, over_bit(): lax.ppermute(value, 'clip', [(i, i ^ 1 << bit) for i in range(count)])  39.1 us
    ppermute x47, starting transfers between devices, over_bit(): lax.ppermute(value, 'clip', [(i, i ^ 1 << bit) for i in range(count)])  35.6 us
    ppermute x20, starting transfers between devices, over_head(): return lax.ppermute(value, 'head', [(0, 1), (1, 0)])  25.5 us
    ppermute x4, starting transfers between devices, to_reader(): return (lax.ppermute(far_rows, 'clip', [(b, a) for a, b in far]), second)  21.8 us
    unnamed x168, local copies, waits for them, and re-layouts  15.3 us
  transfers between devices with their start and end apart: 83, of which 32 were waited for; matrix products, arithmetic and copies ran while one was open for 11% of the time, Pallas kernels for 26%

profile of v3, /device:TPU:0, one launch (start us, length us, event | category | flops | bytes accessed | tf_op | source)
XLA Modules:
  0.0 469.9 jit_solution(14583113377652375262)
XLA Ops:
  3.0 2.2 dynamic-slice_bitcast_fusion
  5.2 2.5 collective-permute-start.1
  12.9 3.9 first_project.1
  16.8 7.9 %attend.5 = (bf16[512,384]{1,0:T(8,128)(2,1)S(1)}, bf16[6,512,512]{2,1,0:T(8,128)(2,1)}) custom-call(s32[72]{0:T(128)S(1)} %concatenate.129.info, bf16[3,768,384]{2,1,0:T(8,128)(2,1)S(1)} %get-tuple-element.202.refs_0_.refs_1_.refs_2_.refs_3_.refs_4_.refs_5_.own_b_ref.refs_6_, ...), custom_call_target="tpu_custom_call" | custom-call | bytes 4 | tf_op jit(solution)/shard_map/attend/pallas_call | solution.py:134
  25.4 2.9 collective-permute-done.1.mine_ref
  28.3 1.7 collective-permute-start.4
  30.9 4.2 other_project.1
  36.3 7.9 %attend.6 = (bf16[512,384]{1,0:T(8,128)(2,1)S(1)}, bf16[6,512,512]{2,1,0:T(8,128)(2,1)}) custom-call(s32[72]{0:T(128)S(1)} %concatenate.129.info, bf16[3,768,384]{2,1,0:T(8,128)(2,1)S(1)} %get-tuple-element.209.refs_0_.refs_1_.refs_2_.refs_3_.refs_4_.refs_5_.refs_7_, ...), custom_call_target="tpu_custom_call" | custom-call | bytes 4 | tf_op jit(solution)/shard_map/attend/pallas_call | solution.py:134
  44.6 8.6 %attend.7 = (bf16[512,384]{1,0:T(8,128)(2,1)S(1)}, bf16[256,384]{1,0:T(8,128)(2,1)}, bf16[6,512,512]{2,1,0:T(8,128)(2,1)}) custom-call(s32[72]{0:T(128)S(1)} %concatenate.129.info, bf16[3,768,384]{2,1,0:T(8,128)(2,1)S(1)} %get-tuple-element.202.refs_0_.refs_1_.refs_2_.refs_3_.refs_4_.refs_5_.own_b_ref.refs_6_, ...), custom_call_target="tpu_custom_call" | custom-call | bytes 4 | tf_op jit(solution)/shard_map/attend/pallas_call | solution.py:134
  54.2 1.8 collective-permute-start.8
  56.0 1.8 constant_dynamic-slice_fusion.1
  57.9 6.4 %second_project.1 = (f32[768,768]{1,0:T(8,128)S(1)}, bf16[768,768]{1,0:T(8,128)(2,1)S(1)}, bf16[256,768]{1,0:T(8,128)(2,1)S(1)}, bf16[256,768]{1,0:T(8,128)(2,1)...) custom-call(s32[72]{0:T(128)S(1)} %concatenate.129.info, ...), custom_call_target="tpu_custom_call" | custom-call | bytes 5 | tf_op jit(solution)/shard_map/second_project/pallas_call | solution.py:134
  65.9 4.1 collective-permute-done.8.mine_ref.offer_mine_ref
  75.1 3.4 offer_project.1
  78.5 3.8 collective-permute-done.11.refs_0_
  84.4 18.5 %collective-permute-done.9.refs_0_ = bf16[256,768]{1,0:T(8,128)(2,1)S(1)} collective-permute-done((bf16[256,768]{1,0:T(8,128)(2,1)S(1)}, bf16[256,768]{1,0:T(8,128)(2,1)S(1)}, u32[]{:S(2)}, u32[]{:S(2)}) %collective-permute-start.9) | collective-permute-done | bytes 393248 | tf_op jit(solution)/shard_map/ppermute | solution.py:819
  103.4 8.6 %attend.8 = (bf16[256,768]{1,0:T(8,128)(2,1)S(1)}, bf16[256,768]{1,0:T(8,128)(2,1)S(1)}, bf16[12,256,512]{2,1,0:T(8,128)(2,1)}) custom-call(s32[72]{0:T(128)S(1)} %concatenate.129.info, bf16[256,768]{1,0:T(8,128)(2,1)S(1)} %collective-permute-done.9.refs_0_, bf16[256,768]{1,0:T(8,128)(2,1)S(1)} %collective-permute-done.10.refs_1_, ...), custom_call_target="tpu_custom_call" | custom-call | bytes 8 | tf_op jit(solution)/shard_map/attend/pallas_call | solution.py:134
  112.0 3.9 collective-permute-done.17
  118.5 1.8 collective-permute-start.20
  120.3 5.2 %attend.9 = (bf16[256,384]{1,0:T(8,128)(2,1)S(1)}, bf16[256,384]{1,0:T(8,128)(2,1)S(1)}, bf16[6,256,512]{2,1,0:T(8,128)(2,1)}) custom-call(s32[72]{0:T(128)S(1)} %concatenate.129.info, bf16[256,384]{1,0:T(8,128)(2,1)S(1)} %collective-permute-done.11.refs_0_, bf16[256,384]{1,0:T(8,128)(2,1)S(1)} %collective-permute-done.12.refs_1_, ...), custom_call_target="tpu_custom_call" | custom-call | bytes 4 | tf_op jit(solution)/shard_map/attend/pallas_call | solution.py:134
  125.5 14.7 %collective-permute-done.20.mine_ref = bf16[384,384]{1,0:T(8,128)(2,1)S(1)} collective-permute-done((bf16[384,384]{1,0:T(8,128)(2,1)S(1)}, bf16[384,384]{1,0:T(8,128)(2,1)S(1)}, u32[]{:S(2)}, u32[]{:S(2)}) %collective-permute-start.20) | collective-permute-done | bytes 294944 | tf_op jit(solution)/shard_map/ppermute | solution.py:24
  143.9 2.7 pad_maximum_fusion.up_ref
  147.7 2.5 pad_maximum_fusion.1.down_ref
  153.7 36.5 %mlp.1 = (bf16[768,768]{1,0:T(8,128)(2,1)S(1)}, f32[768,768]{1,0:T(8,128)}, bf16[256,768]{1,0:T(8,128)(2,1)}, bf16[256,768]{1,0:T(8,128)(2,1)S(1)}, bf16[256,384...) custom-call(s32[72]{0:T(128)S(1)} %concatenate.129.info, ...), custom_call_target="tpu_custom_call" | custom-call | bytes 34 | tf_op jit(solution)/shard_map/mlp/pallas_call | solution.py:134
  198.6 2.5 add_convert_fusion.1
  202.4 23.1 %collective-permute-done.31.refs_8_ = bf16[256,384]{1,0:T(8,128)(2,1)S(1)} collective-permute-done((bf16[256,384]{1,0:T(8,128)(2,1)S(1)}, bf16[256,384]{1,0:T(8,128)(2,1)S(1)}, u32[]{:S(2)}, u32[]{:S(2)}) %collective-permute-start.31) | collective-permute-done | bytes 196640 | tf_op jit(solution)/shard_map/ppermute | solution.py:819
  225.7 1.8 collective-permute-start.36
  227.5 9.1 %attend_back.5 = (bf16[256,768]{1,0:T(8,128)(2,1)S(1)}, bf16[256,768]{1,0:T(8,128)(2,1)S(1)}, bf16[2,512,768]{2,1,0:T(8,128)(2,1)S(1)}) custom-call(s32[72]{0:T(128)S(1)} %concatenate.129.info, bf16[256,768]{1,0:T(8,128)(2,1)S(1)} %copy-done.28, bf16[256,768]{1,0:T(8,128)(2,1)S(1)} %collective-permute-done.10.refs_1_, ...), custom_call_target="tpu_custom_call" | custom-call | bytes 12 | tf_op jit(solution)/shard_map/attend_back/pallas_call | solution.py:134
  236.6 3.4 collective-permute-done.36
  240.0 1.8 collective-permute-start.39
  241.8 7.5 %collective-permute-start.37 = (bf16[256,768]{1,0:T(8,128)(2,1)S(1)}, bf16[256,768]{1,0:T(8,128)(2,1)S(1)}, u32[]{:S(2)}, u32[]{:S(2)}) collective-permute-start(bf16[256,768]{1,0:T(8,128)(2,1)S(1)} %get-tuple-element.292), channel_id=1, source_target_pairs={{0,16},{2,18},{4,20},{6,22},{16,24},{18,26},{20,28},{22,30},{1,17}... | collective-permute-start | bytes 1179656 | tf_op jit(solution)/shard_map/ppermute | solution.py:823
  250.4 5.1 %attend_back.6 = (bf16[256,384]{1,0:T(8,128)(2,1)S(1)}, bf16[256,384]{1,0:T(8,128)(2,1)S(1)}, bf16[2,512,384]{2,1,0:T(8,128)(2,1)S(1)}, bf16[2,256,384]{2,1,0:T(8,128)(2,1)S(1)}) custom-call(s32[72]{0:T(128)S(1)} %concatenate.129.info, bf16[256,384]{1,0:T(8,128)(2,1)S(1)} %copy-done.48, bf16[256,384]{1,0:T(8,128)(2,1)S(1)} %copy-done.50, ...), custom_call_target="tpu_custom_call" | custom-call | bytes 6 | tf_op jit(solution)/shard_map/attend_back/pallas_call | solution.py:134
  255.5 2.1 collective-permute-done.40
  258.4 1.8 collective-permute-start.46
  260.2 11.4 %collective-permute-start.41 = (bf16[256,384]{1,0:T(8,128)(2,1)S(1)}, bf16[256,384]{1,0:T(8,128)(2,1)S(1)}, u32[]{:S(2)}, u32[]{:S(2)}) collective-permute-start(bf16[256,384]{1,0:T(8,128)(2,1)S(1)} %get-tuple-element.303), channel_id=1, source_target_pairs={{0,16},{2,18},{4,20},{6,22},{16,24},{18,26},{20,28},{22,30},{1,17}... | collective-permute-start | bytes 589832 | tf_op jit(solution)/shard_map/ppermute | solution.py:823
  273.4 2.3 collective-permute-done.41.far_b_ref
  277.2 8.2 %collective-permute-done.45 = bf16[320,768]{1,0:T(8,128)(2,1)S(1)} collective-permute-done((bf16[320,768]{1,0:T(8,128)(2,1)S(1)}, bf16[320,768]{1,0:T(8,128)(2,1)S(1)}, u32[]{:S(2)}, u32[]{:S(2)}) %collective-permute-start.45) | collective-permute-done | bytes 491552 | tf_op jit(solution)/shard_map/ppermute | solution.py:24
  287.7 16.1 %second_back.1 = (f32[768,768]{1,0:T(8,128)S(1)}, bf16[2,768,384]{2,1,0:T(8,128)(2,1)S(1)}, bf16[256,384]{1,0:T(8,128)(2,1)S(1)}, bf16[2,5,384,384]{3,2,1,0:T(8,...) custom-call(s32[72]{0:T(128)S(1)} %concatenate.129.info, ...), custom_call_target="tpu_custom_call" | custom-call | bytes 12 | tf_op jit(solution)/shard_map/second_back/pallas_call | solution.py:134
  306.3 4.2 collective-permute-start.52
  312.2 7.8 %attend_back.7.own_ref = bf16[3,512,384]{2,1,0:T(8,128)(2,1)S(1)} custom-call(s32[72]{0:T(128)S(1)} %concatenate.129.info, bf16[3,768,384]{2,1,0:T(8,128)(2,1)S(1)} %get-tuple-element.202.refs_0_.refs_1_.refs_2_.refs_3_.refs_4_.refs_5_.own_b_ref.refs_6_, ...), custom_call_target="tpu_custom_call" | custom-call | bytes 6 | tf_op jit(solution)/shard_map/attend_back/pallas_call | solution.py:134
  320.1 8.2 %attend_back.8 = (bf16[3,512,384]{2,1,0:T(8,128)(2,1)S(1)}, bf16[3,256,384]{2,1,0:T(8,128)(2,1)S(1)}) custom-call(s32[72]{0:T(128)S(1)} %concatenate.129.info, bf16[3,768,384]{2,1,0:T(8,128)(2,1)S(1)} %get-tuple-element.202.refs_0_.refs_1_.refs_2_.refs_3_.refs_4_.refs_5_.own_b_ref.refs_6_, ...), custom_call_target="tpu_custom_call" | custom-call | bytes 6 | tf_op jit(solution)/shard_map/attend_back/pallas_call | solution.py:134
  329.2 7.6 %collective-permute-done.52 = bf16[768,768]{1,0:T(8,128)(2,1)S(1)} collective-permute-done((bf16[768,768]{1,0:T(8,128)(2,1)S(1)}, bf16[768,768]{1,0:T(8,128)(2,1)S(1)}, u32[]{:S(2)}, u32[]{:S(2)}) %collective-permute-start.52) | collective-permute-done | bytes 1179680 | tf_op jit(solution)/shard_map/ppermute | solution.py:29
  336.8 2.1 collective-permute-done.51
  339.2 2.5 collective-permute-start.57
  343.4 7.8 %attend_back.9.other_ref = bf16[3,512,384]{2,1,0:T(8,128)(2,1)S(1)} custom-call(s32[72]{0:T(128)S(1)} %concatenate.129.info, bf16[3,768,384]{2,1,0:T(8,128)(2,1)S(1)} %get-tuple-element.209.refs_0_.refs_1_.refs_2_.refs_3_.refs_4_.refs_5_.refs_7_, bf16[3,768,384]{2,1,0:T(8,128)(2,1)S(1)} %get-tuple-element.209.refs_0_.refs_1_.refs_2_.refs_3_.refs_4_.refs_5_.refs_7_, ...), custom_call_target="tpu_custom_call" | custom-call | bytes 6 | tf_op jit(solution)/shard_map/attend_back/pallas_call | solution.py:134
  355.4 12.1 %first_back.1 = (bf16[768,768]{1,0:T(8,128)(2,1)S(1)}, bf16[2,3,384,384]{3,2,1,0:T(8,128)(2,1)S(1)}, bf16[2,3,384,384]{3,2,1,0:T(8,128)(2,1)S(1)}, f32[2,768]{1,0:T(2,128)S(1)}) custom-call(s32[72]{0:T(128)S(1)} %concatenate.129.info, bf16[3,512,384]{2,1,0:T(8,128)(2,1)S(1)} %attend_back.7.own_ref, bf16[3,512,384]{2,1,0:T(8,128)(2,1)S(1)} %attend_back.9.other_ref, ...), custom_call_target="tpu_custom_call" | custom-call | bytes 11 | tf_op jit(solution)/shard_map/first_back/pallas_call | solution.py:134
  367.6 1.9 collective-permute-done.57
  374.8 2.4 collective-permute-start.62
  382.5 2.6 select_bitcast_fusion.1
  385.2 2.5 maximum_convert_fusion.2
  387.7 2.8 maximum_convert_fusion.1
  391.1 2.9 collective-permute-done.61
  393.9 2.0 collective-permute-done.60
  396.1 4.0 collective-permute-start.66
  407.6 4.6 collective-permute-done.66
  412.2 3.0 collective-permute-done.65
  416.0 2.5 collective-permute-start.70
  422.3 12.0 %collective-permute-done.68 = bf16[400,384]{1,0:T(8,128)(2,1)S(1)} collective-permute-done((bf16[400,384]{1,0:T(8,128)(2,1)S(1)}, bf16[400,384]{1,0:T(8,128)(2,1)S(1)}, u32[]{:S(2)}, u32[]{:S(2)}) %collective-permute-start.68) | collective-permute-done | bytes 307232 | tf_op jit(solution)/shard_map/ppermute | solution.py:24
  435.3 3.6 collective-permute-start.75
  448.5 2.2 collective-permute-start.74
  450.8 2.2 collective-permute-done.75
  453.2 6.3 %collective-permute-done.74 = bf16[400,384]{1,0:T(8,128)(2,1)S(1)} collective-permute-done((bf16[400,384]{1,0:T(8,128)(2,1)S(1)}, bf16[400,384]{1,0:T(8,128)(2,1)S(1)}, u32[]{:S(2)}, u32[]{:S(2)}) %collective-permute-start.74) | collective-permute-done | bytes 307232 | tf_op jit(solution)/shard_map/ppermute | solution.py:29
  463.4 2.6 maximum_convert_fusion
  467.4 2.0 maximum_convert_fusion.3
  (401 shorter events, 99.0 us)
Async XLA Ops:
  2.6 7.0 %collective-permute-start = (bf16[256,768]{1,0:T(8,128)(2,1)}, bf16[256,768]{1,0:T(8,128)(2,1)S(1)}, u32[]{:S(2)}, u32[]{:S(2)}) collective-permute-start(bf16[256,768]{1,0:T(8,128)(2,1)} %dynamic-slice_bitcast_fusion.3), channel_id=1, source_target_pairs={{0,2},{2,0},{4,6},{6,4},{8,10},{10,8},{12,14},{14,12},{16,18},{18,... | collective-permute-start | bytes 1179656 | tf_op jit(solution)/shard_map/ppermute | solution.py:29
  5.2 23.1 %collective-permute-start.1 = (bf16[3,384,384]{2,1,0:T(8,128)(2,1)}, bf16[3,384,384]{2,1,0:T(8,128)(2,1)}, u32[]{:S(2)}, u32[]{:S(2)}) collective-permute-start(bf16[3,384,384]{2,1,0:T(8,128)(2,1)} %dynamic-slice_bitcast_fusion), channel_id=1, source_target_pairs={{0,1},{1,0},{2,3},{3,2},{4,5},{5,4},{6,7},{7,6},{8,9},{9,8},{10,11... | collective-permute-start | bytes 2654216 | tf_op jit(solution)/shard_map/ppermute | solution.py:24
  28.3 15.8 %collective-permute-start.4 = (bf16[2,384,384]{2,1,0:T(8,128)(2,1)S(1)}, bf16[2,384,384]{2,1,0:T(8,128)(2,1)}, u32[]{:S(2)}, u32[]{:S(2)}) collective-permute-start(bf16[2,384,384]{2,1,0:T(8,128)(2,1)S(1)} %pad_maximum_fusion.4), channel_id=1, source_target_pairs={{0,1},{1,0},{2,3},{3,2},{4,5},{5,4},{6,7},{7,6},{8,9},{9,8},{10,11... | collective-permute-start | bytes 1769480 | tf_op jit(solution)/shard_map/ppermute | solution.py:24
  35.2 9.0 %collective-permute-start.3 = (bf16[3,256,384]{2,1,0:T(8,128)(2,1)S(1)}, bf16[3,256,384]{2,1,0:T(8,128)(2,1)S(1)}, u32[]{:S(2)}, u32[]{:S(2)}) collective-permute-start(bf16[3,256,384]{2,1,0:T(8,128)(2,1)S(1)} %get-tuple-element.207), channel_id=1, source_target_pairs={{0,2},{2,0},{4,6},{6,4},{8,10},{10,8},{12,14},{14,12},{16,18},{18,... | collective-permute-start | bytes 1769480 | tf_op jit(solution)/shard_map/ppermute | solution.py:29
  44.2 13.6 %collective-permute-start.6 = (bf16[2,384,384]{2,1,0:T(8,128)(2,1)}, bf16[2,384,384]{2,1,0:T(8,128)(2,1)}, u32[]{:S(2)}, u32[]{:S(2)}) collective-permute-start(bf16[2,384,384]{2,1,0:T(8,128)(2,1)} %collective-permute-done.4.mine_ref), channel_id=1, source_target_pairs={{0,2},{2,0},{4,6},{6,4},{8,10},{10,8},{12,14},{14,12},{16,18},{18,... | collective-permute-start | bytes 1769480 | tf_op jit(solution)/shard_map/ppermute | solution.py:29
  54.2 15.9 %collective-permute-start.8 = (bf16[2,384,384]{2,1,0:T(8,128)(2,1)}, bf16[2,384,384]{2,1,0:T(8,128)(2,1)S(1)}, u32[]{:S(2)}, u32[]{:S(2)}) collective-permute-start(bf16[2,384,384]{2,1,0:T(8,128)(2,1)} %dynamic-slice_bitcast_fusion.1), channel_id=1, source_target_pairs={{0,1},{1,0},{2,3},{3,2},{4,5},{5,4},{6,7},{7,6},{8,9},{9,8},{10,11... | collective-permute-start | bytes 1769480 | tf_op jit(solution)/shard_map/ppermute | solution.py:24
  70.1 32.9 %collective-permute-start.16 = (bf16[768,768]{1,0:T(8,128)(2,1)S(1)}, bf16[768,768]{1,0:T(8,128)(2,1)S(1)}, u32[]{:S(2)}, u32[]{:S(2)}) collective-permute-start(bf16[768,768]{1,0:T(8,128)(2,1)S(1)} %bitcast.166), channel_id=1, source_target_pairs={{0,1},{1,0},{2,3},{3,2},{4,5},{5,4},{6,7},{7,6},{8,9},{9,8},{10,11... | collective-permute-start | bytes 3538952 | tf_op jit(solution)/shard_map/ppermute | solution.py:24
  71.8 10.5 %collective-permute-start.11 = (bf16[256,384]{1,0:T(8,128)(2,1)S(1)}, bf16[256,384]{1,0:T(8,128)(2,1)S(1)}, u32[]{:S(2)}, u32[]{:S(2)}) collective-permute-start(bf16[256,384]{1,0:T(8,128)(2,1)S(1)} %get-tuple-element.226), channel_id=1, source_target_pairs={{16,0},{18,2},{20,4},{22,6},{24,16},{26,18},{28,20},{30,22},{17,1}... | collective-permute-start | bytes 589832 | tf_op jit(solution)/shard_map/ppermute | solution.py:819
  73.1 10.5 %collective-permute-start.12 = (bf16[256,384]{1,0:T(8,128)(2,1)S(1)}, bf16[256,384]{1,0:T(8,128)(2,1)S(1)}, u32[]{:S(2)}, u32[]{:S(2)}) collective-permute-start(bf16[256,384]{1,0:T(8,128)(2,1)S(1)} %get-tuple-element.227), channel_id=1, source_target_pairs={{16,8},{18,10},{20,12},{22,14},{24,16},{26,18},{28,20},{30,22},{17... | collective-permute-start | bytes 589832 | tf_op jit(solution)/shard_map/ppermute | solution.py:818
  73.8 9.8 %collective-permute-start.15 = (bf16[256,768]{1,0:T(8,128)(2,1)S(1)}, bf16[256,768]{1,0:T(8,128)(2,1)S(1)}, u32[]{:S(2)}, u32[]{:S(2)}) collective-permute-start(bf16[256,768]{1,0:T(8,128)(2,1)S(1)} %dynamic-slice_bitcast_fusion.2), channel_id=1, source_target_pairs={{0,2},{2,0},{4,6},{6,4},{8,10},{10,8},{12,14},{14,12},{16,18},{18,... | collective-permute-start | bytes 1179656 | tf_op jit(solution)/shard_map/ppermute | solution.py:29
  74.4 10.0 %collective-permute-start.10 = (bf16[256,768]{1,0:T(8,128)(2,1)S(1)}, bf16[256,768]{1,0:T(8,128)(2,1)S(1)}, u32[]{:S(2)}, u32[]{:S(2)}) collective-permute-start(bf16[256,768]{1,0:T(8,128)(2,1)S(1)} %get-tuple-element.225), channel_id=1, source_target_pairs={{16,8},{18,10},{20,12},{22,14},{24,16},{26,18},{28,20},{30,22},{17... | collective-permute-start | bytes 1179656 | tf_op jit(solution)/shard_map/ppermute | solution.py:818
  82.3 20.7 %collective-permute-start.9 = (bf16[256,768]{1,0:T(8,128)(2,1)S(1)}, bf16[256,768]{1,0:T(8,128)(2,1)S(1)}, u32[]{:S(2)}, u32[]{:S(2)}) collective-permute-start(bf16[256,768]{1,0:T(8,128)(2,1)S(1)} %get-tuple-element.224), channel_id=1, source_target_pairs={{16,0},{18,2},{20,4},{22,6},{24,16},{26,18},{28,20},{30,22},{17,1}... | collective-permute-start | bytes 1179656 | tf_op jit(solution)/shard_map/ppermute | solution.py:819
  83.6 19.4 %collective-permute-start.14 = (bf16[2,256,384]{2,1,0:T(8,128)(2,1)S(1)}, bf16[2,256,384]{2,1,0:T(8,128)(2,1)S(1)}, u32[]{:S(2)}, u32[]{:S(2)}) collective-permute-start(bf16[2,256,384]{2,1,0:T(8,128)(2,1)S(1)} %get-tuple-element.230), channel_id=1, source_target_pairs={{0,2},{2,0},{4,6},{6,4},{8,10},{10,8},{12,14},{14,12},{16,18},{18,... | collective-permute-start | bytes 1179656 | tf_op jit(solution)/shard_map/ppermute | solution.py:29
  103.0 12.9 %collective-permute-start.17 = (bf16[320,768]{1,0:T(8,128)(2,1)S(1)}, bf16[320,768]{1,0:T(8,128)(2,1)S(1)}, u32[]{:S(2)}, u32[]{:S(2)}) collective-permute-start(bf16[320,768]{1,0:T(8,128)(2,1)S(1)} %slice.125), channel_id=1, source_target_pairs={{0,1},{1,0},{2,3},{3,2},{4,5},{5,4},{6,7},{7,6},{8,9},{9,8},{10,11... | collective-permute-start | bytes 1474568 | tf_op jit(solution)/shard_map/ppermute | solution.py:24
  115.9 25.0 %collective-permute-start.21 = (bf16[768,768]{1,0:T(8,128)(2,1)S(1)}, bf16[768,768]{1,0:T(8,128)(2,1)S(1)}, u32[]{:S(2)}, u32[]{:S(2)}) collective-permute-start(bf16[768,768]{1,0:T(8,128)(2,1)S(1)} %collective-permute-done.16), channel_id=1, source_target_pairs={{0,2},{2,0},{4,6},{6,4},{8,10},{10,8},{12,14},{14,12},{16,18},{18,... | collective-permute-start | bytes 3538952 | tf_op jit(solution)/shard_map/ppermute | solution.py:29
  116.0 25.0 %collective-permute-start.22 = (bf16[448,768]{1,0:T(8,128)(2,1)S(1)}, bf16[448,768]{1,0:T(8,128)(2,1)S(1)}, u32[]{:S(2)}, u32[]{:S(2)}) collective-permute-start(bf16[448,768]{1,0:T(8,128)(2,1)S(1)} %slice.126), channel_id=1, source_target_pairs={{0,1},{1,0},{2,3},{3,2},{4,5},{5,4},{6,7},{7,6},{8,9},{9,8},{10,11... | collective-permute-start | bytes 2064392 | tf_op jit(solution)/shard_map/ppermute | solution.py:24
  116.3 23.9 %collective-permute-start.18 = (bf16[256,768]{1,0:T(8,128)(2,1)S(1)}, bf16[256,768]{1,0:T(8,128)(2,1)S(1)}, u32[]{:S(2)}, u32[]{:S(2)}) collective-permute-start(bf16[256,768]{1,0:T(8,128)(2,1)S(1)} %get-tuple-element.245), channel_id=1, source_target_pairs={{0,16},{2,18},{4,20},{6,22},{16,24},{18,26},{20,28},{22,30},{1,17}... | collective-permute-start | bytes 1179656 | tf_op jit(solution)/shard_map/ppermute | solution.py:823
  117.8 23.2 %collective-permute-start.19 = (bf16[256,768]{1,0:T(8,128)(2,1)S(1)}, bf16[256,768]{1,0:T(8,128)(2,1)S(1)}, u32[]{:S(2)}, u32[]{:S(2)}) collective-permute-start(bf16[256,768]{1,0:T(8,128)(2,1)S(1)} %get-tuple-element.246), channel_id=1, source_target_pairs={{8,16},{10,18},{12,20},{14,22},{16,24},{18,26},{20,28},{22,30},{9,... | collective-permute-start | bytes 1179656 | tf_op jit(solution)/shard_map/ppermute | solution.py:822
  118.5 21.7 %collective-permute-start.20 = (bf16[384,384]{1,0:T(8,128)(2,1)S(1)}, bf16[384,384]{1,0:T(8,128)(2,1)S(1)}, u32[]{:S(2)}, u32[]{:S(2)}) collective-permute-start(bf16[384,384]{1,0:T(8,128)(2,1)S(1)} %dynamic-slice_bitcast_fusion.4), channel_id=1, source_target_pairs={{0,1},{1,0},{2,3},{3,2},{4,5},{5,4},{6,7},{7,6},{8,9},{9,8},{10,11... | collective-permute-start | bytes 884744 | tf_op jit(solution)/shard_map/ppermute | solution.py:24
  192.9 8.2 %collective-permute-start.34 = (bf16[2,768,768]{2,1,0:T(8,128)(2,1)}, bf16[2,768,768]{2,1,0:T(8,128)(2,1)S(1)}, u32[]{:S(2)}, u32[]{:S(2)}) collective-permute-start(bf16[2,768,768]{2,1,0:T(8,128)(2,1)} %get-tuple-element.279), channel_id=1, source_target_pairs={{0,2},{2,0},{4,6},{6,4},{8,10},{10,8},{12,14},{14,12},{16,18},{18,... | collective-permute-start | bytes 7077896 | tf_op jit(solution)/shard_map/ppermute | solution.py:29
  193.1 32.5 %collective-permute-start.33 = (bf16[768,768]{1,0:T(8,128)(2,1)S(1)}, bf16[768,768]{1,0:T(8,128)(2,1)S(1)}, u32[]{:S(2)}, u32[]{:S(2)}) collective-permute-start(bf16[768,768]{1,0:T(8,128)(2,1)S(1)} %get-tuple-element.273), channel_id=1, source_target_pairs={{0,1},{1,0},{2,3},{3,2},{4,5},{5,4},{6,7},{7,6},{8,9},{9,8},{10,11... | collective-permute-start | bytes 3538952 | tf_op jit(solution)/shard_map/ppermute | solution.py:24
  193.4 32.2 %collective-permute-start.29 = (bf16[256,768]{1,0:T(8,128)(2,1)}, bf16[256,768]{1,0:T(8,128)(2,1)S(1)}, u32[]{:S(2)}, u32[]{:S(2)}) collective-permute-start(bf16[256,768]{1,0:T(8,128)(2,1)} %get-tuple-element.274), channel_id=1, source_target_pairs={{16,0},{18,2},{20,4},{22,6},{24,16},{26,18},{28,20},{30,22},{17,1}... | collective-permute-start | bytes 1179656 | tf_op jit(solution)/shard_map/ppermute | solution.py:819
  194.7 30.9 %collective-permute-start.30 = (bf16[256,768]{1,0:T(8,128)(2,1)}, bf16[256,768]{1,0:T(8,128)(2,1)S(1)}, u32[]{:S(2)}, u32[]{:S(2)}) collective-permute-start(bf16[256,768]{1,0:T(8,128)(2,1)} %copy-done.66), channel_id=1, source_target_pairs={{16,8},{18,10},{20,12},{22,14},{24,16},{26,18},{28,20},{30,22},{17... | collective-permute-start | bytes 1179656 | tf_op jit(solution)/shard_map/ppermute | solution.py:818
  197.3 28.3 %collective-permute-start.31 = (bf16[256,384]{1,0:T(8,128)(2,1)S(1)}, bf16[256,384]{1,0:T(8,128)(2,1)S(1)}, u32[]{:S(2)}, u32[]{:S(2)}) collective-permute-start(bf16[256,384]{1,0:T(8,128)(2,1)S(1)} %get-tuple-element.276), channel_id=1, source_target_pairs={{16,0},{18,2},{20,4},{22,6},{24,16},{26,18},{28,20},{30,22},{17,1}... | collective-permute-start | bytes 589832 | tf_op jit(solution)/shard_map/ppermute | solution.py:819
  201.1 24.5 %collective-permute-start.32 = (bf16[256,384]{1,0:T(8,128)(2,1)S(1)}, bf16[256,384]{1,0:T(8,128)(2,1)S(1)}, u32[]{:S(2)}, u32[]{:S(2)}) collective-permute-start(bf16[256,384]{1,0:T(8,128)(2,1)S(1)} %get-tuple-element.277), channel_id=1, source_target_pairs={{16,8},{18,10},{20,12},{22,14},{24,16},{26,18},{28,20},{30,22},{17... | collective-permute-start | bytes 589832 | tf_op jit(solution)/shard_map/ppermute | solution.py:818
  225.7 14.3 %collective-permute-start.36 = (bf16[384,768]{1,0:T(8,128)(2,1)S(1)}, bf16[384,768]{1,0:T(8,128)(2,1)S(1)}, u32[]{:S(2)}, u32[]{:S(2)}) collective-permute-start(bf16[384,768]{1,0:T(8,128)(2,1)S(1)} %slice_bitcast_fusion.5), channel_id=1, source_target_pairs={{0,1},{1,0},{2,3},{3,2},{4,5},{5,4},{6,7},{7,6},{8,9},{9,8},{10,11... | collective-permute-start | bytes 1769480 | tf_op jit(solution)/shard_map/ppermute | solution.py:24
  240.0 17.6 %collective-permute-start.39 = (bf16[384,768]{1,0:T(8,128)(2,1)S(1)}, bf16[384,768]{1,0:T(8,128)(2,1)S(1)}, u32[]{:S(2)}, u32[]{:S(2)}) collective-permute-start(bf16[384,768]{1,0:T(8,128)(2,1)S(1)} %slice_bitcast_fusion.4), channel_id=1, source_target_pairs={{0,1},{1,0},{2,3},{3,2},{4,5},{5,4},{6,7},{7,6},{8,9},{9,8},{10,11... | collective-permute-start | bytes 1769480 | tf_op jit(solution)/shard_map/ppermute | solution.py:24
  241.8 15.8 %collective-permute-start.37 = (bf16[256,768]{1,0:T(8,128)(2,1)S(1)}, bf16[256,768]{1,0:T(8,128)(2,1)S(1)}, u32[]{:S(2)}, u32[]{:S(2)}) collective-permute-start(bf16[256,768]{1,0:T(8,128)(2,1)S(1)} %get-tuple-element.292), channel_id=1, source_target_pairs={{0,16},{2,18},{4,20},{6,22},{16,24},{18,26},{20,28},{22,30},{1,17}... | collective-permute-start | bytes 1179656 | tf_op jit(solution)/shard_map/ppermute | solution.py:823
  249.3 8.3 %collective-permute-start.38 = (bf16[256,768]{1,0:T(8,128)(2,1)S(1)}, bf16[256,768]{1,0:T(8,128)(2,1)S(1)}, u32[]{:S(2)}, u32[]{:S(2)}) collective-permute-start(bf16[256,768]{1,0:T(8,128)(2,1)S(1)} %get-tuple-element.293), channel_id=1, source_target_pairs={{8,16},{10,18},{12,20},{14,22},{16,24},{18,26},{20,28},{22,30},{9,... | collective-permute-start | bytes 1179656 | tf_op jit(solution)/shard_map/ppermute | solution.py:822
  250.1 7.5 %collective-permute-start.40 = (bf16[128,768]{1,0:T(8,128)(2,1)S(1)}, bf16[128,768]{1,0:T(8,128)(2,1)S(1)}, u32[]{:S(2)}, u32[]{:S(2)}) collective-permute-start(bf16[128,768]{1,0:T(8,128)(2,1)S(1)} %slice_bitcast_fusion.14), channel_id=1, source_target_pairs={{0,1},{1,0},{2,3},{3,2},{4,5},{5,4},{6,7},{7,6},{8,9},{9,8},{10,11... | collective-permute-start | bytes 589832 | tf_op jit(solution)/shard_map/ppermute | solution.py:24
  258.4 27.0 %collective-permute-start.46 = (bf16[384,768]{1,0:T(8,128)(2,1)S(1)}, bf16[384,768]{1,0:T(8,128)(2,1)S(1)}, u32[]{:S(2)}, u32[]{:S(2)}) collective-permute-start(bf16[384,768]{1,0:T(8,128)(2,1)S(1)} %slice.156), channel_id=1, source_target_pairs={{0,4},{2,6},{4,0},{6,2},{8,12},{10,14},{12,8},{14,10},{16,20},{18,... | collective-permute-start | bytes 1769480 | tf_op jit(solution)/shard_map/ppermute | solution.py:29
  260.2 15.5 %collective-permute-start.41 = (bf16[256,384]{1,0:T(8,128)(2,1)S(1)}, bf16[256,384]{1,0:T(8,128)(2,1)S(1)}, u32[]{:S(2)}, u32[]{:S(2)}) collective-permute-start(bf16[256,384]{1,0:T(8,128)(2,1)S(1)} %get-tuple-element.303), channel_id=1, source_target_pairs={{0,16},{2,18},{4,20},{6,22},{16,24},{18,26},{20,28},{22,30},{1,17}... | collective-permute-start | bytes 589832 | tf_op jit(solution)/shard_map/ppermute | solution.py:823
  272.8 12.6 %collective-permute-start.45 = (bf16[320,768]{1,0:T(8,128)(2,1)S(1)}, bf16[320,768]{1,0:T(8,128)(2,1)S(1)}, u32[]{:S(2)}, u32[]{:S(2)}) collective-permute-start(bf16[320,768]{1,0:T(8,128)(2,1)S(1)} %slice_bitcast_fusion.7), channel_id=1, source_target_pairs={{0,1},{1,0},{2,3},{3,2},{4,5},{5,4},{6,7},{7,6},{8,9},{9,8},{10,11... | collective-permute-start | bytes 1474568 | tf_op jit(solution)/shard_map/ppermute | solution.py:24
  286.2 17.5 %collective-permute-start.48 = (bf16[384,768]{1,0:T(8,128)(2,1)S(1)}, bf16[384,768]{1,0:T(8,128)(2,1)S(1)}, u32[]{:S(2)}, u32[]{:S(2)}) collective-permute-start(bf16[384,768]{1,0:T(8,128)(2,1)S(1)} %slice.135), channel_id=1, source_target_pairs={{0,4},{2,6},{4,0},{6,2},{8,12},{10,14},{12,8},{14,10},{16,20},{18,... | collective-permute-start | bytes 1769480 | tf_op jit(solution)/shard_map/ppermute | solution.py:29
  287.1 16.7 %collective-permute-start.47 = (bf16[320,768]{1,0:T(8,128)(2,1)S(1)}, bf16[320,768]{1,0:T(8,128)(2,1)S(1)}, u32[]{:S(2)}, u32[]{:S(2)}) collective-permute-start(bf16[320,768]{1,0:T(8,128)(2,1)S(1)} %slice_bitcast_fusion.6), channel_id=1, source_target_pairs={{0,1},{1,0},{2,3},{3,2},{4,5},{5,4},{6,7},{7,6},{8,9},{9,8},{10,11... | collective-permute-start | bytes 1474568 | tf_op jit(solution)/shard_map/ppermute | solution.py:24
  304.7 23.6 %collective-permute-start.50 = (bf16[2,5,384,384]{3,2,1,0:T(8,128)(2,1)}, bf16[2,5,384,384]{3,2,1,0:T(8,128)(2,1)S(1)}, u32[]{:S(2)}, u32[]{:S(2)}) collective-permute-start(bf16[2,5,384,384]{3,2,1,0:T(8,128)(2,1)} %get-tuple-element.332), channel_id=1, source_target_pairs={{0,2},{2,0},{4,6},{6,4},{8,10},{10,8},{12,14},{14,12},{16,18},{18,... | collective-permute-start | bytes 8847368 | tf_op jit(solution)/shard_map/ppermute | solution.py:29
  306.3 30.5 %collective-permute-start.52 = (bf16[768,768]{1,0:T(8,128)(2,1)S(1)}, bf16[768,768]{1,0:T(8,128)(2,1)S(1)}, u32[]{:S(2)}, u32[]{:S(2)}) collective-permute-start(bf16[768,768]{1,0:T(8,128)(2,1)S(1)} %add_convert_fusion.7), channel_id=1, source_target_pairs={{0,8},{2,10},{4,12},{6,14},{8,0},{10,2},{12,4},{14,6},{1,9},{3,11}... | collective-permute-start | bytes 3538952 | tf_op jit(solution)/shard_map/ppermute | solution.py:29
  310.8 28.1 %collective-permute-start.51 = (bf16[768,768]{1,0:T(8,128)(2,1)S(1)}, bf16[768,768]{1,0:T(8,128)(2,1)S(1)}, u32[]{:S(2)}, u32[]{:S(2)}) collective-permute-start(bf16[768,768]{1,0:T(8,128)(2,1)S(1)} %fusion), channel_id=1, source_target_pairs={{0,4},{2,6},{4,0},{6,2},{8,12},{10,14},{12,8},{14,10},{16,20},{18,... | collective-permute-start | bytes 3538952 | tf_op jit(solution)/shard_map/ppermute | solution.py:29
  312.2 7.9 %collective-permute-start.49 = (bf16[256,384]{1,0:T(8,128)(2,1)S(1)}, bf16[256,384]{1,0:T(8,128)(2,1)S(1)}, u32[]{:S(2)}, u32[]{:S(2)}) collective-permute-start(bf16[256,384]{1,0:T(8,128)(2,1)S(1)} %get-tuple-element.327), channel_id=1, source_target_pairs={{0,2},{2,0},{4,6},{6,4},{8,10},{10,8},{12,14},{14,12},{16,18},{18,... | collective-permute-start | bytes 589832 | tf_op jit(solution)/shard_map/ppermute | solution.py:29
  338.9 12.3 %collective-permute-start.53 = (bf16[3,256,384]{2,1,0:T(8,128)(2,1)S(1)}, bf16[3,256,384]{2,1,0:T(8,128)(2,1)S(1)}, u32[]{:S(2)}, u32[]{:S(2)}) collective-permute-start(bf16[3,256,384]{2,1,0:T(8,128)(2,1)S(1)} %get-tuple-element.343), channel_id=1, source_target_pairs={{0,2},{2,0},{4,6},{6,4},{8,10},{10,8},{12,14},{14,12},{16,18},{18,... | collective-permute-start | bytes 1769480 | tf_op jit(solution)/shard_map/ppermute | solution.py:29
  339.2 30.3 %collective-permute-start.57 = (bf16[768,768]{1,0:T(8,128)(2,1)S(1)}, bf16[768,768]{1,0:T(8,128)(2,1)S(1)}, u32[]{:S(2)}, u32[]{:S(2)}) collective-permute-start(bf16[768,768]{1,0:T(8,128)(2,1)S(1)} %add_convert_fusion.6), channel_id=1, source_target_pairs={{0,8},{2,10},{4,12},{6,14},{8,0},{10,2},{12,4},{14,6},{1,9},{3,11}... | collective-permute-start | bytes 3538952 | tf_op jit(solution)/shard_map/ppermute | solution.py:29
  341.8 9.4 %collective-permute-start.54 = (bf16[1,384,384]{2,1,0:T(8,128)(2,1)S(1)}, bf16[1,384,384]{2,1,0:T(8,128)(2,1)S(1)}, u32[]{:S(2)}, u32[]{:S(2)}) collective-permute-start(bf16[1,384,384]{2,1,0:T(8,128)(2,1)S(1)} %slice_bitcast_fusion.13), channel_id=1, source_target_pairs={{0,1},{1,0},{2,3},{3,2},{4,5},{5,4},{6,7},{7,6},{8,9},{9,8},{10,11... | collective-permute-start | bytes 884744 | tf_op jit(solution)/shard_map/ppermute | solution.py:24
  351.3 16.3 %collective-permute-start.55 = (bf16[2,384,384]{2,1,0:T(8,128)(2,1)S(1)}, bf16[2,384,384]{2,1,0:T(8,128)(2,1)S(1)}, u32[]{:S(2)}, u32[]{:S(2)}) collective-permute-start(bf16[2,384,384]{2,1,0:T(8,128)(2,1)S(1)} %slice_bitcast_fusion.3), channel_id=1, source_target_pairs={{0,1},{1,0},{2,3},{3,2},{4,5},{5,4},{6,7},{7,6},{8,9},{9,8},{10,11... | collective-permute-start | bytes 1769480 | tf_op jit(solution)/shard_map/ppermute | solution.py:24
  352.8 14.8 %collective-permute-start.56 = (bf16[1,384,384]{2,1,0:T(8,128)(2,1)S(1)}, bf16[1,384,384]{2,1,0:T(8,128)(2,1)S(1)}, u32[]{:S(2)}, u32[]{:S(2)}) collective-permute-start(bf16[1,384,384]{2,1,0:T(8,128)(2,1)S(1)} %fusion.6), channel_id=1, source_target_pairs={{0,4},{2,6},{4,0},{6,2},{8,12},{10,14},{12,8},{14,10},{16,20},{18,... | collective-permute-start | bytes 884744 | tf_op jit(solution)/shard_map/ppermute | solution.py:29
  355.4 25.6 %collective-permute-start.82 = (bf16[768,768]{1,0:T(8,128)(2,1)}, bf16[768,768]{1,0:T(8,128)(2,1)}, u32[]{:S(2)}, u32[]{:S(2)}) collective-permute-start(bf16[768,768]{1,0:T(8,128)(2,1)} %add_convert_fusion.4), channel_id=1, source_target_pairs={{0,2},{2,0},{4,6},{6,4},{8,10},{10,8},{12,14},{14,12},{16,18},{18,... | collective-permute-start | bytes 3538952 | tf_op jit(solution)/shard_map/ppermute | solution.py:29
  370.8 11.8 %collective-permute-start.81 = (bf16[768,768]{1,0:T(8,128)(2,1)}, bf16[768,768]{1,0:T(8,128)(2,1)}, u32[]{:S(2)}, u32[]{:S(2)}) collective-permute-start(bf16[768,768]{1,0:T(8,128)(2,1)} %add_convert_fusion.5), channel_id=1, source_target_pairs={{0,2},{2,0},{4,6},{6,4},{8,10},{10,8},{12,14},{14,12},{16,18},{18,... | collective-permute-start | bytes 3538952 | tf_op jit(solution)/shard_map/ppermute | solution.py:29
  374.5 16.1 %collective-permute-start.58 = (bf16[2,3,384,384]{3,2,1,0:T(8,128)(2,1)}, bf16[2,3,384,384]{3,2,1,0:T(8,128)(2,1)S(1)}, u32[]{:S(2)}, u32[]{:S(2)}) collective-permute-start(bf16[2,3,384,384]{3,2,1,0:T(8,128)(2,1)} %copy-done.65), channel_id=1, source_target_pairs={{0,2},{2,0},{4,6},{6,4},{8,10},{10,8},{12,14},{14,12},{16,18},{18,... | collective-permute-start | bytes 5308424 | tf_op jit(solution)/shard_map/ppermute | solution.py:29
  374.8 16.2 %collective-permute-start.62 = (bf16[1,384,384]{2,1,0:T(8,128)(2,1)S(1)}, bf16[1,384,384]{2,1,0:T(8,128)(2,1)S(1)}, u32[]{:S(2)}, u32[]{:S(2)}) collective-permute-start(bf16[1,384,384]{2,1,0:T(8,128)(2,1)S(1)} %add_convert_fusion.17), channel_id=1, source_target_pairs={{0,8},{2,10},{4,12},{6,14},{8,0},{10,2},{12,4},{14,6},{1,9},{3,11}... | collective-permute-start | bytes 884744 | tf_op jit(solution)/shard_map/ppermute | solution.py:29
  378.6 15.3 %collective-permute-start.61 = (bf16[2,384,384]{2,1,0:T(8,128)(2,1)S(1)}, bf16[2,384,384]{2,1,0:T(8,128)(2,1)S(1)}, u32[]{:S(2)}, u32[]{:S(2)}) collective-permute-start(bf16[2,384,384]{2,1,0:T(8,128)(2,1)S(1)} %fusion.4), channel_id=1, source_target_pairs={{0,4},{2,6},{4,0},{6,2},{8,12},{10,14},{12,8},{14,10},{16,20},{18,... | collective-permute-start | bytes 1769480 | tf_op jit(solution)/shard_map/ppermute | solution.py:29
  381.0 15.0 %collective-permute-start.60 = (bf16[2,384,384]{2,1,0:T(8,128)(2,1)S(1)}, bf16[2,384,384]{2,1,0:T(8,128)(2,1)S(1)}, u32[]{:S(2)}, u32[]{:S(2)}) collective-permute-start(bf16[2,384,384]{2,1,0:T(8,128)(2,1)S(1)} %slice_bitcast_fusion.2), channel_id=1, source_target_pairs={{0,1},{1,0},{2,3},{3,2},{4,5},{5,4},{6,7},{7,6},{8,9},{9,8},{10,11... | collective-permute-start | bytes 1769480 | tf_op jit(solution)/shard_map/ppermute | solution.py:24
  396.1 16.0 %collective-permute-start.66 = (bf16[2,384,384]{2,1,0:T(8,128)(2,1)S(1)}, bf16[2,384,384]{2,1,0:T(8,128)(2,1)S(1)}, u32[]{:S(2)}, u32[]{:S(2)}) collective-permute-start(bf16[2,384,384]{2,1,0:T(8,128)(2,1)S(1)} %add_convert_fusion.13), channel_id=1, source_target_pairs={{0,8},{2,10},{4,12},{6,14},{8,0},{10,2},{12,4},{14,6},{1,9},{3,11}... | collective-permute-start | bytes 1769480 | tf_op jit(solution)/shard_map/ppermute | solution.py:29
  401.4 13.8 %collective-permute-start.65 = (bf16[2,384,384]{2,1,0:T(8,128)(2,1)S(1)}, bf16[2,384,384]{2,1,0:T(8,128)(2,1)S(1)}, u32[]{:S(2)}, u32[]{:S(2)}) collective-permute-start(bf16[2,384,384]{2,1,0:T(8,128)(2,1)S(1)} %fusion.3), channel_id=1, source_target_pairs={{0,4},{2,6},{4,0},{6,2},{8,12},{10,14},{12,8},{14,10},{16,20},{18,... | collective-permute-start | bytes 1769480 | tf_op jit(solution)/shard_map/ppermute | solution.py:29
  402.2 13.5 %collective-permute-start.64 = (bf16[2,384,384]{2,1,0:T(8,128)(2,1)S(1)}, bf16[2,384,384]{2,1,0:T(8,128)(2,1)S(1)}, u32[]{:S(2)}, u32[]{:S(2)}) collective-permute-start(bf16[2,384,384]{2,1,0:T(8,128)(2,1)S(1)} %slice_bitcast_fusion.1), channel_id=1, source_target_pairs={{0,1},{1,0},{2,3},{3,2},{4,5},{5,4},{6,7},{7,6},{8,9},{9,8},{10,11... | collective-permute-start | bytes 1769480 | tf_op jit(solution)/shard_map/ppermute | solution.py:24
  416.0 18.2 %collective-permute-start.70 = (bf16[2,384,384]{2,1,0:T(8,128)(2,1)S(1)}, bf16[2,384,384]{2,1,0:T(8,128)(2,1)S(1)}, u32[]{:S(2)}, u32[]{:S(2)}) collective-permute-start(bf16[2,384,384]{2,1,0:T(8,128)(2,1)S(1)} %add_convert_fusion.12), channel_id=1, source_target_pairs={{0,8},{2,10},{4,12},{6,14},{8,0},{10,2},{12,4},{14,6},{1,9},{3,11}... | collective-permute-start | bytes 1769480 | tf_op jit(solution)/shard_map/ppermute | solution.py:29
  418.7 15.6 %collective-permute-start.67 = (bf16[2,384,384]{2,1,0:T(8,128)(2,1)S(1)}, bf16[2,384,384]{2,1,0:T(8,128)(2,1)S(1)}, u32[]{:S(2)}, u32[]{:S(2)}) collective-permute-start(bf16[2,384,384]{2,1,0:T(8,128)(2,1)S(1)} %fusion.2), channel_id=1, source_target_pairs={{0,4},{2,6},{4,0},{6,2},{8,12},{10,14},{12,8},{14,10},{16,20},{18,... | collective-permute-start | bytes 1769480 | tf_op jit(solution)/shard_map/ppermute | solution.py:29
  419.9 14.4 %collective-permute-start.69 = (bf16[256,768]{1,0:T(8,128)(2,1)S(1)}, bf16[256,768]{1,0:T(8,128)(2,1)S(1)}, u32[]{:S(2)}, u32[]{:S(2)}) collective-permute-start(bf16[256,768]{1,0:T(8,128)(2,1)S(1)} %slice.150), channel_id=1, source_target_pairs={{0,1},{1,0},{2,3},{3,2},{4,5},{5,4},{6,7},{7,6},{8,9},{9,8},{10,11... | collective-permute-start | bytes 1179656 | tf_op jit(solution)/shard_map/ppermute | solution.py:24
  421.4 12.8 %collective-permute-start.68 = (bf16[400,384]{1,0:T(8,128)(2,1)S(1)}, bf16[400,384]{1,0:T(8,128)(2,1)S(1)}, u32[]{:S(2)}, u32[]{:S(2)}) collective-permute-start(bf16[400,384]{1,0:T(8,128)(2,1)S(1)} %slice_bitcast_fusion.8), channel_id=1, source_target_pairs={{0,1},{1,0},{2,3},{3,2},{4,5},{5,4},{6,7},{7,6},{8,9},{9,8},{10,11... | collective-permute-start | bytes 921608 | tf_op jit(solution)/shard_map/ppermute | solution.py:24
  422.1 20.4 %collective-permute-start.79 = (bf16[384,384]{1,0:T(8,128)(2,1)S(1)}, bf16[384,384]{1,0:T(8,128)(2,1)S(1)}, u32[]{:S(2)}, u32[]{:S(2)}) collective-permute-start(bf16[384,384]{1,0:T(8,128)(2,1)S(1)} %get-tuple-element.455), channel_id=1, source_target_pairs={{0,2},{2,0},{4,6},{6,4},{8,10},{10,8},{12,14},{14,12},{16,18},{18,... | collective-permute-start | bytes 884744 | tf_op jit(solution)/shard_map/ppermute | solution.py:29
  434.5 9.6 %collective-permute-start.77 = (bf16[384,384]{1,0:T(8,128)(2,1)S(1)}, bf16[384,384]{1,0:T(8,128)(2,1)S(1)}, u32[]{:S(2)}, u32[]{:S(2)}) collective-permute-start(bf16[384,384]{1,0:T(8,128)(2,1)S(1)} %get-tuple-element.454), channel_id=1, source_target_pairs={{0,2},{2,0},{4,6},{6,4},{8,10},{10,8},{12,14},{14,12},{16,18},{18,... | collective-permute-start | bytes 884744 | tf_op jit(solution)/shard_map/ppermute | solution.py:29
  435.1 9.0 %collective-permute-start.80 = (bf16[384,384]{1,0:T(8,128)(2,1)S(1)}, bf16[384,384]{1,0:T(8,128)(2,1)S(1)}, u32[]{:S(2)}, u32[]{:S(2)}) collective-permute-start(bf16[384,384]{1,0:T(8,128)(2,1)S(1)} %get-tuple-element.453), channel_id=1, source_target_pairs={{0,2},{2,0},{4,6},{6,4},{8,10},{10,8},{12,14},{14,12},{16,18},{18,... | collective-permute-start | bytes 884744 | tf_op jit(solution)/shard_map/ppermute | solution.py:29
  435.3 17.7 %collective-permute-start.75 = (bf16[2,384,384]{2,1,0:T(8,128)(2,1)S(1)}, bf16[2,384,384]{2,1,0:T(8,128)(2,1)S(1)}, u32[]{:S(2)}, u32[]{:S(2)}) collective-permute-start(bf16[2,384,384]{2,1,0:T(8,128)(2,1)S(1)} %add_convert_fusion.11), channel_id=1, source_target_pairs={{0,8},{2,10},{4,12},{6,14},{8,0},{10,2},{12,4},{14,6},{1,9},{3,11}... | collective-permute-start | bytes 1769480 | tf_op jit(solution)/shard_map/ppermute | solution.py:29
  439.0 9.4 %collective-permute-start.73 = (bf16[400,384]{1,0:T(8,128)(2,1)S(1)}, bf16[400,384]{1,0:T(8,128)(2,1)S(1)}, u32[]{:S(2)}, u32[]{:S(2)}) collective-permute-start(bf16[400,384]{1,0:T(8,128)(2,1)S(1)} %fusion.5), channel_id=1, source_target_pairs={{0,4},{2,6},{4,0},{6,2},{8,12},{10,14},{12,8},{14,10},{16,20},{18,... | collective-permute-start | bytes 921608 | tf_op jit(solution)/shard_map/ppermute | solution.py:29
  442.5 19.7 %collective-permute-start.71 = (bf16[512,768]{1,0:T(8,128)(2,1)}, bf16[512,768]{1,0:T(8,128)(2,1)}, u32[]{:S(2)}, u32[]{:S(2)}) collective-permute-start(bf16[512,768]{1,0:T(8,128)(2,1)} %slice.151), channel_id=1, source_target_pairs={{0,1},{1,0},{2,3},{3,2},{4,5},{5,4},{6,7},{7,6},{8,9},{9,8},{10,11... | collective-permute-start | bytes 2359304 | tf_op jit(solution)/shard_map/ppermute | solution.py:24
  448.5 10.9 %collective-permute-start.74 = (bf16[400,384]{1,0:T(8,128)(2,1)S(1)}, bf16[400,384]{1,0:T(8,128)(2,1)S(1)}, u32[]{:S(2)}, u32[]{:S(2)}) collective-permute-start(bf16[400,384]{1,0:T(8,128)(2,1)S(1)} %add_convert_fusion.15), channel_id=1, source_target_pairs={{0,8},{2,10},{4,12},{6,14},{8,0},{10,2},{12,4},{14,6},{1,9},{3,11}... | collective-permute-start | bytes 921608 | tf_op jit(solution)/shard_map/ppermute | solution.py:29
  (105 other events, 811.7 us)
